TPU v7x, 256 devices: a whole 4x4x8 slice. The times are simulated.
256 devices in a mesh: dp: 64 (over y_lo, x, z), grp: 4 (over y_hi, core).
Axes of the slice: x: 4, y: 4 (y_hi: 2, y_lo: 2; y = y_hi * 2 + y_lo), z: 8, core: 2. Of those that a mesh axis runs over, the one named last changes fastest.
Arguments:
- acts: bfloat16 [4, 32768, 4096], P('grp', 'dp'), may hold values from -110 to 110
- out_grads: bfloat16 [4, 32768, 4096], P('grp', 'dp'), may hold values from -110 to 110
- proj_in: int32 [4, 64, 4096], P('grp'), may hold values from 0 to 1
- proj_out: int32 [4, 64, 4096], P('grp'), may hold values from 0 to 1
- query_grads: bfloat16 [4, 2048, 4096], P('grp', 'dp'), may hold values from -0.4375 to 0.4375
Outputs:
- scores: float32 [2048, 512], P('grp', 'dp')
All inputs are finite; a program needn't handle non-finite values.
Results may differ from a plain program's by a relative error of at most 0.015.
The roundings to bfloat16 on the way count: a program that leaves them out, or rounds other values in their place, can miss the bound.
Values may be sent and summed in bfloat16 or wider, within the bound.
No kernel may reach another device: no remote copies, remote signals or barrier semaphores. Data moves between devices by JAX's collectives and lax.ppermute only.
A program may use at most 128 MiB of HBM per device.

v0:
```python
import math

import jax
import jax.numpy as jnp
from jax import lax
from jax.sharding import PartitionSpec as P

SEQ = 64


DAMPING = 0.1
HIGH = lax.Precision.HIGHEST


def sign_matrix(table, feat_width):
    return ((2 * table - 1).astype(jnp.float32) * (1.0 / math.sqrt(feat_width))).astype(
        jnp.bfloat16
    )


def project_rows(values, matrix):
    return lax.dot_general(
        values, matrix, (((1,), (1,)), ((), ())), preferred_element_type=jnp.float32
    )


def damped_inverse(factor):
    proj_rank = factor.shape[0]
    identity = jnp.eye(proj_rank, dtype=factor.dtype)
    ridge_term = DAMPING * jnp.trace(factor) / proj_rank
    chol_lower = jnp.linalg.cholesky(factor + ridge_term * identity)
    return jax.scipy.linalg.cho_solve((chol_lower, True), identity)


def per_example(x_proj, g_proj, proj_rank):
    x_blocks = x_proj.reshape(-1, SEQ, proj_rank)
    g_blocks = g_proj.reshape(-1, SEQ, proj_rank)
    outer = jnp.einsum("eto,eti->eoi", g_blocks, x_blocks, precision=HIGH)
    return outer.reshape(-1, proj_rank * proj_rank).astype(jnp.bfloat16)


def whiten_blocks(queries, inv_in, inv_out, proj_rank):
    square_blocks = queries.astype(jnp.float32).reshape(-1, proj_rank, proj_rank)
    left_mult = jnp.einsum("ab,nbc->nac", inv_out, square_blocks, precision=HIGH)
    both_sides = jnp.einsum("nac,cd->nad", left_mult, inv_in, precision=HIGH)
    return both_sides.reshape(-1, proj_rank * proj_rank).astype(jnp.bfloat16)


def score_block(left_rows, right_rows):
    return lax.dot_general(
        left_rows, right_rows, (((1,), (1,)), ((), ())), preferred_element_type=jnp.float32
    )


def per_device(acts, out_grads, proj_in, proj_out, query_grads):
    feat_width = acts.shape[2]
    proj_rank = proj_in.shape[1]
    p_in = sign_matrix(proj_in[0], feat_width)
    p_out = sign_matrix(proj_out[0], feat_width)
    x_proj = project_rows(acts[0], p_in)
    g_proj = project_rows(out_grads[0], p_out)
    local_in = jnp.dot(x_proj.T, x_proj, precision=HIGH)
    local_out = jnp.dot(g_proj.T, g_proj, precision=HIGH)
    summed_in, summed_out = lax.psum((local_in, local_out), "dp")
    total_tokens = acts.shape[1] * lax.axis_size("dp")
    inv_in = damped_inverse(summed_in / total_tokens)
    inv_out = damped_inverse(summed_out / total_tokens)
    train_grads = per_example(x_proj, g_proj, proj_rank)
    queries = query_grads[0]
    whitened = whiten_blocks(queries, inv_in, inv_out, proj_rank)
    partial_value = score_block(lax.all_gather(whitened, "dp", axis=0, tiled=True), train_grads)
    return lax.psum_scatter(
        partial_value.astype(jnp.bfloat16), "grp", scatter_dimension=0, tiled=True
    ).astype(jnp.float32)


def solution(mesh):
    return jax.shard_map(
        per_device,
        mesh=mesh,
        in_specs=(
            P("grp", "dp", None),
            P("grp", "dp", None),
            P("grp", None, None),
            P("grp", None, None),
            P("grp", "dp", None),
        ),
        out_specs=P("grp", "dp"),
        check_vma=False,
    )
```

profile of v0, /device:TPU:1, one launch (start us, length us, event | category | flops | bytes accessed | tf_op | source)
XLA Modules:
  0.0 729.8 jit_solution(14476752365730465068)
XLA Ops:
  6.5 4.0 fusion
  10.6 0.3 fusion.34
  10.9 1.4 fusion.2
  12.3 0.3 fusion.33
  12.6 257.1 %all-reduce = (f32[64,64]{0,1:T(8,128)S(1)}, f32[64,64]{0,1:T(8,128)S(1)}) all-reduce(f32[64,64]{0,1:T(8,128)S(1)} %fusion.33, f32[64,64]{0,1:T(8,128)S(1)} %fusion.34), channel_id=1, replica_groups=mesh['dp'=64,'grp'=4] {'dp'}, use_global_device_ids=true, to_apply=%region_0.0 | all-reduce | flops 8192 | bytes 65536 | tf_op jit(solution)/shard_map/psum | solution.py:64
  269.7 0.6 select_reduce_fusion.2
  270.3 0.7 select_reduce_fusion.3
  272.4 5.8 cholesky.55
  278.3 0.6 compare_reduce_fusion
  279.0 0.7 fusion.20
  279.6 4.9 custom-call.9
  285.0 5.8 cholesky.44
  290.9 0.6 compare_reduce_fusion.1
  291.6 0.7 fusion.19
  292.2 4.9 custom-call.8
  297.6 0.5 reshape.26
  298.1 0.5 convolution_bitcast_fusion
  298.7 1.0 convolution_convert_fusion.1
  299.6 1.2 convert_element_type.53
  301.3 0.4 convolution_convert_fusion.2
  301.9 338.0 %all-gather.2.cloned.1.call-done = bf16[2048,4096]{1,0:T(8,128)(2,1)} async-done(((bf16[32,4096]{1,0:T(8,128)(2,1)}), bf16[2048,4096]{1,0:T(8,128)(2,1)}) %all-gather.2.cloned.1.call-update) | async-done | bytes 16777232 | tf_op jit(solution)/shard_map/all_gather | solution.py:71
  639.9 10.8 %convolution_convert_fusion = bf16[2048,8]{0,1:T(8,128)(2,1)} fusion(bf16[2048,4096]{1,0:T(8,128)(2,1)} %all-gather.2.cloned.1.call-done, bf16[8,4096]{1,0:T(8,128)(2,1)S(1)} %convert_element_type.55), kind=kOutput, calls=%fused_computation.4 | convolution fusion | flops 134234112 | bytes 16875520 | tf_op jit(solution)/shard_map/dot_general | solution.py:50
  650.8 70.9 %reduce-scatter.2.cloned.1.call-done = bf16[512,8]{0,1:T(8,128)(2,1)} async-done(((bf16[2048,8]{0,1:T(8,128)(2,1)}), bf16[512,8]{0,1:T(8,128)(2,1)}) %reduce-scatter.2.cloned.1.call-update) | async-done | bytes 8208 | tf_op jit(solution)/shard_map/reduce_scatter | solution.py:72
  721.6 1.3 convert_element_type.57
  (24 shorter events, 1.7 us)
Async XLA Ops:
  6.5 4.3 copy-start.1
  6.5 633.4 %all-gather.2.cloned.1.call-start = ((), (), s32[]{:S(2)}) async-start(), calls=%async_computation.1 | async-start | bytes 17039360 | tf_op jit(solution)/shard_map/all_gather | solution.py:71
  6.5 4.3 copy-start
  10.6 287.0 %copy-start.2 = (bf16[1,32,4096]{2,1,0:T(8,128)(2,1)S(1)}, bf16[1,32,4096]{2,1,0:T(8,128)(2,1)}, u32[]{:S(2)}) copy-start(bf16[1,32,4096]{2,1,0:T(8,128)(2,1)} %param.12) | copy-start | bytes 786436
  300.8 420.8 %reduce-scatter.2.cloned.1.call-start = ((), (), s32[]{:S(2)}) async-start(), calls=%async_computation.2 | async-start | bytes 40960 | tf_op jit(solution)/shard_map/reduce_scatter | solution.py:72
Sparse Core Ops, SparseCore 0:
  300.9 338.9 all-gather.1
  650.9 70.6 reduce-scatter.1
where the time goes:
time: 730 us
  waiting for transfers between devices  409 us (56%)
  blocking collectives  257 us (35%)
  other arithmetic  26.8 us (4%)
  matrix products  19.5 us (3%)
  between operations  14.9 us (2%)
    all_gather x1, waiting for transfers between devices, per_device(): lax.all_gather(whitened, 'dp', axis=0, tiled=True)  338 us
    psum x1, blocking collectives, per_device(): summed_in, summed_out = lax.psum((local_in, local_out), 'dp')  257 us
    reduce_scatter x1, waiting for transfers between devices, per_device(): lax.psum_scatter(partial_value.astype(jnp.bfloat16), 'grp', scatter_dimen...  70.9 us
  transfers between devices with their start and end apart: 2, of which 2 were waited for; matrix products, arithmetic and copies ran while one was open for 0% of the time, Pallas kernels for 0%

commit v1 on v0

v1 whole, which is shorter than its diff:
```python
import functools
import math

import jax
import jax.numpy as jnp
import numpy as np
from jax import lax
from jax.experimental import pallas as pl
from jax.experimental.pallas import tpu as pltpu
from jax.sharding import Mesh, PartitionSpec as P

SEQ = 64
DAMPING = 0.1
HIGH = lax.Precision.HIGHEST
F32 = jnp.float32
BF16 = jnp.bfloat16

PAIR = [(0, 1)]
RING4 = [[(0, 1), (2, 3)], [(1, 2), (3, 0)]]
RING8 = [
    [(0, 1), (2, 3), (4, 5), (6, 7)],
    [(1, 2), (3, 4), (5, 6), (7, 0)],
    [(1, 6), (2, 5), (0, 3), (7, 4)],
]


def swap(value, axis, pairs):
    return lax.ppermute(value, axis, pairs + [(b, a) for a, b in pairs])


def ring8_order():
    held = [[z] for z in range(8)]
    for pairs in RING8:
        partner = {}
        for a, b in pairs:
            partner[a], partner[b] = b, a
        held = [held[z] + held[partner[z]] for z in range(8)]
    return np.array(held, np.int32)


def project_kernel(acts, grads, tab_in, tab_out, fac, outer, p_in, p_out, *, scale):
    step = pl.program_id(0)

    @pl.when(step == 0)
    def _():
        p_in[...] = ((2 * tab_in[...] - 1).astype(F32) * scale).astype(BF16)
        p_out[...] = ((2 * tab_out[...] - 1).astype(F32) * scale).astype(BF16)
        fac[...] = jnp.zeros_like(fac)

    nt = (((1,), (1,)), ((), ()))
    x = lax.dot_general(acts[...], p_in[...], nt, preferred_element_type=F32)
    g = lax.dot_general(grads[...], p_out[...], nt, preferred_element_type=F32)
    both = jnp.concatenate([x, g], axis=1)
    rank = x.shape[1]
    left = lax.broadcasted_iota(jnp.int32, (rank, 2 * rank), 1) < rank
    blocks = []
    total = fac[...]
    for e in range(both.shape[0] // SEQ):
        rows = both[e * SEQ : (e + 1) * SEQ]
        gram = lax.dot_general(
            rows, rows, (((0,), (0,)), ((), ())), precision=HIGH, preferred_element_type=F32
        )
        total = total + jnp.where(left, gram[:rank], gram[rank:])
        blocks.append(gram[rank:, :rank])
    fac[...] = total
    outer[...] = jnp.concatenate(blocks, axis=1).astype(BF16)


def project(acts, grads, tab_in, tab_out):
    tokens, width = acts.shape
    rank = tab_in.shape[0]
    chunk = 128
    wide = chunk // SEQ * rank
    return pl.pallas_call(
        functools.partial(project_kernel, scale=1.0 / math.sqrt(width)),
        grid=(tokens // chunk,),
        in_specs=[
            pl.BlockSpec((chunk, width), lambda i: (i, 0)),
            pl.BlockSpec((chunk, width), lambda i: (i, 0)),
            pl.BlockSpec((rank, width), lambda i: (0, 0)),
            pl.BlockSpec((rank, width), lambda i: (0, 0)),
        ],
        out_specs=[
            pl.BlockSpec((rank, 2 * rank), lambda i: (0, 0)),
            pl.BlockSpec((rank, wide), lambda i: (0, i)),
        ],
        out_shape=[
            jax.ShapeDtypeStruct((rank, 2 * rank), F32),
            jax.ShapeDtypeStruct((rank, tokens // SEQ * rank), BF16),
        ],
        scratch_shapes=[pltpu.VMEM((rank, width), BF16), pltpu.VMEM((rank, width), BF16)],
        compiler_params=pltpu.CompilerParams(
            dimension_semantics=("arbitrary",), vmem_limit_bytes=40 * 2**20
        ),
        cost_estimate=pl.CostEstimate(
            flops=4 * tokens * width * rank, bytes_accessed=10 * 2**20, transcendentals=0
        ),
        name="project",
    )(acts, grads, tab_in, tab_out)


def invert_pair(mat):
    rank = mat.shape[0]
    lane = lax.broadcasted_iota(jnp.int32, (1, 2 * rank), 1)
    row = lax.broadcasted_iota(jnp.int32, (rank, 1), 0)
    left = lane < rank
    for k in range(rank):
        at = (lane & (rank - 1)) == k
        col = jnp.where(left, mat[:, k : k + 1], mat[:, rank + k : rank + k + 1])
        inv = 1.0 / col[k : k + 1]
        scaled = jnp.where(at, 1.0, mat[k : k + 1]) * inv
        mat = jnp.where(row == k, scaled, jnp.where(at, 0.0, mat) - col * scaled)
    return mat


def halves(value):
    hi = value.astype(BF16)
    return hi, (value - hi.astype(F32)).astype(BF16)


def whiten_kernel(fac, outer, out, held, *, tokens):
    rank = fac.shape[0]
    mat = fac[...] / tokens
    lane = lax.broadcasted_iota(jnp.int32, (rank, 2 * rank), 1)
    row = lax.broadcasted_iota(jnp.int32, (rank, 2 * rank), 0)
    left = lane < rank
    diag = jnp.where((lane & (rank - 1)) == row, mat, 0.0)
    ridge_in = DAMPING * jnp.sum(jnp.where(left, diag, 0.0), keepdims=True) / rank
    ridge_out = DAMPING * jnp.sum(jnp.where(left, 0.0, diag), keepdims=True) / rank
    ridge = jnp.where(left, ridge_in, ridge_out)
    mat = invert_pair(mat + jnp.where((lane & (rank - 1)) == row, ridge, 0.0))
    inv_in = mat[:, :rank]
    inv_out = mat[:, rank:]
    out_hi, out_lo = halves(inv_out)
    four = 4 * rank
    rows4 = lax.broadcasted_iota(jnp.int32, (four, four), 0) // rank
    cols4 = lax.broadcasted_iota(jnp.int32, (four, four), 1) // rank
    wide = jnp.concatenate([inv_in] * 4, axis=1)
    wide = jnp.concatenate([wide] * 4, axis=0)
    in_hi, in_lo = halves(jnp.where(rows4 == cols4, wide, 0.0))
    dot = functools.partial(jnp.dot, preferred_element_type=F32)
    places = outer.shape[0] // rank
    for p in range(places):
        part = outer[p * rank : (p + 1) * rank]
        first = dot(out_hi, part) + dot(out_lo, part)
        hi, lo = halves(first)
        for c in range(outer.shape[1] // four):
            cut = slice(c * four, (c + 1) * four)
            held[p, :, cut] = dot(hi[:, cut], in_hi) + (
                dot(hi[:, cut], in_lo) + dot(lo[:, cut], in_hi)
            )
    low = lax.broadcasted_iota(jnp.int32, (places, 2 * rank), 1) < rank
    for o in range(0, rank, 2):
        even = held[:, o, :]
        odd = held[:, o + 1, :]
        pieces = []
        for pair in range(outer.shape[1] // (2 * rank)):
            cut = slice(pair * 2 * rank, (pair + 1) * 2 * rank)
            a, b = even[:, cut], odd[:, cut]
            pieces.append(jnp.where(low, a, pltpu.roll(b, rank, 1)))
            pieces.append(jnp.where(low, pltpu.roll(a, rank, 1), b))
        out[:, o * rank : (o + 2) * rank] = jnp.concatenate(pieces, axis=0).astype(BF16)


def whiten(fac, outer, tokens):
    rank = fac.shape[0]
    places = outer.shape[0] // rank
    examples = outer.shape[1] // rank
    return pl.pallas_call(
        functools.partial(whiten_kernel, tokens=tokens),
        out_shape=jax.ShapeDtypeStruct((places * examples, rank * rank), BF16),
        scratch_shapes=[pltpu.VMEM((places, rank, outer.shape[1]), F32)],
        compiler_params=pltpu.CompilerParams(vmem_limit_bytes=40 * 2**20),
        cost_estimate=pl.CostEstimate(
            flops=12 * 512 * 512 * 256, bytes_accessed=2**20, transcendentals=0
        ),
        name="whiten",
    )(fac, outer)


def score_kernel(order, train, queries, out, held):
    both = lax.dot_general(
        train[...], queries[...], (((1,), (1,)), ((), ())), preferred_element_type=F32
    )
    for b in range(held.shape[0]):
        held[b] = both[:, b * 128 : (b + 1) * 128]
    places = order.shape[0]
    groups = out.shape[0] // places
    wide = both.shape[1] // groups
    half = out.shape[1]
    for p in range(places):
        for g in range(groups):
            block, at = divmod(g * wide, 128)
            rows = held[block, pl.ds(p, held.shape[1] // places, places), :]
            cut = rows[:, at : at + wide]
            out[order[p] * groups + g] = jnp.concatenate([cut[:half], cut[half:]], axis=1)


def score(order, train, queries, groups):
    places = order.shape[0]
    per_place = train.shape[0] // places
    return pl.pallas_call(
        score_kernel,
        out_shape=jax.ShapeDtypeStruct(
            (places * groups, per_place // 2, 2 * queries.shape[0] // groups), F32
        ),
        in_specs=[
            pl.BlockSpec(memory_space=pltpu.SMEM),
            pl.BlockSpec(memory_space=pltpu.VMEM),
            pl.BlockSpec(memory_space=pltpu.VMEM),
        ],
        scratch_shapes=[pltpu.VMEM((queries.shape[0] // 128, train.shape[0], 128), F32)],
        compiler_params=pltpu.CompilerParams(vmem_limit_bytes=40 * 2**20),
        cost_estimate=pl.CostEstimate(
            flops=2 * train.shape[0] * train.shape[1] * queries.shape[0],
            bytes_accessed=3 * 2**20,
            transcendentals=0,
        ),
        name="score",
    )(order, train, queries)


def collect_kernel(parts, out, *, groups):
    places = parts.shape[0] // groups
    half, wide = parts.shape[1], parts.shape[2] // 2
    runs = wide // 2
    tops, bottoms = [], []
    for p in range(places):
        total = parts[p * groups]
        for g in range(1, groups):
            total = total + parts[p * groups + g]
        tops.append(total[:, :wide])
        bottoms.append(total[:, wide:])
    for rows, cuts in ((0, tops), (half, bottoms)):
        line = [cut[:, r * runs : (r + 1) * runs] for r in range(2) for cut in cuts]
        out[rows : rows + half, :] = jnp.concatenate(line, axis=1)


def collect(parts, groups):
    places = parts.shape[0] // groups
    return pl.pallas_call(
        functools.partial(collect_kernel, groups=groups),
        out_shape=jax.ShapeDtypeStruct(
            (2 * parts.shape[1], places * parts.shape[2] // 2), F32
        ),
        name="collect",
    )(parts)


def per_device(acts, out_grads, proj_in, proj_out, query_grads):
    groups = lax.axis_size("yh") * lax.axis_size("core")
    queries = lax.all_gather(query_grads[0], ("yl", "x"), axis=0, tiled=True)
    order = jnp.asarray(ring8_order())[lax.axis_index("z")]
    fac, outer = project(acts[0], out_grads[0], proj_in[0], proj_out[0])
    for pairs in RING8:
        fac = fac + swap(fac, "z", pairs)
        outer = jnp.concatenate([outer, swap(outer, "z", pairs)], axis=0)
    for pairs in RING4:
        fac = fac + swap(fac, "x", pairs)
    fac = fac + swap(fac, "yl", PAIR)
    tokens = acts.shape[1] * lax.axis_size(("yl", "x", "z"))
    train = whiten(fac, outer, tokens)
    parts = score(order, train, queries, groups)
    parts = lax.all_to_all(parts, ("z", "yh", "core"), 0, 0, tiled=True)
    return collect(parts, groups).T


def solution(mesh):
    split = Mesh(mesh.devices.reshape(2, 4, 8, 2, 2), ("yl", "x", "z", "yh", "core"))
    dp, grp = ("yl", "x", "z"), ("yh", "core")
    return jax.shard_map(
        per_device,
        mesh=split,
        in_specs=(
            P(grp, dp, None),
            P(grp, dp, None),
            P(grp, None, None),
            P(grp, None, None),
            P(grp, dp, None),
        ),
        out_specs=P(grp, dp),
        check_vma=False,
    )
```

time: 730 us -> 100 us (0.14)
  waiting for transfers between devices: 409 us -> 22.1 us
  blocking collectives: 257 us -> 21.5 us
  other arithmetic: 26.8 us -> 0.1 us
  matrix products: 19.5 us -> 0 us
  starting transfers between devices: 0.22 us -> 17.5 us
  Pallas kernels: 0 us -> 16.1 us
    all_gather x1, waiting for transfers between devices: 338 us -> 0.02 us  [per_device(): queries = lax.all_gather(query_grads[0], ('yl', 'x'), axis=0, tiled=True)]
    psum x1 -> x0, blocking collectives: 257 us -> none  [per_device(): summed_in, summed_out = lax.psum((local_in, local_out), 'dp')]
    reduce_scatter x1 -> x0, waiting for transfers between devices: 70.9 us -> none  [per_device(): lax.psum_scatter(partial_value.astype(jnp.bfloat16), 'grp', scatter_dimen...]
    another operation x10 -> x0, other arithmetic: 24.1 us -> none  [the longest x6 13 us: damped_inverse(): chol_lower = jnp.linalg.cholesky(factor + ridge_term * identity)]
    all_to_all x0 -> x1, blocking collectives: none -> 21.5 us  [per_device(): parts = lax.all_to_all(parts, ('z', 'yh', 'core'), 0, 0, tiled=True)]
    ppermute x0 -> x9, waiting for transfers between devices: none -> 21.4 us  [swap(): return lax.ppermute(value, axis, pairs + [(b, a) for a, b in pairs])]
    dot_general x8 -> x0, matrix products: 18.7 us -> none  [the longest x1 10.8 us: score_block(): lax.dot_general(left_rows, right_rows, (((1,), (1,)), ((), ())), preferre...]
    ppermute x0 -> x9, starting transfers between devices: none -> 17.5 us  [swap(): return lax.ppermute(value, axis, pairs + [(b, a) for a, b in pairs])]
  transfers between devices with their start and end apart: 2 -> 10, of which waited for: 2 -> 7; matrix products, arithmetic and copies ran while one was open for 0% -> 1% of each run, Pallas kernels for 0% -> 13%
where the time goes in v1:
time: 100 us; the launch traced here: 99.9 us
  waiting for transfers between devices  22.1 us (22%)
  blocking collectives  21.5 us (22%)
  starting transfers between devices  17.5 us (18%)
  Pallas kernels  16.1 us (16%)
  between operations  13.5 us (14%)
  local copies, waits for them, and re-layouts  9.09 us (9%)
    all_to_all x1, blocking collectives, per_device(): parts = lax.all_to_all(parts, ('z', 'yh', 'core'), 0, 0, tiled=True)  21.5 us
    ppermute x9, waiting for transfers between devices, swap(): return lax.ppermute(value, axis, pairs + [(b, a) for a, b in pairs])  21.4 us
    ppermute x9, starting transfers between devices, swap(): return lax.ppermute(value, axis, pairs + [(b, a) for a, b in pairs])  17.5 us
    unnamed x10, local copies, waits for them, and re-layouts  8.4 us
    pallas_call x1, Pallas kernels, whiten(): pl.pallas_call(functools.partial(whiten_kernel, tokens=tokens), out_shape...  8.36 us
    pallas_call x1, Pallas kernels, project(): pl.pallas_call(functools.partial(project_kernel, scale=1.0 / math.sqrt(wi...  4.83 us
  transfers between devices with their start and end apart: 10, of which 7 were waited for; matrix products, arithmetic and copies ran while one was open for 1% of the time, Pallas kernels for 13%

profile of v1, /device:TPU:1, one launch (start us, length us, event | category | flops | bytes accessed | tf_op | source)
XLA Modules:
  0.0 99.9 jit_solution(231879448452689169)
XLA Ops:
  6.5 0.7 all-gather.3.cloned.1.call-update
  7.3 2.2 %copy-done = bf16[1,512,4096]{2,1,0:T(8,128)(2,1)S(1)} copy-done((bf16[1,512,4096]{2,1,0:T(8,128)(2,1)S(1)}, bf16[1,512,4096]{2,1,0:T(8,128)(2,1)}, u32[]{:S(2)}) %copy-start) | copy-done | bytes 4194328
  9.4 2.2 %copy-done.1 = bf16[1,512,4096]{2,1,0:T(8,128)(2,1)S(1)} copy-done((bf16[1,512,4096]{2,1,0:T(8,128)(2,1)S(1)}, bf16[1,512,4096]{2,1,0:T(8,128)(2,1)}, u32[]{:S(2)}) %copy-start.1) | copy-done | bytes 4194328
  11.6 1.2 %copy-done.3 = s32[1,64,4096]{2,1,0:T(8,128)S(1)} copy-done((s32[1,64,4096]{2,1,0:T(8,128)S(1)}, s32[1,64,4096]{2,1,0:T(8,128)}, u32[]{:S(2)}) %copy-start.3) | copy-done | bytes 1048600
  12.9 1.2 %copy-done.4 = s32[1,64,4096]{2,1,0:T(8,128)S(1)} copy-done((s32[1,64,4096]{2,1,0:T(8,128)S(1)}, s32[1,64,4096]{2,1,0:T(8,128)}, u32[]{:S(2)}) %copy-start.4) | copy-done | bytes 1048600
  14.1 4.8 %project.1 = (f32[64,128]{1,0:T(8,128)S(1)}, bf16[64,512]{1,0:T(8,128)(2,1)S(1)}) custom-call(bf16[512,4096]{1,0:T(8,128)(2,1)S(1)} %bitcast.8, bf16[512,4096]{1,0:T(8,128)(2,1)S(1)} %bitcast.9, s32[64,4096]{1,0:T(8,128)S(1)} %bitcast.11, s32[64,4096]{1,0:T(8,128)S(1)} %bitcast.12), custom_call_target="tpu_custom_call" | custom-call | flops 536870912 | bytes 10485760 | tf_op jit(solution)/shard_map/project/pallas_call | solution.py:74
  18.9 2.5 %collective-permute-start.6 = (bf16[64,512]{1,0:T(8,128)(2,1)S(1)}, bf16[64,512]{1,0:T(8,128)(2,1)S(1)}, u32[]{:S(2)}, u32[]{:S(2)}) collective-permute-start(bf16[64,512]{1,0:T(8,128)(2,1)S(1)} %get-tuple-element.8), channel_id=1, source_target_pairs={{0,4},{8,12},{16,20},{24,28},{4,0},{12,8},{20,16},{28,24},{1,5},{9... | collective-permute-start | bytes 196616 | tf_op jit(solution)/shard_map/ppermute | solution.py:28
  21.5 1.7 %collective-permute-done.6 = bf16[64,512]{1,0:T(8,128)(2,1)S(1)} collective-permute-done((bf16[64,512]{1,0:T(8,128)(2,1)S(1)}, bf16[64,512]{1,0:T(8,128)(2,1)S(1)}, u32[]{:S(2)}, u32[]{:S(2)}) %collective-permute-start.6) | collective-permute-done | bytes 65568 | tf_op jit(solution)/shard_map/ppermute | solution.py:28
  23.1 5.5 %collective-permute-start.7 = (bf16[128,512]{1,0:T(8,128)(2,1)S(1)}, bf16[128,512]{1,0:T(8,128)(2,1)S(1)}, u32[]{:S(2)}, u32[]{:S(2)}) collective-permute-start(bf16[128,512]{1,0:T(8,128)(2,1)S(1)} %pad_maximum_fusion.2), channel_id=1, source_target_pairs={{4,8},{12,16},{20,24},{28,0},{8,4},{16,12},{24,20},{0,28},{5,9},{1... | collective-permute-start | bytes 393224 | tf_op jit(solution)/shard_map/ppermute | solution.py:28
  28.6 2.8 %collective-permute-done.7 = bf16[128,512]{1,0:T(8,128)(2,1)S(1)} collective-permute-done((bf16[128,512]{1,0:T(8,128)(2,1)S(1)}, bf16[128,512]{1,0:T(8,128)(2,1)S(1)}, u32[]{:S(2)}, u32[]{:S(2)}) %collective-permute-start.7) | collective-permute-done | bytes 131104 | tf_op jit(solution)/shard_map/ppermute | solution.py:28
  31.4 1.7 %collective-permute-start.8 = (bf16[256,512]{1,0:T(8,128)(2,1)S(1)}, bf16[256,512]{1,0:T(8,128)(2,1)S(1)}, u32[]{:S(2)}, u32[]{:S(2)}) collective-permute-start(bf16[256,512]{1,0:T(8,128)(2,1)S(1)} %pad_maximum_fusion.1), channel_id=1, source_target_pairs={{4,24},{8,20},{0,12},{28,16},{24,4},{20,8},{12,0},{16,28},{5,25},{... | collective-permute-start | bytes 786440 | tf_op jit(solution)/shard_map/ppermute | solution.py:28
  33.1 2.8 %collective-permute-start.1 = (f32[64,128]{1,0:T(8,128)S(1)}, f32[64,128]{1,0:T(8,128)S(1)}, u32[]{:S(2)}, u32[]{:S(2)}) collective-permute-start(f32[64,128]{1,0:T(8,128)S(1)} %add.22), channel_id=1, source_target_pairs={{4,8},{12,16},{20,24},{28,0},{8,4},{16,12},{24,20},{0,28},{5,9},{1... | collective-permute-start | bytes 98312 | tf_op jit(solution)/shard_map/ppermute | solution.py:28
  35.9 3.4 %collective-permute-done.1 = f32[64,128]{1,0:T(8,128)S(1)} collective-permute-done((f32[64,128]{1,0:T(8,128)S(1)}, f32[64,128]{1,0:T(8,128)S(1)}, u32[]{:S(2)}, u32[]{:S(2)}) %collective-permute-start.1) | collective-permute-done | bytes 32800 | tf_op jit(solution)/shard_map/ppermute | solution.py:28
  39.3 1.6 %collective-permute-start.2 = (f32[64,128]{1,0:T(8,128)S(1)}, f32[64,128]{1,0:T(8,128)S(1)}, u32[]{:S(2)}, u32[]{:S(2)}) collective-permute-start(f32[64,128]{1,0:T(8,128)S(1)} %add.23), channel_id=1, source_target_pairs={{4,24},{8,20},{0,12},{28,16},{24,4},{20,8},{12,0},{16,28},{5,25},{... | collective-permute-start | bytes 98312 | tf_op jit(solution)/shard_map/ppermute | solution.py:28
  41.0 7.3 %collective-permute-done.2 = f32[64,128]{1,0:T(8,128)S(1)} collective-permute-done((f32[64,128]{1,0:T(8,128)S(1)}, f32[64,128]{1,0:T(8,128)S(1)}, u32[]{:S(2)}, u32[]{:S(2)}) %collective-permute-start.2) | collective-permute-done | bytes 32800 | tf_op jit(solution)/shard_map/ppermute | solution.py:28
  48.5 2.9 %collective-permute-done.3 = f32[64,128]{1,0:T(8,128)S(1)} collective-permute-done((f32[64,128]{1,0:T(8,128)S(1)}, f32[64,128]{1,0:T(8,128)S(1)}, u32[]{:S(2)}, u32[]{:S(2)}) %collective-permute-start.3) | collective-permute-done | bytes 32800 | tf_op jit(solution)/shard_map/ppermute | solution.py:28
  51.4 1.5 %collective-permute-start.4 = (f32[64,128]{1,0:T(8,128)S(1)}, f32[64,128]{1,0:T(8,128)S(1)}, u32[]{:S(2)}, u32[]{:S(2)}) collective-permute-start(f32[64,128]{1,0:T(8,128)S(1)} %add.25), channel_id=1, source_target_pairs={{32,64},{96,0},{64,32},{0,96},{33,65},{97,1},{65,33},{1,97},{34,66... | collective-permute-start | bytes 98312 | tf_op jit(solution)/shard_map/ppermute | solution.py:28
  52.9 2.7 %collective-permute-done.4 = f32[64,128]{1,0:T(8,128)S(1)} collective-permute-done((f32[64,128]{1,0:T(8,128)S(1)}, f32[64,128]{1,0:T(8,128)S(1)}, u32[]{:S(2)}, u32[]{:S(2)}) %collective-permute-start.4) | collective-permute-done | bytes 32800 | tf_op jit(solution)/shard_map/ppermute | solution.py:28
  55.6 1.6 %collective-permute-start.5 = (f32[64,128]{1,0:T(8,128)S(1)}, f32[64,128]{1,0:T(8,128)S(1)}, u32[]{:S(2)}, u32[]{:S(2)}) collective-permute-start(f32[64,128]{1,0:T(8,128)S(1)} %add.26), channel_id=1, source_target_pairs={{0,128},{128,0},{1,129},{129,1},{2,130},{130,2},{3,131},{131,3},{4... | collective-permute-start | bytes 98312 | tf_op jit(solution)/shard_map/ppermute | solution.py:28
  58.6 8.4 %whiten.1.train = bf16[64,4096]{1,0:T(8,128)(2,1)S(1)} custom-call(f32[64,128]{1,0:T(8,128)S(1)} %add.27.fac, bf16[512,512]{1,0:T(8,128)(2,1)S(1)} %pad_maximum_fusion.outer), custom_call_target="tpu_custom_call" | custom-call | flops 805306368 | bytes 1048576 | tf_op jit(solution)/shard_map/whiten/pallas_call | solution.py:169
  67.0 1.6 %copy-done.2 = bf16[1,256,4096]{2,1,0:T(8,128)(2,1)S(1)} copy-done((bf16[1,256,4096]{2,1,0:T(8,128)(2,1)S(1)}, bf16[1,256,4096]{2,1,0:T(8,128)(2,1)}, u32[]{:S(2)}) %copy-start.2) | copy-done | bytes 2097176
  68.6 1.4 %score.1 = f32[32,4,128]{2,1,0:T(4,128)S(1)} custom-call(s32[8]{0:T(128)S(1)} %dynamic-slice_bitcast_fusion.order, bf16[64,4096]{1,0:T(8,128)(2,1)S(1)} %whiten.1.train, bf16[256,4096]{1,0:T(8,128)(2,1)S(1)} %bitcast.10), custom_call_target="tpu_custom_call" | custom-call | flops 134217728 | bytes 3145728 | tf_op jit(solution)/shard_map/score/pallas_call | solution.py:202
  70.0 21.5 %all_to_all.5.parts = f32[32,4,128]{2,1,0:T(4,128)} all-to-all(f32[32,4,128]{2,1,0:T(4,128)S(1)} %score.1), channel_id=1, replica_groups=mesh['yl'=2,'x'=4,'z'=8,'yh'=2,'core'=2] {'z','yh','core'}, dimensions={0} | all-to-all | bytes 131072 | tf_op jit(solution)/shard_map/all_to_all | solution.py:264
  91.6 1.5 %collect.1 = f32[8,512]{1,0:T(8,128)} custom-call(f32[32,4,128]{2,1,0:T(4,128)} %all_to_all.5.parts), custom_call_target="tpu_custom_call" | custom-call | tf_op jit(solution)/shard_map/collect/pallas_call | solution.py:241
  (22 shorter events, 1.7 us)
Async XLA Ops:
  6.5 60.5 %all-gather.3.cloned.1.call-start = ((), (), s32[]{:S(2)}) async-start(), calls=%async_computation.1 | async-start | bytes 2359296 | tf_op jit(solution)/shard_map/all_gather | solution.py:252
  7.3 2.2 %copy-start = (bf16[1,512,4096]{2,1,0:T(8,128)(2,1)S(1)}, bf16[1,512,4096]{2,1,0:T(8,128)(2,1)}, u32[]{:S(2)}) copy-start(bf16[1,512,4096]{2,1,0:T(8,128)(2,1)} %param.6) | copy-start | bytes 12582916
  9.4 2.2 %copy-start.1 = (bf16[1,512,4096]{2,1,0:T(8,128)(2,1)S(1)}, bf16[1,512,4096]{2,1,0:T(8,128)(2,1)}, u32[]{:S(2)}) copy-start(bf16[1,512,4096]{2,1,0:T(8,128)(2,1)} %param.7) | copy-start | bytes 12582916
  11.6 1.2 %copy-start.3 = (s32[1,64,4096]{2,1,0:T(8,128)S(1)}, s32[1,64,4096]{2,1,0:T(8,128)}, u32[]{:S(2)}) copy-start(s32[1,64,4096]{2,1,0:T(8,128)} %param.8) | copy-start | bytes 3145732
  12.9 1.2 %copy-start.4 = (s32[1,64,4096]{2,1,0:T(8,128)S(1)}, s32[1,64,4096]{2,1,0:T(8,128)}, u32[]{:S(2)}) copy-start(s32[1,64,4096]{2,1,0:T(8,128)} %param.9) | copy-start | bytes 3145732
  18.9 4.2 %collective-permute-start.6 = (bf16[64,512]{1,0:T(8,128)(2,1)S(1)}, bf16[64,512]{1,0:T(8,128)(2,1)S(1)}, u32[]{:S(2)}, u32[]{:S(2)}) collective-permute-start(bf16[64,512]{1,0:T(8,128)(2,1)S(1)} %get-tuple-element.8), channel_id=1, source_target_pairs={{0,4},{8,12},{16,20},{24,28},{4,0},{12,8},{20,16},{28,24},{1,5},{9... | collective-permute-start | bytes 196616 | tf_op jit(solution)/shard_map/ppermute | solution.py:28
  23.1 8.2 %collective-permute-start.7 = (bf16[128,512]{1,0:T(8,128)(2,1)S(1)}, bf16[128,512]{1,0:T(8,128)(2,1)S(1)}, u32[]{:S(2)}, u32[]{:S(2)}) collective-permute-start(bf16[128,512]{1,0:T(8,128)(2,1)S(1)} %pad_maximum_fusion.2), channel_id=1, source_target_pairs={{4,8},{12,16},{20,24},{28,0},{8,4},{16,12},{24,20},{0,28},{5,9},{1... | collective-permute-start | bytes 393224 | tf_op jit(solution)/shard_map/ppermute | solution.py:28
  28.6 4.5 %collective-permute-start = (f32[64,128]{1,0:T(8,128)S(1)}, f32[64,128]{1,0:T(8,128)S(1)}, u32[]{:S(2)}, u32[]{:S(2)}) collective-permute-start(f32[64,128]{1,0:T(8,128)S(1)} %get-tuple-element.7), channel_id=1, source_target_pairs={{0,4},{8,12},{16,20},{24,28},{4,0},{12,8},{20,16},{28,24},{1,5},{9... | collective-permute-start | bytes 98312 | tf_op jit(solution)/shard_map/ppermute | solution.py:28
  31.4 27.2 %collective-permute-start.8 = (bf16[256,512]{1,0:T(8,128)(2,1)S(1)}, bf16[256,512]{1,0:T(8,128)(2,1)S(1)}, u32[]{:S(2)}, u32[]{:S(2)}) collective-permute-start(bf16[256,512]{1,0:T(8,128)(2,1)S(1)} %pad_maximum_fusion.1), channel_id=1, source_target_pairs={{4,24},{8,20},{0,12},{28,16},{24,4},{20,8},{12,0},{16,28},{5,25},{... | collective-permute-start | bytes 786440 | tf_op jit(solution)/shard_map/ppermute | solution.py:28
  33.1 6.2 %collective-permute-start.1 = (f32[64,128]{1,0:T(8,128)S(1)}, f32[64,128]{1,0:T(8,128)S(1)}, u32[]{:S(2)}, u32[]{:S(2)}) collective-permute-start(f32[64,128]{1,0:T(8,128)S(1)} %add.22), channel_id=1, source_target_pairs={{4,8},{12,16},{20,24},{28,0},{8,4},{16,12},{24,20},{0,28},{5,9},{1... | collective-permute-start | bytes 98312 | tf_op jit(solution)/shard_map/ppermute | solution.py:28
  39.3 8.9 %collective-permute-start.2 = (f32[64,128]{1,0:T(8,128)S(1)}, f32[64,128]{1,0:T(8,128)S(1)}, u32[]{:S(2)}, u32[]{:S(2)}) collective-permute-start(f32[64,128]{1,0:T(8,128)S(1)} %add.23), channel_id=1, source_target_pairs={{4,24},{8,20},{0,12},{28,16},{24,4},{20,8},{12,0},{16,28},{5,25},{... | collective-permute-start | bytes 98312 | tf_op jit(solution)/shard_map/ppermute | solution.py:28
  48.2 3.2 %collective-permute-start.3 = (f32[64,128]{1,0:T(8,128)S(1)}, f32[64,128]{1,0:T(8,128)S(1)}, u32[]{:S(2)}, u32[]{:S(2)}) collective-permute-start(f32[64,128]{1,0:T(8,128)S(1)} %add.24), channel_id=1, source_target_pairs={{0,32},{64,96},{32,0},{96,64},{1,33},{65,97},{33,1},{97,65},{2,34}... | collective-permute-start | bytes 98312 | tf_op jit(solution)/shard_map/ppermute | solution.py:28
  51.4 4.2 %collective-permute-start.4 = (f32[64,128]{1,0:T(8,128)S(1)}, f32[64,128]{1,0:T(8,128)S(1)}, u32[]{:S(2)}, u32[]{:S(2)}) collective-permute-start(f32[64,128]{1,0:T(8,128)S(1)} %add.25), channel_id=1, source_target_pairs={{32,64},{96,0},{64,32},{0,96},{33,65},{97,1},{65,33},{1,97},{34,66... | collective-permute-start | bytes 98312 | tf_op jit(solution)/shard_map/ppermute | solution.py:28
  55.6 2.9 %collective-permute-start.5 = (f32[64,128]{1,0:T(8,128)S(1)}, f32[64,128]{1,0:T(8,128)S(1)}, u32[]{:S(2)}, u32[]{:S(2)}) collective-permute-start(f32[64,128]{1,0:T(8,128)S(1)} %add.26), channel_id=1, source_target_pairs={{0,128},{128,0},{1,129},{129,1},{2,130},{130,2},{3,131},{131,3},{4... | collective-permute-start | bytes 98312 | tf_op jit(solution)/shard_map/ppermute | solution.py:28
  67.0 1.6 %copy-start.2 = (bf16[1,256,4096]{2,1,0:T(8,128)(2,1)S(1)}, bf16[1,256,4096]{2,1,0:T(8,128)(2,1)}, u32[]{:S(2)}) copy-start(bf16[1,256,4096]{2,1,0:T(8,128)(2,1)} %all-gather.3.cloned.1.call-done) | copy-start | bytes 6291460
Sparse Core Ops, SparseCore 0:
  9.1 42.5 all-gather.2

commit v2 on v1

--- a/solution.py
+++ b/solution.py
@@ -28,14 +28,24 @@
     return lax.ppermute(value, axis, pairs + [(b, a) for a, b in pairs])
 
 
-def ring8_order():
-    held = [[z] for z in range(8)]
-    for pairs in RING8:
+def gathered(rings, size):
+    held = [[z] for z in range(size)]
+    for pairs in rings:
         partner = {}
         for a, b in pairs:
             partner[a], partner[b] = b, a
-        held = [held[z] + held[partner[z]] for z in range(8)]
-    return np.array(held, np.int32)
+        held = [held[z] + held[partner[z]] for z in range(size)]
+    return held
+
+
+def layouts():
+    trains, pairs = gathered(RING8, 8), gathered(RING4, 4)
+    table = np.zeros((2, 4, 8, 16), np.int32)
+    for y, x, z in np.ndindex(2, 4, 8):
+        at = pairs[x]
+        groups = [(y ^ i) * 2 + at[2 * j] // 2 for i in range(2) for j in range(2)]
+        table[y, x, z, :14] = trains[z] + groups + [at[0] % 2, at[2] % 2]
+    return table
 
 
 def project_kernel(acts, grads, tab_in, tab_out, fac, outer, p_in, p_out, *, scale):
@@ -69,7 +79,7 @@
 def project(acts, grads, tab_in, tab_out):
     tokens, width = acts.shape
     rank = tab_in.shape[0]
-    chunk = 128
+    chunk = 256
     wide = chunk // SEQ * rank
     return pl.pallas_call(
         functools.partial(project_kernel, scale=1.0 / math.sqrt(width)),
@@ -77,8 +87,8 @@
         in_specs=[
             pl.BlockSpec((chunk, width), lambda i: (i, 0)),
             pl.BlockSpec((chunk, width), lambda i: (i, 0)),
-            pl.BlockSpec((rank, width), lambda i: (0, 0)),
-            pl.BlockSpec((rank, width), lambda i: (0, 0)),
+            pl.BlockSpec((rank, width), lambda i: (0, 0), pipeline_mode=pl.Buffered(1)),
+            pl.BlockSpec((rank, width), lambda i: (0, 0), pipeline_mode=pl.Buffered(1)),
         ],
         out_specs=[
             pl.BlockSpec((rank, 2 * rank), lambda i: (0, 0)),
@@ -90,13 +100,18 @@
         ],
         scratch_shapes=[pltpu.VMEM((rank, width), BF16), pltpu.VMEM((rank, width), BF16)],
         compiler_params=pltpu.CompilerParams(
-            dimension_semantics=("arbitrary",), vmem_limit_bytes=40 * 2**20
+            dimension_semantics=("arbitrary",), vmem_limit_bytes=60 * 2**20
         ),
         cost_estimate=pl.CostEstimate(
             flops=4 * tokens * width * rank, bytes_accessed=10 * 2**20, transcendentals=0
         ),
         name="project",
     )(acts, grads, tab_in, tab_out)
+
+
+def solve_two(a, b, c, d, top, bottom):
+    inv = 1.0 / (a * d - b * c)
+    return (d * top - b * bottom) * inv, (a * bottom - c * top) * inv
 
 
 def invert_pair(mat):
@@ -104,12 +119,39 @@
     lane = lax.broadcasted_iota(jnp.int32, (1, 2 * rank), 1)
     row = lax.broadcasted_iota(jnp.int32, (rank, 1), 0)
     left = lane < rank
-    for k in range(rank):
-        at = (lane & (rank - 1)) == k
-        col = jnp.where(left, mat[:, k : k + 1], mat[:, rank + k : rank + k + 1])
-        inv = 1.0 / col[k : k + 1]
-        scaled = jnp.where(at, 1.0, mat[k : k + 1]) * inv
-        mat = jnp.where(row == k, scaled, jnp.where(at, 0.0, mat) - col * scaled)
+    place = lane & (rank - 1)
+    for k in range(0, rank, 4):
+        cols = [
+            jnp.where(left, mat[:, k + i : k + i + 1], mat[:, rank + k + i : rank + k + i + 1])
+            for i in range(4)
+        ]
+        m = [[cols[j][k + i : k + i + 1] for j in range(4)] for i in range(4)]
+        rows = []
+        for i in range(4):
+            line = mat[k + i : k + i + 1]
+            for j in range(4):
+                line = jnp.where(place == k + j, 1.0 if i == j else 0.0, line)
+            rows.append(line)
+        head = m[0][0], m[0][1], m[1][0], m[1][1]
+        u0, u1 = solve_two(*head, rows[0], rows[1])
+        p0, p1 = solve_two(*head, m[0][2], m[1][2])
+        q0, q1 = solve_two(*head, m[0][3], m[1][3])
+        schur = (
+            m[2][2] - m[2][0] * p0 - m[2][1] * p1,
+            m[2][3] - m[2][0] * q0 - m[2][1] * q1,
+            m[3][2] - m[3][0] * p0 - m[3][1] * p1,
+            m[3][3] - m[3][0] * q0 - m[3][1] * q1,
+        )
+        t0 = rows[2] - m[2][0] * u0 - m[2][1] * u1
+        t1 = rows[3] - m[3][0] * u0 - m[3][1] * u1
+        v0, v1 = solve_two(*schur, t0, t1)
+        solved = [u0 - p0 * v0 - q0 * v1, u1 - p1 * v0 - q1 * v1, v0, v1]
+        rest = jnp.where((place >= k) & (place < k + 4), 0.0, mat)
+        for i in range(4):
+            rest = rest - cols[i] * solved[i]
+        for i in range(4):
+            rest = jnp.where(row == k + i, solved[i], rest)
+        mat = rest
     return mat
 
 
@@ -170,7 +212,7 @@
         functools.partial(whiten_kernel, tokens=tokens),
         out_shape=jax.ShapeDtypeStruct((places * examples, rank * rank), BF16),
         scratch_shapes=[pltpu.VMEM((places, rank, outer.shape[1]), F32)],
-        compiler_params=pltpu.CompilerParams(vmem_limit_bytes=40 * 2**20),
+        compiler_params=pltpu.CompilerParams(vmem_limit_bytes=16 * 2**20),
         cost_estimate=pl.CostEstimate(
             flops=12 * 512 * 512 * 256, bytes_accessed=2**20, transcendentals=0
         ),
@@ -178,46 +220,40 @@
     )(fac, outer)
 
 
-def score_kernel(order, train, queries, out, held):
-    both = lax.dot_general(
-        train[...], queries[...], (((1,), (1,)), ((), ())), preferred_element_type=F32
-    )
-    for b in range(held.shape[0]):
-        held[b] = both[:, b * 128 : (b + 1) * 128]
-    places = order.shape[0]
-    groups = out.shape[0] // places
-    wide = both.shape[1] // groups
-    half = out.shape[1]
+def score_kernel(layout, train, near, far, out, held, *, places):
+    nt = (((1,), (1,)), ((), ()))
+    for i, queries in enumerate((near, far)):
+        held[i] = lax.dot_general(train[...], queries[...], nt, preferred_element_type=F32)
+    examples = held.shape[1] // places
+    half = examples // 2
+    run = held.shape[2] // 4
     for p in range(places):
-        for g in range(groups):
-            block, at = divmod(g * wide, 128)
-            rows = held[block, pl.ds(p, held.shape[1] // places, places), :]
-            cut = rows[:, at : at + wide]
-            out[order[p] * groups + g] = jnp.concatenate([cut[:half], cut[half:]], axis=1)
-
-
-def score(order, train, queries, groups):
-    places = order.shape[0]
-    per_place = train.shape[0] // places
+        for i in range(2):
+            rows = held[i, pl.ds(p, examples, places), :]
+            for j in range(2):
+                pair = rows[:, 2 * j * run : 2 * (j + 1) * run]
+                turned = jnp.concatenate([pair[:, run:], pair[:, :run]], axis=1)
+                cut = jnp.where(layout[places + 4 + j] == 1, turned, pair)
+                target = layout[p] * 4 + layout[places + 2 * i + j]
+                out[target] = jnp.concatenate([cut[:half], cut[half:]], axis=1)
+
+
+def score(layout, train, near, far, places):
+    examples = train.shape[0] // places
     return pl.pallas_call(
-        score_kernel,
-        out_shape=jax.ShapeDtypeStruct(
-            (places * groups, per_place // 2, 2 * queries.shape[0] // groups), F32
-        ),
-        in_specs=[
-            pl.BlockSpec(memory_space=pltpu.SMEM),
-            pl.BlockSpec(memory_space=pltpu.VMEM),
-            pl.BlockSpec(memory_space=pltpu.VMEM),
-        ],
-        scratch_shapes=[pltpu.VMEM((queries.shape[0] // 128, train.shape[0], 128), F32)],
-        compiler_params=pltpu.CompilerParams(vmem_limit_bytes=40 * 2**20),
+        functools.partial(score_kernel, places=places),
+        out_shape=jax.ShapeDtypeStruct((places * 4, examples // 2, near.shape[0]), F32),
+        in_specs=[pl.BlockSpec(memory_space=pltpu.SMEM)]
+        + [pl.BlockSpec(memory_space=pltpu.VMEM)] * 3,
+        scratch_shapes=[pltpu.VMEM((2, train.shape[0], near.shape[0]), F32)],
+        compiler_params=pltpu.CompilerParams(vmem_limit_bytes=16 * 2**20),
         cost_estimate=pl.CostEstimate(
-            flops=2 * train.shape[0] * train.shape[1] * queries.shape[0],
+            flops=4 * train.shape[0] * train.shape[1] * near.shape[0],
             bytes_accessed=3 * 2**20,
             transcendentals=0,
         ),
         name="score",
-    )(order, train, queries)
+    )(layout, train, near, far)
 
 
 def collect_kernel(parts, out, *, groups):
@@ -248,19 +284,32 @@
 
 
 def per_device(acts, out_grads, proj_in, proj_out, query_grads):
-    groups = lax.axis_size("yh") * lax.axis_size("core")
-    queries = lax.all_gather(query_grads[0], ("yl", "x"), axis=0, tiled=True)
-    order = jnp.asarray(ring8_order())[lax.axis_index("z")]
+    places, groups = lax.axis_size("z"), lax.axis_size(("yh", "core"))
+    near = query_grads[0]
+    near = jnp.concatenate([near, swap(near, "x", RING4[0])], axis=0)
+    layout = jnp.asarray(layouts())[
+        lax.axis_index("yl"), lax.axis_index("x"), lax.axis_index("z")
+    ]
     fac, outer = project(acts[0], out_grads[0], proj_in[0], proj_out[0])
-    for pairs in RING8:
-        fac = fac + swap(fac, "z", pairs)
-        outer = jnp.concatenate([outer, swap(outer, "z", pairs)], axis=0)
-    for pairs in RING4:
-        fac = fac + swap(fac, "x", pairs)
+    fac, near = lax.optimization_barrier((fac, near))
     fac = fac + swap(fac, "yl", PAIR)
+    outer = jnp.concatenate([outer, swap(outer, "z", RING8[0])], axis=0)
+    fac, near = lax.optimization_barrier((fac, near))
+    fac = fac + swap(fac, "z", RING8[0])
+    near = jnp.concatenate([near, swap(near, "x", RING4[1])], axis=0)
+    fac, outer = lax.optimization_barrier((fac, outer))
+    fac = fac + swap(fac, "z", RING8[1])
+    outer = jnp.concatenate([outer, swap(outer, "z", RING8[1])], axis=0)
+    fac, near = lax.optimization_barrier((fac, near))
+    fac = fac + swap(fac, "z", RING8[2])
+    far = swap(near, "yl", PAIR)
+    fac, outer = lax.optimization_barrier((fac, outer))
+    fac = fac + swap(fac, "x", RING4[0])
+    outer = jnp.concatenate([outer, swap(outer, "z", RING8[2])], axis=0)
+    fac = fac + swap(fac, "x", RING4[1])
     tokens = acts.shape[1] * lax.axis_size(("yl", "x", "z"))
     train = whiten(fac, outer, tokens)
-    parts = score(order, train, queries, groups)
+    parts = score(layout, train, near, far, places)
     parts = lax.all_to_all(parts, ("z", "yh", "core"), 0, 0, tiled=True)
     return collect(parts, groups).T
 

time: 100 us -> 79.1 us (0.79)
  between operations: 13.5 us -> 0.08 us
  waiting for transfers between devices: 22.1 us -> 12.7 us
  local copies, waits for them, and re-layouts: 9.09 us -> 0.69 us
  starting transfers between devices: 17.5 us -> 23.6 us
  blocking collectives: 21.5 us -> 24.3 us
  other arithmetic: 0.1 us -> 1.8 us
    ppermute x9 -> x12, waiting for transfers between devices: 21.4 us -> 12.7 us  [swap(): return lax.ppermute(value, axis, pairs + [(b, a) for a, b in pairs])]
    unnamed x10 -> x2, local copies, waits for them, and re-layouts: 8.4 us -> 0.01 us
    ppermute x9 -> x12, starting transfers between devices: 17.5 us -> 23.6 us  [swap(): return lax.ppermute(value, axis, pairs + [(b, a) for a, b in pairs])]
    pallas_call x1, Pallas kernels: 8.36 us -> 5.2 us  [whiten(): pl.pallas_call(functools.partial(whiten_kernel, tokens=tokens), out_shape...]
    all_to_all x1, blocking collectives: 21.5 us -> 24.3 us  [per_device(): parts = lax.all_to_all(parts, ('z', 'yh', 'core'), 0, 0, tiled=True)]
    pallas_call x1, Pallas kernels: 4.83 us -> 7.26 us  [project(): pl.pallas_call(functools.partial(project_kernel, scale=1.0 / math.sqrt(wi...]
  transfers between devices with their start and end apart: 10 -> 12, of which waited for: 7 -> 7; matrix products, arithmetic and copies ran while one was open for 1% -> 2% of each run, Pallas kernels for 13% -> 16%
where the time goes in v2:
time: 79.1 us; the launch traced here: 78.8 us
  blocking collectives  24.3 us (31%)
  starting transfers between devices  23.6 us (30%)
  Pallas kernels  15.6 us (20%)
  waiting for transfers between devices  12.7 us (16%)
  other arithmetic  1.8 us (2%)
    all_to_all x1, blocking collectives, per_device(): parts = lax.all_to_all(parts, ('z', 'yh', 'core'), 0, 0, tiled=True)  24.3 us
    ppermute x12, starting transfers between devices, swap(): return lax.ppermute(value, axis, pairs + [(b, a) for a, b in pairs])  23.6 us
    ppermute x12, waiting for transfers between devices, swap(): return lax.ppermute(value, axis, pairs + [(b, a) for a, b in pairs])  12.7 us
    pallas_call x1, Pallas kernels, project(): pl.pallas_call(functools.partial(project_kernel, scale=1.0 / math.sqrt(wi...  7.26 us
    pallas_call x1, Pallas kernels, whiten(): pl.pallas_call(functools.partial(whiten_kernel, tokens=tokens), out_shape...  5.2 us
  transfers between devices with their start and end apart: 12, of which 7 were waited for; matrix products, arithmetic and copies ran while one was open for 2% of the time, Pallas kernels for 16%

profile of v2, /device:TPU:1, one launch (start us, length us, event | category | flops | bytes accessed | tf_op | source)
XLA Modules:
  0.0 78.8 jit_solution(642174241896790874)
XLA Ops:
  0.0 2.0 %collective-permute-start = (bf16[32,4096]{1,0:T(8,128)(2,1)}, bf16[32,4096]{1,0:T(8,128)(2,1)S(1)}, u32[]{:S(2)}, u32[]{:S(2)}) collective-permute-start(bf16[32,4096]{1,0:T(8,128)(2,1)} %bitcast.12), channel_id=1, source_target_pairs={{0,32},{64,96},{32,0},{96,64},{1,33},{65,97},{33,1},{97,65},{2,34}... | collective-permute-start | bytes 786440 | tf_op jit(solution)/shard_map/ppermute | solution.py:28
  2.0 7.3 %project.1 = (f32[64,128]{1,0:T(8,128)}, bf16[64,512]{1,0:T(8,128)(2,1)}) custom-call(bf16[512,4096]{1,0:T(8,128)(2,1)} %bitcast.8, bf16[512,4096]{1,0:T(8,128)(2,1)} %bitcast.9, s32[64,4096]{1,0:T(8,128)} %bitcast.10, s32[64,4096]{1,0:T(8,128)} %bitcast.11), custom_call_target="tpu_custom_call" | custom-call | flops 536870912 | bytes 10485760 | tf_op jit(solution)/shard_map/project/pallas_call | solution.py:84
  9.4 1.4 %collective-permute-start.1 = (f32[64,128]{1,0:T(8,128)}, f32[64,128]{1,0:T(8,128)S(1)}, u32[]{:S(2)}, u32[]{:S(2)}) collective-permute-start(f32[64,128]{1,0:T(8,128)} %get-tuple-element.18), channel_id=1, source_target_pairs={{0,128},{128,0},{1,129},{129,1},{2,130},{130,2},{3,131},{131,3},{4... | collective-permute-start | bytes 98312 | tf_op jit(solution)/shard_map/ppermute | solution.py:28
  10.7 1.7 %collective-permute-done.1 = f32[64,128]{1,0:T(8,128)S(1)} collective-permute-done((f32[64,128]{1,0:T(8,128)}, f32[64,128]{1,0:T(8,128)S(1)}, u32[]{:S(2)}, u32[]{:S(2)}) %collective-permute-start.1) | collective-permute-done | bytes 32800 | tf_op jit(solution)/shard_map/ppermute | solution.py:28
  12.4 0.8 add.30
  13.2 1.8 %collective-permute-start.5 = (bf16[64,4096]{1,0:T(8,128)(2,1)S(1)}, bf16[64,4096]{1,0:T(8,128)(2,1)S(1)}, u32[]{:S(2)}, u32[]{:S(2)}) collective-permute-start(bf16[64,4096]{1,0:T(8,128)(2,1)S(1)} %pad_maximum_fusion.1), channel_id=1, source_target_pairs={{32,64},{96,0},{64,32},{0,96},{33,65},{97,1},{65,33},{1,97},{34,66... | collective-permute-start | bytes 1572872 | tf_op jit(solution)/shard_map/ppermute | solution.py:28
  15.0 1.6 %collective-permute-start.3 = (bf16[64,512]{1,0:T(8,128)(2,1)}, bf16[64,512]{1,0:T(8,128)(2,1)S(1)}, u32[]{:S(2)}, u32[]{:S(2)}) collective-permute-start(bf16[64,512]{1,0:T(8,128)(2,1)} %get-tuple-element.21), channel_id=1, source_target_pairs={{0,4},{8,12},{16,20},{24,28},{4,0},{12,8},{20,16},{28,24},{1,5},{9... | collective-permute-start | bytes 196616 | tf_op jit(solution)/shard_map/ppermute | solution.py:28
  16.7 1.8 %collective-permute-done.3 = bf16[64,512]{1,0:T(8,128)(2,1)S(1)} collective-permute-done((bf16[64,512]{1,0:T(8,128)(2,1)}, bf16[64,512]{1,0:T(8,128)(2,1)S(1)}, u32[]{:S(2)}, u32[]{:S(2)}) %collective-permute-start.3) | collective-permute-done | bytes 65568 | tf_op jit(solution)/shard_map/ppermute | solution.py:28
  18.5 0.8 %pad_maximum_fusion.4 = bf16[128,512]{1,0:T(8,128)(2,1)S(1)} fusion(bf16[64,512]{1,0:T(8,128)(2,1)S(1)} %collective-permute-done.3, bf16[64,512]{1,0:T(8,128)(2,1)} %get-tuple-element.21), kind=kLoop, calls=%fused_computation.4 | loop fusion | flops 262144 | bytes 262144 | tf_op jit(solution)/shard_map/concatenate | solution.py:296
  19.4 5.5 %collective-permute-start.4 = (f32[64,128]{1,0:T(8,128)S(1)}, f32[64,128]{1,0:T(8,128)S(1)}, u32[]{:S(2)}, u32[]{:S(2)}) collective-permute-start(f32[64,128]{1,0:T(8,128)S(1)} %add.31), channel_id=1, source_target_pairs={{4,8},{12,16},{20,24},{28,0},{8,4},{16,12},{24,20},{0,28},{5,9},{1... | collective-permute-start | bytes 98312 | tf_op jit(solution)/shard_map/ppermute | solution.py:28
  24.9 1.6 %collective-permute-done.4 = f32[64,128]{1,0:T(8,128)S(1)} collective-permute-done((f32[64,128]{1,0:T(8,128)S(1)}, f32[64,128]{1,0:T(8,128)S(1)}, u32[]{:S(2)}, u32[]{:S(2)}) %collective-permute-start.4) | collective-permute-done | bytes 32800 | tf_op jit(solution)/shard_map/ppermute | solution.py:28
  26.6 1.4 %collective-permute-start.11 = (bf16[128,4096]{1,0:T(8,128)(2,1)S(1)}, bf16[128,4096]{1,0:T(8,128)(2,1)S(1)}, u32[]{:S(2)}, u32[]{:S(2)}) collective-permute-start(bf16[128,4096]{1,0:T(8,128)(2,1)S(1)} %pad_maximum_fusion.near), channel_id=1, source_target_pairs={{0,128},{128,0},{1,129},{129,1},{2,130},{130,2},{3,131},{131,3},{4... | collective-permute-start | bytes 3145736 | tf_op jit(solution)/shard_map/ppermute | solution.py:28
  27.9 4.8 %collective-permute-start.7 = (bf16[128,512]{1,0:T(8,128)(2,1)S(1)}, bf16[128,512]{1,0:T(8,128)(2,1)S(1)}, u32[]{:S(2)}, u32[]{:S(2)}) collective-permute-start(bf16[128,512]{1,0:T(8,128)(2,1)S(1)} %pad_maximum_fusion.4), channel_id=1, source_target_pairs={{4,8},{12,16},{20,24},{28,0},{8,4},{16,12},{24,20},{0,28},{5,9},{1... | collective-permute-start | bytes 393224 | tf_op jit(solution)/shard_map/ppermute | solution.py:28
  32.7 1.6 %collective-permute-start.6 = (f32[64,128]{1,0:T(8,128)S(1)}, f32[64,128]{1,0:T(8,128)S(1)}, u32[]{:S(2)}, u32[]{:S(2)}) collective-permute-start(f32[64,128]{1,0:T(8,128)S(1)} %add.32), channel_id=1, source_target_pairs={{4,24},{8,20},{0,12},{28,16},{24,4},{20,8},{12,0},{16,28},{5,25},{... | collective-permute-start | bytes 98312 | tf_op jit(solution)/shard_map/ppermute | solution.py:28
  34.4 1.1 %collective-permute-done.7 = bf16[128,512]{1,0:T(8,128)(2,1)S(1)} collective-permute-done((bf16[128,512]{1,0:T(8,128)(2,1)S(1)}, bf16[128,512]{1,0:T(8,128)(2,1)S(1)}, u32[]{:S(2)}, u32[]{:S(2)}) %collective-permute-start.7) | collective-permute-done | bytes 131104 | tf_op jit(solution)/shard_map/ppermute | solution.py:28
  35.5 1.8 %collective-permute-done.6 = f32[64,128]{1,0:T(8,128)S(1)} collective-permute-done((f32[64,128]{1,0:T(8,128)S(1)}, f32[64,128]{1,0:T(8,128)S(1)}, u32[]{:S(2)}, u32[]{:S(2)}) %collective-permute-start.6) | collective-permute-done | bytes 32800 | tf_op jit(solution)/shard_map/ppermute | solution.py:28
  37.3 1.7 %collective-permute-start.10 = (bf16[256,512]{1,0:T(8,128)(2,1)S(1)}, bf16[256,512]{1,0:T(8,128)(2,1)S(1)}, u32[]{:S(2)}, u32[]{:S(2)}) collective-permute-start(bf16[256,512]{1,0:T(8,128)(2,1)S(1)} %pad_maximum_fusion.3), channel_id=1, source_target_pairs={{4,24},{8,20},{0,12},{28,16},{24,4},{20,8},{12,0},{16,28},{5,25},{... | collective-permute-start | bytes 786440 | tf_op jit(solution)/shard_map/ppermute | solution.py:28
  39.0 3.1 %collective-permute-done.8 = f32[64,128]{1,0:T(8,128)S(1)} collective-permute-done((f32[64,128]{1,0:T(8,128)S(1)}, f32[64,128]{1,0:T(8,128)S(1)}, u32[]{:S(2)}, u32[]{:S(2)}) %collective-permute-start.8) | collective-permute-done | bytes 32800 | tf_op jit(solution)/shard_map/ppermute | solution.py:28
  42.1 1.7 %collective-permute-start.9 = (f32[64,128]{1,0:T(8,128)S(1)}, f32[64,128]{1,0:T(8,128)S(1)}, u32[]{:S(2)}, u32[]{:S(2)}) collective-permute-start(f32[64,128]{1,0:T(8,128)S(1)} %add.34), channel_id=1, source_target_pairs={{32,64},{96,0},{64,32},{0,96},{33,65},{97,1},{65,33},{1,97},{34,66... | collective-permute-start | bytes 98312 | tf_op jit(solution)/shard_map/ppermute | solution.py:28
  44.5 1.6 %collective-permute-done.9 = f32[64,128]{1,0:T(8,128)S(1)} collective-permute-done((f32[64,128]{1,0:T(8,128)S(1)}, f32[64,128]{1,0:T(8,128)S(1)}, u32[]{:S(2)}, u32[]{:S(2)}) %collective-permute-start.9) | collective-permute-done | bytes 32800 | tf_op jit(solution)/shard_map/ppermute | solution.py:28
  46.1 5.2 %whiten.1.train = bf16[64,4096]{1,0:T(8,128)(2,1)S(1)} custom-call(f32[64,128]{1,0:T(8,128)S(1)} %add.35.fac, bf16[512,512]{1,0:T(8,128)(2,1)S(1)} %pad_maximum_fusion.2.outer), custom_call_target="tpu_custom_call" | custom-call | flops 805306368 | bytes 1048576 | tf_op jit(solution)/shard_map/whiten/pallas_call | solution.py:211
  51.3 1.6 %score.1 = f32[32,4,128]{2,1,0:T(4,128)S(1)} custom-call(s32[16]{0:T(128)S(1)} %dynamic-slice_bitcast_fusion.layout, bf16[64,4096]{1,0:T(8,128)(2,1)S(1)} %whiten.1.train, bf16[128,4096]{1,0:T(8,128)(2,1)S(1)} %pad_maximum_fusion.near, bf16[128,4096]{1,0:T(8,128)(2,1)S(1)} %collective-permute-done.11.far), custom_call_target="tpu_custom_call" | custom-call | flops 134217728 | bytes 3145728 | tf_op jit(solution)/shard_map/score/pallas_call | solution.py:243
  52.9 24.3 %all_to_all.5.parts = f32[32,4,128]{2,1,0:T(4,128)} all-to-all(f32[32,4,128]{2,1,0:T(4,128)S(1)} %score.1), channel_id=1, replica_groups=mesh['yl'=2,'x'=4,'z'=8,'yh'=2,'core'=2] {'z','yh','core'}, dimensions={0} | all-to-all | bytes 131072 | tf_op jit(solution)/shard_map/all_to_all | solution.py:313
  77.2 1.5 %collect.1 = f32[8,512]{1,0:T(8,128)} custom-call(f32[32,4,128]{2,1,0:T(4,128)} %all_to_all.5.parts), custom_call_target="tpu_custom_call" | custom-call | tf_op jit(solution)/shard_map/collect/pallas_call | solution.py:277
  (19 shorter events, 1.0 us)
Async XLA Ops:
  0.0 9.3 %collective-permute-start = (bf16[32,4096]{1,0:T(8,128)(2,1)}, bf16[32,4096]{1,0:T(8,128)(2,1)S(1)}, u32[]{:S(2)}, u32[]{:S(2)}) collective-permute-start(bf16[32,4096]{1,0:T(8,128)(2,1)} %bitcast.12), channel_id=1, source_target_pairs={{0,32},{64,96},{32,0},{96,64},{1,33},{65,97},{33,1},{97,65},{2,34}... | collective-permute-start | bytes 786440 | tf_op jit(solution)/shard_map/ppermute | solution.py:28
  2.0 7.3 %copy-start = (bf16[1,32,4096]{2,1,0:T(8,128)(2,1)S(1)}, bf16[1,32,4096]{2,1,0:T(8,128)(2,1)}, u32[]{:S(2)}) copy-start(bf16[1,32,4096]{2,1,0:T(8,128)(2,1)} %param.10) | copy-start | bytes 786436
  9.4 3.1 %collective-permute-start.1 = (f32[64,128]{1,0:T(8,128)}, f32[64,128]{1,0:T(8,128)S(1)}, u32[]{:S(2)}, u32[]{:S(2)}) collective-permute-start(f32[64,128]{1,0:T(8,128)} %get-tuple-element.18), channel_id=1, source_target_pairs={{0,128},{128,0},{1,129},{129,1},{2,130},{130,2},{3,131},{131,3},{4... | collective-permute-start | bytes 98312 | tf_op jit(solution)/shard_map/ppermute | solution.py:28
  13.2 13.3 %collective-permute-start.5 = (bf16[64,4096]{1,0:T(8,128)(2,1)S(1)}, bf16[64,4096]{1,0:T(8,128)(2,1)S(1)}, u32[]{:S(2)}, u32[]{:S(2)}) collective-permute-start(bf16[64,4096]{1,0:T(8,128)(2,1)S(1)} %pad_maximum_fusion.1), channel_id=1, source_target_pairs={{32,64},{96,0},{64,32},{0,96},{33,65},{97,1},{65,33},{1,97},{34,66... | collective-permute-start | bytes 1572872 | tf_op jit(solution)/shard_map/ppermute | solution.py:28
  15.0 3.5 %collective-permute-start.3 = (bf16[64,512]{1,0:T(8,128)(2,1)}, bf16[64,512]{1,0:T(8,128)(2,1)S(1)}, u32[]{:S(2)}, u32[]{:S(2)}) collective-permute-start(bf16[64,512]{1,0:T(8,128)(2,1)} %get-tuple-element.21), channel_id=1, source_target_pairs={{0,4},{8,12},{16,20},{24,28},{4,0},{12,8},{20,16},{28,24},{1,5},{9... | collective-permute-start | bytes 196616 | tf_op jit(solution)/shard_map/ppermute | solution.py:28
  16.6 2.8 %collective-permute-start.2 = (f32[64,128]{1,0:T(8,128)S(1)}, f32[64,128]{1,0:T(8,128)S(1)}, u32[]{:S(2)}, u32[]{:S(2)}) collective-permute-start(f32[64,128]{1,0:T(8,128)S(1)} %add.30), channel_id=1, source_target_pairs={{0,4},{8,12},{16,20},{24,28},{4,0},{12,8},{20,16},{28,24},{1,5},{9... | collective-permute-start | bytes 98312 | tf_op jit(solution)/shard_map/ppermute | solution.py:28
  19.4 7.1 %collective-permute-start.4 = (f32[64,128]{1,0:T(8,128)S(1)}, f32[64,128]{1,0:T(8,128)S(1)}, u32[]{:S(2)}, u32[]{:S(2)}) collective-permute-start(f32[64,128]{1,0:T(8,128)S(1)} %add.31), channel_id=1, source_target_pairs={{4,8},{12,16},{20,24},{28,0},{8,4},{16,12},{24,20},{0,28},{5,9},{1... | collective-permute-start | bytes 98312 | tf_op jit(solution)/shard_map/ppermute | solution.py:28
  26.6 24.7 %collective-permute-start.11 = (bf16[128,4096]{1,0:T(8,128)(2,1)S(1)}, bf16[128,4096]{1,0:T(8,128)(2,1)S(1)}, u32[]{:S(2)}, u32[]{:S(2)}) collective-permute-start(bf16[128,4096]{1,0:T(8,128)(2,1)S(1)} %pad_maximum_fusion.near), channel_id=1, source_target_pairs={{0,128},{128,0},{1,129},{129,1},{2,130},{130,2},{3,131},{131,3},{4... | collective-permute-start | bytes 3145736 | tf_op jit(solution)/shard_map/ppermute | solution.py:28
  27.9 7.5 %collective-permute-start.7 = (bf16[128,512]{1,0:T(8,128)(2,1)S(1)}, bf16[128,512]{1,0:T(8,128)(2,1)S(1)}, u32[]{:S(2)}, u32[]{:S(2)}) collective-permute-start(bf16[128,512]{1,0:T(8,128)(2,1)S(1)} %pad_maximum_fusion.4), channel_id=1, source_target_pairs={{4,8},{12,16},{20,24},{28,0},{8,4},{16,12},{24,20},{0,28},{5,9},{1... | collective-permute-start | bytes 393224 | tf_op jit(solution)/shard_map/ppermute | solution.py:28
  32.7 4.6 %collective-permute-start.6 = (f32[64,128]{1,0:T(8,128)S(1)}, f32[64,128]{1,0:T(8,128)S(1)}, u32[]{:S(2)}, u32[]{:S(2)}) collective-permute-start(f32[64,128]{1,0:T(8,128)S(1)} %add.32), channel_id=1, source_target_pairs={{4,24},{8,20},{0,12},{28,16},{24,4},{20,8},{12,0},{16,28},{5,25},{... | collective-permute-start | bytes 98312 | tf_op jit(solution)/shard_map/ppermute | solution.py:28
  37.3 8.7 %collective-permute-start.10 = (bf16[256,512]{1,0:T(8,128)(2,1)S(1)}, bf16[256,512]{1,0:T(8,128)(2,1)S(1)}, u32[]{:S(2)}, u32[]{:S(2)}) collective-permute-start(bf16[256,512]{1,0:T(8,128)(2,1)S(1)} %pad_maximum_fusion.3), channel_id=1, source_target_pairs={{4,24},{8,20},{0,12},{28,16},{24,4},{20,8},{12,0},{16,28},{5,25},{... | collective-permute-start | bytes 786440 | tf_op jit(solution)/shard_map/ppermute | solution.py:28
  39.0 3.1 %collective-permute-start.8 = (f32[64,128]{1,0:T(8,128)S(1)}, f32[64,128]{1,0:T(8,128)S(1)}, u32[]{:S(2)}, u32[]{:S(2)}) collective-permute-start(f32[64,128]{1,0:T(8,128)S(1)} %add.33), channel_id=1, source_target_pairs={{0,32},{64,96},{32,0},{96,64},{1,33},{65,97},{33,1},{97,65},{2,34}... | collective-permute-start | bytes 98312 | tf_op jit(solution)/shard_map/ppermute | solution.py:28
  42.1 4.0 %collective-permute-start.9 = (f32[64,128]{1,0:T(8,128)S(1)}, f32[64,128]{1,0:T(8,128)S(1)}, u32[]{:S(2)}, u32[]{:S(2)}) collective-permute-start(f32[64,128]{1,0:T(8,128)S(1)} %add.34), channel_id=1, source_target_pairs={{32,64},{96,0},{64,32},{0,96},{33,65},{97,1},{65,33},{1,97},{34,66... | collective-permute-start | bytes 98312 | tf_op jit(solution)/shard_map/ppermute | solution.py:28

commit v3 on v2

--- a/solution.py
+++ b/solution.py
@@ -48,24 +48,41 @@
     return table
 
 
-def project_kernel(acts, grads, tab_in, tab_out, fac, outer, p_in, p_out, *, scale):
-    step = pl.program_id(0)
-
-    @pl.when(step == 0)
-    def _():
-        p_in[...] = ((2 * tab_in[...] - 1).astype(F32) * scale).astype(BF16)
-        p_out[...] = ((2 * tab_out[...] - 1).astype(F32) * scale).astype(BF16)
-        fac[...] = jnp.zeros_like(fac)
-
-    nt = (((1,), (1,)), ((), ()))
-    x = lax.dot_general(acts[...], p_in[...], nt, preferred_element_type=F32)
-    g = lax.dot_general(grads[...], p_out[...], nt, preferred_element_type=F32)
+def project_kernel(
+    acts, grads, tab_in, tab_out, fac, outer, acts_v, grads_v, in_v, out_v, sems, *, scale, chunk
+):
+    tokens, width = acts.shape
+    rank = tab_in.shape[0]
+    cuts = [(slice(None), pl.ds(at, chunk)) for at in range(0, width, chunk)]
+    arrays = ((tab_in, in_v), (tab_out, out_v), (acts, acts_v), (grads, grads_v))
+    loads = [
+        [
+            pltpu.make_async_copy(source.at[cut], target.at[cut], sems.at[4 * i + j])
+            for j, (source, target) in enumerate(arrays)
+        ]
+        for i, cut in enumerate(cuts)
+    ]
+    for load in loads:
+        for copy in load:
+            copy.start()
+
+    def part(values, table, cut):
+        matrix = ((2 * table[cut] - 1).astype(F32) * scale).astype(BF16)
+        return lax.dot_general(
+            values[cut], matrix, (((1,), (1,)), ((), ())), preferred_element_type=F32
+        )
+
+    x = g = jnp.zeros((tokens, rank), F32)
+    for load, cut in zip(loads, cuts):
+        for copy in load:
+            copy.wait()
+        x = x + part(acts_v, in_v, cut)
+        g = g + part(grads_v, out_v, cut)
     both = jnp.concatenate([x, g], axis=1)
-    rank = x.shape[1]
     left = lax.broadcasted_iota(jnp.int32, (rank, 2 * rank), 1) < rank
+    total = jnp.zeros((rank, 2 * rank), F32)
     blocks = []
-    total = fac[...]
-    for e in range(both.shape[0] // SEQ):
+    for e in range(tokens // SEQ):
         rows = both[e * SEQ : (e + 1) * SEQ]
         gram = lax.dot_general(
             rows, rows, (((0,), (0,)), ((), ())), precision=HIGH, preferred_element_type=F32
@@ -80,28 +97,22 @@
     tokens, width = acts.shape
     rank = tab_in.shape[0]
     chunk = 256
-    wide = chunk // SEQ * rank
-    return pl.pallas_call(
-        functools.partial(project_kernel, scale=1.0 / math.sqrt(width)),
-        grid=(tokens // chunk,),
-        in_specs=[
-            pl.BlockSpec((chunk, width), lambda i: (i, 0)),
-            pl.BlockSpec((chunk, width), lambda i: (i, 0)),
-            pl.BlockSpec((rank, width), lambda i: (0, 0), pipeline_mode=pl.Buffered(1)),
-            pl.BlockSpec((rank, width), lambda i: (0, 0), pipeline_mode=pl.Buffered(1)),
-        ],
-        out_specs=[
-            pl.BlockSpec((rank, 2 * rank), lambda i: (0, 0)),
-            pl.BlockSpec((rank, wide), lambda i: (0, i)),
-        ],
+    return pl.pallas_call(
+        functools.partial(project_kernel, scale=1.0 / math.sqrt(width), chunk=chunk),
+        in_specs=[pl.BlockSpec(memory_space=pl.ANY)] * 4,
+        out_specs=[pl.BlockSpec(memory_space=pltpu.VMEM)] * 2,
         out_shape=[
             jax.ShapeDtypeStruct((rank, 2 * rank), F32),
             jax.ShapeDtypeStruct((rank, tokens // SEQ * rank), BF16),
         ],
-        scratch_shapes=[pltpu.VMEM((rank, width), BF16), pltpu.VMEM((rank, width), BF16)],
-        compiler_params=pltpu.CompilerParams(
-            dimension_semantics=("arbitrary",), vmem_limit_bytes=60 * 2**20
-        ),
+        scratch_shapes=[
+            pltpu.VMEM((tokens, width), BF16),
+            pltpu.VMEM((tokens, width), BF16),
+            pltpu.VMEM((rank, width), jnp.int32),
+            pltpu.VMEM((rank, width), jnp.int32),
+            pltpu.SemaphoreType.DMA((4 * width // chunk,)),
+        ],
+        compiler_params=pltpu.CompilerParams(vmem_limit_bytes=53 * 2**20 + 2**18),
         cost_estimate=pl.CostEstimate(
             flops=4 * tokens * width * rank, bytes_accessed=10 * 2**20, transcendentals=0
         ),
@@ -160,7 +171,7 @@
     return hi, (value - hi.astype(F32)).astype(BF16)
 
 
-def whiten_kernel(fac, outer, out, held, *, tokens):
+def invert_kernel(fac, out, *, tokens):
     rank = fac.shape[0]
     mat = fac[...] / tokens
     lane = lax.broadcasted_iota(jnp.int32, (rank, 2 * rank), 1)
@@ -170,23 +181,43 @@
     ridge_in = DAMPING * jnp.sum(jnp.where(left, diag, 0.0), keepdims=True) / rank
     ridge_out = DAMPING * jnp.sum(jnp.where(left, 0.0, diag), keepdims=True) / rank
     ridge = jnp.where(left, ridge_in, ridge_out)
-    mat = invert_pair(mat + jnp.where((lane & (rank - 1)) == row, ridge, 0.0))
+    out[...] = invert_pair(mat + jnp.where((lane & (rank - 1)) == row, ridge, 0.0))
+
+
+def invert(fac, tokens):
+    return pl.pallas_call(
+        functools.partial(invert_kernel, tokens=tokens),
+        out_shape=jax.ShapeDtypeStruct(fac.shape, F32),
+        compiler_params=pltpu.CompilerParams(vmem_limit_bytes=4 * 2**20),
+        cost_estimate=pl.CostEstimate(
+            flops=25 * 10**8, bytes_accessed=2**16, transcendentals=0
+        ),
+        name="invert",
+    )(fac)
+
+
+def whiten_kernel(inverses, near, far, out, held):
+    rank = inverses.shape[0]
+    mat = inverses[...]
     inv_in = mat[:, :rank]
     inv_out = mat[:, rank:]
     out_hi, out_lo = halves(inv_out)
     four = 4 * rank
     rows4 = lax.broadcasted_iota(jnp.int32, (four, four), 0) // rank
     cols4 = lax.broadcasted_iota(jnp.int32, (four, four), 1) // rank
-    wide = jnp.concatenate([inv_in] * 4, axis=1)
-    wide = jnp.concatenate([wide] * 4, axis=0)
-    in_hi, in_lo = halves(jnp.where(rows4 == cols4, wide, 0.0))
+    tiled = jnp.concatenate([inv_in] * 4, axis=1)
+    tiled = jnp.concatenate([tiled] * 4, axis=0)
+    in_hi, in_lo = halves(jnp.where(rows4 == cols4, tiled, 0.0))
     dot = functools.partial(jnp.dot, preferred_element_type=F32)
-    places = outer.shape[0] // rank
+    half = near.shape[0] // rank
+    places = 2 * half
+    wide = near.shape[1]
     for p in range(places):
-        part = outer[p * rank : (p + 1) * rank]
+        at = p % half * rank
+        part = (near if p < half else far)[at : at + rank, :]
         first = dot(out_hi, part) + dot(out_lo, part)
         hi, lo = halves(first)
-        for c in range(outer.shape[1] // four):
+        for c in range(wide // four):
             cut = slice(c * four, (c + 1) * four)
             held[p, :, cut] = dot(hi[:, cut], in_hi) + (
                 dot(hi[:, cut], in_lo) + dot(lo[:, cut], in_hi)
@@ -196,7 +227,7 @@
         even = held[:, o, :]
         odd = held[:, o + 1, :]
         pieces = []
-        for pair in range(outer.shape[1] // (2 * rank)):
+        for pair in range(wide // (2 * rank)):
             cut = slice(pair * 2 * rank, (pair + 1) * 2 * rank)
             a, b = even[:, cut], odd[:, cut]
             pieces.append(jnp.where(low, a, pltpu.roll(b, rank, 1)))
@@ -204,20 +235,20 @@
         out[:, o * rank : (o + 2) * rank] = jnp.concatenate(pieces, axis=0).astype(BF16)
 
 
-def whiten(fac, outer, tokens):
-    rank = fac.shape[0]
-    places = outer.shape[0] // rank
-    examples = outer.shape[1] // rank
-    return pl.pallas_call(
-        functools.partial(whiten_kernel, tokens=tokens),
+def whiten(inverses, near, far):
+    rank = inverses.shape[0]
+    places = 2 * near.shape[0] // rank
+    examples = near.shape[1] // rank
+    return pl.pallas_call(
+        whiten_kernel,
         out_shape=jax.ShapeDtypeStruct((places * examples, rank * rank), BF16),
-        scratch_shapes=[pltpu.VMEM((places, rank, outer.shape[1]), F32)],
+        scratch_shapes=[pltpu.VMEM((places, rank, near.shape[1]), F32)],
         compiler_params=pltpu.CompilerParams(vmem_limit_bytes=16 * 2**20),
         cost_estimate=pl.CostEstimate(
-            flops=12 * 512 * 512 * 256, bytes_accessed=2**20, transcendentals=0
+            flops=60 * 10**8, bytes_accessed=2**20, transcendentals=0
         ),
         name="whiten",
-    )(fac, outer)
+    )(inverses, near, far)
 
 
 def score_kernel(layout, train, near, far, out, held, *, places):
@@ -279,36 +310,43 @@
         out_shape=jax.ShapeDtypeStruct(
             (2 * parts.shape[1], places * parts.shape[2] // 2), F32
         ),
+        compiler_params=pltpu.CompilerParams(vmem_limit_bytes=4 * 2**20),
         name="collect",
     )(parts)
 
 
 def per_device(acts, out_grads, proj_in, proj_out, query_grads):
     places, groups = lax.axis_size("z"), lax.axis_size(("yh", "core"))
-    near = query_grads[0]
-    near = jnp.concatenate([near, swap(near, "x", RING4[0])], axis=0)
+    tie = lax.optimization_barrier
+    own = query_grads[0]
+    got = swap(own, "x", RING4[0])
     layout = jnp.asarray(layouts())[
         lax.axis_index("yl"), lax.axis_index("x"), lax.axis_index("z")
     ]
     fac, outer = project(acts[0], out_grads[0], proj_in[0], proj_out[0])
-    fac, near = lax.optimization_barrier((fac, near))
+    fac, outer, own, got = tie((fac, outer, own, got))
+    seen = swap(outer, "z", RING8[0])
     fac = fac + swap(fac, "yl", PAIR)
-    outer = jnp.concatenate([outer, swap(outer, "z", RING8[0])], axis=0)
-    fac, near = lax.optimization_barrier((fac, near))
+    own = jnp.concatenate([own, got], axis=0)
+    got = swap(own, "x", RING4[1])
     fac = fac + swap(fac, "z", RING8[0])
-    near = jnp.concatenate([near, swap(near, "x", RING4[1])], axis=0)
-    fac, outer = lax.optimization_barrier((fac, outer))
+    fac, outer, seen = tie((fac, outer, seen))
+    outer = jnp.concatenate([outer, seen], axis=0)
+    seen = swap(outer, "z", RING8[1])
     fac = fac + swap(fac, "z", RING8[1])
-    outer = jnp.concatenate([outer, swap(outer, "z", RING8[1])], axis=0)
-    fac, near = lax.optimization_barrier((fac, near))
+    fac, own, got = tie((fac, own, got))
+    near = jnp.concatenate([own, got], axis=0)
+    far = swap(near, "yl", PAIR)
     fac = fac + swap(fac, "z", RING8[2])
-    far = swap(near, "yl", PAIR)
-    fac, outer = lax.optimization_barrier((fac, outer))
+    fac, outer, seen = tie((fac, outer, seen))
+    outer = jnp.concatenate([outer, seen], axis=0)
+    seen = swap(outer, "z", RING8[2])
     fac = fac + swap(fac, "x", RING4[0])
-    outer = jnp.concatenate([outer, swap(outer, "z", RING8[2])], axis=0)
     fac = fac + swap(fac, "x", RING4[1])
     tokens = acts.shape[1] * lax.axis_size(("yl", "x", "z"))
-    train = whiten(fac, outer, tokens)
+    inverses = invert(fac, tokens)
+    inverses, outer, seen = tie((inverses, outer, seen))
+    train = whiten(inverses, outer, seen)
     parts = score(layout, train, near, far, places)
     parts = lax.all_to_all(parts, ("z", "yh", "core"), 0, 0, tiled=True)
     return collect(parts, groups).T

time: 79.1 us -> 72.1 us (0.912)
  Pallas kernels: 15.6 us -> 13.4 us
  other arithmetic: 1.8 us -> 0.03 us
  waiting for transfers between devices: 12.7 us -> 11.3 us
  starting transfers between devices: 23.6 us -> 22.5 us
    pallas_call x1, Pallas kernels: 7.26 us -> 5.73 us  [project(): pl.pallas_call(functools.partial(project_kernel, scale=1.0 / math.sqrt(wi...]
    ppermute x12, waiting for transfers between devices: 12.7 us -> 11.3 us  [swap(): return lax.ppermute(value, axis, pairs + [(b, a) for a, b in pairs])]
    ppermute x12, starting transfers between devices: 23.6 us -> 22.5 us  [swap(): return lax.ppermute(value, axis, pairs + [(b, a) for a, b in pairs])]
    concatenate x5 -> x0, other arithmetic: 1.01 us -> none  [the longest x1 0.85 us: per_device(): outer = jnp.concatenate([outer, swap(outer, 'z', RING8[0])], axis=0)]
    pallas_call x1, Pallas kernels: 1.54 us -> 0.7 us  [collect(): pl.pallas_call(functools.partial(collect_kernel, groups=groups), out_shap...]
    pallas_call x1 -> x2, Pallas kernels: 5.2 us -> 5.42 us  [the longest x1 2.88 us: invert(): pl.pallas_call(functools.partial(invert_kernel, tokens=tokens), out_shape...]
  transfers between devices with their start and end apart: 12 -> 12, of which waited for: 7 -> 6; matrix products, arithmetic and copies ran while one was open for 2% -> 1% of each run, Pallas kernels for 16% -> 15%
where the time goes in v3:
time: 72.1 us; the launch traced here: 72 us
  blocking collectives  23.7 us (33%)
  starting transfers between devices  22.5 us (31%)
  Pallas kernels  13.4 us (19%)
  waiting for transfers between devices  11.3 us (16%)
  local copies, waits for them, and re-layouts  0.84 us (1%)
    all_to_all x1, blocking collectives, per_device(): parts = lax.all_to_all(parts, ('z', 'yh', 'core'), 0, 0, tiled=True)  23.7 us
    ppermute x12, starting transfers between devices, swap(): return lax.ppermute(value, axis, pairs + [(b, a) for a, b in pairs])  22.5 us
    ppermute x12, waiting for transfers between devices, swap(): return lax.ppermute(value, axis, pairs + [(b, a) for a, b in pairs])  11.3 us
    pallas_call x1, Pallas kernels, project(): pl.pallas_call(functools.partial(project_kernel, scale=1.0 / math.sqrt(wi...  5.73 us
    pallas_call x1, Pallas kernels, invert(): pl.pallas_call(functools.partial(invert_kernel, tokens=tokens), out_shape...  2.88 us
    pallas_call x1, Pallas kernels, whiten(): pl.pallas_call(whiten_kernel, out_shape=jax.ShapeDtypeStruct((places * ex...  2.54 us
    pallas_call x1, Pallas kernels, score(): pl.pallas_call(functools.partial(score_kernel, places=places), out_shape=...  1.57 us
  transfers between devices with their start and end apart: 12, of which 6 were waited for; matrix products, arithmetic and copies ran while one was open for 1% of the time, Pallas kernels for 15%

profile of v3, /device:TPU:1, one launch (start us, length us, event | category | flops | bytes accessed | tf_op | source)
XLA Modules:
  0.0 72.0 jit_solution(7416001835458234874)
XLA Ops:
  0.0 2.0 %collective-permute-start = (bf16[32,4096]{1,0:T(8,128)(2,1)}, bf16[32,4096]{1,0:T(8,128)(2,1)S(1)}, u32[]{:S(2)}, u32[]{:S(2)}) collective-permute-start(bf16[32,4096]{1,0:T(8,128)(2,1)} %bitcast.12), channel_id=1, source_target_pairs={{0,32},{64,96},{32,0},{96,64},{1,33},{65,97},{33,1},{97,65},{2,34}... | collective-permute-start | bytes 786440 | tf_op jit(solution)/shard_map/ppermute | solution.py:28
  2.0 5.7 %project.1 = (f32[64,128]{1,0:T(8,128)S(1)}, bf16[64,512]{1,0:T(8,128)(2,1)S(1)}) custom-call(bf16[512,4096]{1,0:T(8,128)(2,1)} %bitcast.8, bf16[512,4096]{1,0:T(8,128)(2,1)} %bitcast.9, s32[64,4096]{1,0:T(8,128)} %bitcast.10, s32[64,4096]{1,0:T(8,128)} %bitcast.11), custom_call_target="tpu_custom_call" | custom-call | flops 536870912 | bytes 10485760 | tf_op jit(solution)/shard_map/project/pallas_call | solution.py:100
  7.9 3.0 %collective-permute-start.5 = (bf16[64,4096]{1,0:T(8,128)(2,1)S(1)}, bf16[64,4096]{1,0:T(8,128)(2,1)S(1)}, u32[]{:S(2)}, u32[]{:S(2)}) collective-permute-start(bf16[64,4096]{1,0:T(8,128)(2,1)S(1)} %constant_dynamic-update-slice_fusion), channel_id=1, source_target_pairs={{32,64},{96,0},{64,32},{0,96},{33,65},{97,1},{65,33},{1,97},{34,66... | collective-permute-start | bytes 1572872 | tf_op jit(solution)/shard_map/ppermute | solution.py:28
  10.8 1.3 %collective-permute-start.1 = (f32[64,128]{1,0:T(8,128)S(1)}, f32[64,128]{1,0:T(8,128)S(1)}, u32[]{:S(2)}, u32[]{:S(2)}) collective-permute-start(f32[64,128]{1,0:T(8,128)S(1)} %get-tuple-element.25), channel_id=1, source_target_pairs={{0,128},{128,0},{1,129},{129,1},{2,130},{130,2},{3,131},{131,3},{4... | collective-permute-start | bytes 98312 | tf_op jit(solution)/shard_map/ppermute | solution.py:28
  12.1 1.6 %collective-permute-start.3 = (bf16[64,512]{1,0:T(8,128)(2,1)S(1)}, bf16[64,512]{1,0:T(8,128)(2,1)S(1)}, u32[]{:S(2)}, u32[]{:S(2)}) collective-permute-start(bf16[64,512]{1,0:T(8,128)(2,1)S(1)} %get-tuple-element.31), channel_id=1, source_target_pairs={{0,4},{8,12},{16,20},{24,28},{4,0},{12,8},{20,16},{28,24},{1,5},{9... | collective-permute-start | bytes 196616 | tf_op jit(solution)/shard_map/ppermute | solution.py:28
  13.8 1.5 %collective-permute-start.2 = (f32[64,128]{1,0:T(8,128)S(1)}, f32[64,128]{1,0:T(8,128)S(1)}, u32[]{:S(2)}, u32[]{:S(2)}) collective-permute-start(f32[64,128]{1,0:T(8,128)S(1)} %add.30), channel_id=1, source_target_pairs={{0,4},{8,12},{16,20},{24,28},{4,0},{12,8},{20,16},{28,24},{1,5},{9... | collective-permute-start | bytes 98312 | tf_op jit(solution)/shard_map/ppermute | solution.py:28
  15.2 1.7 %collective-permute-done.2 = f32[64,128]{1,0:T(8,128)S(1)} collective-permute-done((f32[64,128]{1,0:T(8,128)S(1)}, f32[64,128]{1,0:T(8,128)S(1)}, u32[]{:S(2)}, u32[]{:S(2)}) %collective-permute-start.2) | collective-permute-done | bytes 32800 | tf_op jit(solution)/shard_map/ppermute | solution.py:28
  16.9 5.4 %collective-permute-start.4 = (f32[64,128]{1,0:T(8,128)S(1)}, f32[64,128]{1,0:T(8,128)S(1)}, u32[]{:S(2)}, u32[]{:S(2)}) collective-permute-start(f32[64,128]{1,0:T(8,128)S(1)} %add.31), channel_id=1, source_target_pairs={{4,8},{12,16},{20,24},{28,0},{8,4},{16,12},{24,20},{0,28},{5,9},{1... | collective-permute-start | bytes 98312 | tf_op jit(solution)/shard_map/ppermute | solution.py:28
  22.4 0.1 collective-permute-start.7
  22.5 1.2 %collective-permute-done.4 = f32[64,128]{1,0:T(8,128)S(1)} collective-permute-done((f32[64,128]{1,0:T(8,128)S(1)}, f32[64,128]{1,0:T(8,128)S(1)}, u32[]{:S(2)}, u32[]{:S(2)}) %collective-permute-start.4) | collective-permute-done | bytes 32800 | tf_op jit(solution)/shard_map/ppermute | solution.py:28
  23.7 2.1 %collective-permute-start.6 = (f32[64,128]{1,0:T(8,128)S(1)}, f32[64,128]{1,0:T(8,128)S(1)}, u32[]{:S(2)}, u32[]{:S(2)}) collective-permute-start(f32[64,128]{1,0:T(8,128)S(1)} %add.32), channel_id=1, source_target_pairs={{4,24},{8,20},{0,12},{28,16},{24,4},{20,8},{12,0},{16,28},{5,25},{... | collective-permute-start | bytes 98312 | tf_op jit(solution)/shard_map/ppermute | solution.py:28
  25.9 1.6 %collective-permute-start.11 = (bf16[128,4096]{1,0:T(8,128)(2,1)S(1)}, bf16[128,4096]{1,0:T(8,128)(2,1)S(1)}, u32[]{:S(2)}, u32[]{:S(2)}) collective-permute-start(bf16[128,4096]{1,0:T(8,128)(2,1)S(1)} %constant_dynamic-update-slice_fusion.6.near), channel_id=1, source_target_pairs={{0,128},{128,0},{1,129},{129,1},{2,130},{130,2},{3,131},{131,3},{4... | collective-permute-start | bytes 3145736 | tf_op jit(solution)/shard_map/ppermute | solution.py:28
  27.5 0.9 %collective-permute-done.6 = f32[64,128]{1,0:T(8,128)S(1)} collective-permute-done((f32[64,128]{1,0:T(8,128)S(1)}, f32[64,128]{1,0:T(8,128)S(1)}, u32[]{:S(2)}, u32[]{:S(2)}) %collective-permute-start.6) | collective-permute-done | bytes 32800 | tf_op jit(solution)/shard_map/ppermute | solution.py:28
  28.6 2.0 %collective-permute-start.10 = (bf16[256,512]{1,0:T(8,128)(2,1)S(1)}, bf16[256,512]{1,0:T(8,128)(2,1)S(1)}, u32[]{:S(2)}, u32[]{:S(2)}) collective-permute-start(bf16[256,512]{1,0:T(8,128)(2,1)S(1)} %constant_dynamic-update-slice_fusion.4.near), channel_id=1, source_target_pairs={{4,24},{8,20},{0,12},{28,16},{24,4},{20,8},{12,0},{16,28},{5,25},{... | collective-permute-start | bytes 786440 | tf_op jit(solution)/shard_map/ppermute | solution.py:28
  30.6 1.0 %collective-permute-done.8 = f32[64,128]{1,0:T(8,128)S(1)} collective-permute-done((f32[64,128]{1,0:T(8,128)S(1)}, f32[64,128]{1,0:T(8,128)S(1)}, u32[]{:S(2)}, u32[]{:S(2)}) %collective-permute-start.8) | collective-permute-done | bytes 32800 | tf_op jit(solution)/shard_map/ppermute | solution.py:28
  31.6 1.8 %collective-permute-start.9 = (f32[64,128]{1,0:T(8,128)S(1)}, f32[64,128]{1,0:T(8,128)S(1)}, u32[]{:S(2)}, u32[]{:S(2)}) collective-permute-start(f32[64,128]{1,0:T(8,128)S(1)} %add.34), channel_id=1, source_target_pairs={{32,64},{96,0},{64,32},{0,96},{33,65},{97,1},{65,33},{1,97},{34,66... | collective-permute-start | bytes 98312 | tf_op jit(solution)/shard_map/ppermute | solution.py:28
  33.3 0.7 dynamic-slice_bitcast_fusion.layout
  34.0 1.5 %collective-permute-done.9 = f32[64,128]{1,0:T(8,128)S(1)} collective-permute-done((f32[64,128]{1,0:T(8,128)S(1)}, f32[64,128]{1,0:T(8,128)S(1)}, u32[]{:S(2)}, u32[]{:S(2)}) %collective-permute-start.9) | collective-permute-done | bytes 32800 | tf_op jit(solution)/shard_map/ppermute | solution.py:28
  35.6 2.9 %invert.1.inverses = f32[64,128]{1,0:T(8,128)S(1)} custom-call(f32[64,128]{1,0:T(8,128)S(1)} %add.35.fac), custom_call_target="tpu_custom_call" | custom-call | flops 2500000000 | bytes 65536 | tf_op jit(solution)/shard_map/invert/pallas_call | solution.py:188
  38.5 2.5 %whiten.1.train = bf16[64,4096]{1,0:T(8,128)(2,1)S(1)} custom-call(f32[64,128]{1,0:T(8,128)S(1)} %invert.1.inverses, bf16[256,512]{1,0:T(8,128)(2,1)S(1)} %constant_dynamic-update-slice_fusion.4.near, bf16[256,512]{1,0:T(8,128)(2,1)S(1)} %collective-permute-done.10.far), custom_call_target="tpu_custom_call" | custom-call | flops 6000000000 | bytes 1048576 | tf_op jit(solution)/shard_map/whiten/pallas_call | solution.py:242
  41.0 5.0 %collective-permute-done.11.far = bf16[128,4096]{1,0:T(8,128)(2,1)S(1)} collective-permute-done((bf16[128,4096]{1,0:T(8,128)(2,1)S(1)}, bf16[128,4096]{1,0:T(8,128)(2,1)S(1)}, u32[]{:S(2)}, u32[]{:S(2)}) %collective-permute-start.11) | collective-permute-done | bytes 1048608 | tf_op jit(solution)/shard_map/ppermute | solution.py:28
  46.0 1.6 %score.1 = f32[32,4,128]{2,1,0:T(4,128)S(1)} custom-call(s32[16]{0:T(128)S(1)} %dynamic-slice_bitcast_fusion.layout, bf16[64,4096]{1,0:T(8,128)(2,1)S(1)} %whiten.1.train, bf16[128,4096]{1,0:T(8,128)(2,1)S(1)} %constant_dynamic-update-slice_fusion.6.near, bf16[128,4096]{1,0:T(8,128)(2,1)S(1)} %collective-permute-done.11.far), custom_call_target="tpu_custom_call" | custom-call | flops 134217728 | bytes 3145728 | tf_op jit(solution)/shard_map/score/pallas_call | solution.py:274
  47.6 23.7 %all_to_all.5.parts = f32[32,4,128]{2,1,0:T(4,128)S(1)} all-to-all(f32[32,4,128]{2,1,0:T(4,128)S(1)} %score.1), channel_id=1, replica_groups=mesh['yl'=2,'x'=4,'z'=8,'yh'=2,'core'=2] {'z','yh','core'}, dimensions={0} | all-to-all | bytes 131072 | tf_op jit(solution)/shard_map/all_to_all | solution.py:351
  71.3 0.7 collect.1
  (23 shorter events, 0.3 us)
Async XLA Ops:
  0.0 7.8 %collective-permute-start = (bf16[32,4096]{1,0:T(8,128)(2,1)}, bf16[32,4096]{1,0:T(8,128)(2,1)S(1)}, u32[]{:S(2)}, u32[]{:S(2)}) collective-permute-start(bf16[32,4096]{1,0:T(8,128)(2,1)} %bitcast.12), channel_id=1, source_target_pairs={{0,32},{64,96},{32,0},{96,64},{1,33},{65,97},{33,1},{97,65},{2,34}... | collective-permute-start | bytes 786440 | tf_op jit(solution)/shard_map/ppermute | solution.py:28
  2.0 5.8 %copy-start = (bf16[1,32,4096]{2,1,0:T(8,128)(2,1)S(1)}, bf16[1,32,4096]{2,1,0:T(8,128)(2,1)}, u32[]{:S(2)}) copy-start(bf16[1,32,4096]{2,1,0:T(8,128)(2,1)} %param.10) | copy-start | bytes 786436
  7.9 15.8 %collective-permute-start.5 = (bf16[64,4096]{1,0:T(8,128)(2,1)S(1)}, bf16[64,4096]{1,0:T(8,128)(2,1)S(1)}, u32[]{:S(2)}, u32[]{:S(2)}) collective-permute-start(bf16[64,4096]{1,0:T(8,128)(2,1)S(1)} %constant_dynamic-update-slice_fusion), channel_id=1, source_target_pairs={{32,64},{96,0},{64,32},{0,96},{33,65},{97,1},{65,33},{1,97},{34,66... | collective-permute-start | bytes 1572872 | tf_op jit(solution)/shard_map/ppermute | solution.py:28
  10.8 2.9 %collective-permute-start.1 = (f32[64,128]{1,0:T(8,128)S(1)}, f32[64,128]{1,0:T(8,128)S(1)}, u32[]{:S(2)}, u32[]{:S(2)}) collective-permute-start(f32[64,128]{1,0:T(8,128)S(1)} %get-tuple-element.25), channel_id=1, source_target_pairs={{0,128},{128,0},{1,129},{129,1},{2,130},{130,2},{3,131},{131,3},{4... | collective-permute-start | bytes 98312 | tf_op jit(solution)/shard_map/ppermute | solution.py:28
  12.1 4.8 %collective-permute-start.3 = (bf16[64,512]{1,0:T(8,128)(2,1)S(1)}, bf16[64,512]{1,0:T(8,128)(2,1)S(1)}, u32[]{:S(2)}, u32[]{:S(2)}) collective-permute-start(bf16[64,512]{1,0:T(8,128)(2,1)S(1)} %get-tuple-element.31), channel_id=1, source_target_pairs={{0,4},{8,12},{16,20},{24,28},{4,0},{12,8},{20,16},{28,24},{1,5},{9... | collective-permute-start | bytes 196616 | tf_op jit(solution)/shard_map/ppermute | solution.py:28
  13.8 3.1 %collective-permute-start.2 = (f32[64,128]{1,0:T(8,128)S(1)}, f32[64,128]{1,0:T(8,128)S(1)}, u32[]{:S(2)}, u32[]{:S(2)}) collective-permute-start(f32[64,128]{1,0:T(8,128)S(1)} %add.30), channel_id=1, source_target_pairs={{0,4},{8,12},{16,20},{24,28},{4,0},{12,8},{20,16},{28,24},{1,5},{9... | collective-permute-start | bytes 98312 | tf_op jit(solution)/shard_map/ppermute | solution.py:28
  16.9 6.7 %collective-permute-start.4 = (f32[64,128]{1,0:T(8,128)S(1)}, f32[64,128]{1,0:T(8,128)S(1)}, u32[]{:S(2)}, u32[]{:S(2)}) collective-permute-start(f32[64,128]{1,0:T(8,128)S(1)} %add.31), channel_id=1, source_target_pairs={{4,8},{12,16},{20,24},{28,0},{8,4},{16,12},{24,20},{0,28},{5,9},{1... | collective-permute-start | bytes 98312 | tf_op jit(solution)/shard_map/ppermute | solution.py:28
  22.4 6.1 %collective-permute-start.7 = (bf16[128,512]{1,0:T(8,128)(2,1)S(1)}, bf16[128,512]{1,0:T(8,128)(2,1)S(1)}, u32[]{:S(2)}, u32[]{:S(2)}) collective-permute-start(bf16[128,512]{1,0:T(8,128)(2,1)S(1)} %constant_dynamic-update-slice_fusion.2), channel_id=1, source_target_pairs={{4,8},{12,16},{20,24},{28,0},{8,4},{16,12},{24,20},{0,28},{5,9},{1... | collective-permute-start | bytes 393224 | tf_op jit(solution)/shard_map/ppermute | solution.py:28
  23.7 4.8 %collective-permute-start.6 = (f32[64,128]{1,0:T(8,128)S(1)}, f32[64,128]{1,0:T(8,128)S(1)}, u32[]{:S(2)}, u32[]{:S(2)}) collective-permute-start(f32[64,128]{1,0:T(8,128)S(1)} %add.32), channel_id=1, source_target_pairs={{4,24},{8,20},{0,12},{28,16},{24,4},{20,8},{12,0},{16,28},{5,25},{... | collective-permute-start | bytes 98312 | tf_op jit(solution)/shard_map/ppermute | solution.py:28
  25.9 20.1 %collective-permute-start.11 = (bf16[128,4096]{1,0:T(8,128)(2,1)S(1)}, bf16[128,4096]{1,0:T(8,128)(2,1)S(1)}, u32[]{:S(2)}, u32[]{:S(2)}) collective-permute-start(bf16[128,4096]{1,0:T(8,128)(2,1)S(1)} %constant_dynamic-update-slice_fusion.6.near), channel_id=1, source_target_pairs={{0,128},{128,0},{1,129},{129,1},{2,130},{130,2},{3,131},{131,3},{4... | collective-permute-start | bytes 3145736 | tf_op jit(solution)/shard_map/ppermute | solution.py:28
  28.4 3.1 %collective-permute-start.8 = (f32[64,128]{1,0:T(8,128)S(1)}, f32[64,128]{1,0:T(8,128)S(1)}, u32[]{:S(2)}, u32[]{:S(2)}) collective-permute-start(f32[64,128]{1,0:T(8,128)S(1)} %add.33), channel_id=1, source_target_pairs={{0,32},{64,96},{32,0},{96,64},{1,33},{65,97},{33,1},{97,65},{2,34}... | collective-permute-start | bytes 98312 | tf_op jit(solution)/shard_map/ppermute | solution.py:28
  28.6 9.9 %collective-permute-start.10 = (bf16[256,512]{1,0:T(8,128)(2,1)S(1)}, bf16[256,512]{1,0:T(8,128)(2,1)S(1)}, u32[]{:S(2)}, u32[]{:S(2)}) collective-permute-start(bf16[256,512]{1,0:T(8,128)(2,1)S(1)} %constant_dynamic-update-slice_fusion.4.near), channel_id=1, source_target_pairs={{4,24},{8,20},{0,12},{28,16},{24,4},{20,8},{12,0},{16,28},{5,25},{... | collective-permute-start | bytes 786440 | tf_op jit(solution)/shard_map/ppermute | solution.py:28
  31.6 4.0 %collective-permute-start.9 = (f32[64,128]{1,0:T(8,128)S(1)}, f32[64,128]{1,0:T(8,128)S(1)}, u32[]{:S(2)}, u32[]{:S(2)}) collective-permute-start(f32[64,128]{1,0:T(8,128)S(1)} %add.34), channel_id=1, source_target_pairs={{32,64},{96,0},{64,32},{0,96},{33,65},{97,1},{65,33},{1,97},{34,66... | collective-permute-start | bytes 98312 | tf_op jit(solution)/shard_map/ppermute | solution.py:28

commit v4 on v3

--- a/solution.py
+++ b/solution.py
@@ -18,10 +18,12 @@
 PAIR = [(0, 1)]
 RING4 = [[(0, 1), (2, 3)], [(1, 2), (3, 0)]]
 RING8 = [
+    [(0, 5), (1, 4), (2, 7), (3, 6)],
     [(0, 1), (2, 3), (4, 5), (6, 7)],
     [(1, 2), (3, 4), (5, 6), (7, 0)],
-    [(1, 6), (2, 5), (0, 3), (7, 4)],
 ]
+
+RING8_LAST = [RING8[1], RING8[2], [(1, 6), (2, 5), (0, 3), (7, 4)]]
 
 
 def swap(value, axis, pairs):
@@ -36,6 +38,22 @@
             partner[a], partner[b] = b, a
         held = [held[z] + held[partner[z]] for z in range(size)]
     return held
+
+
+def join_kernel(a, b, out):
+    rows = a.shape[0]
+    out[:rows, :] = a[...]
+    out[rows:, :] = b[...]
+
+
+def join(a, b, work):
+    return pl.pallas_call(
+        join_kernel,
+        out_shape=jax.ShapeDtypeStruct((2 * a.shape[0], a.shape[1]), a.dtype),
+        compiler_params=pltpu.CompilerParams(vmem_limit_bytes=4 * 2**20),
+        cost_estimate=pl.CostEstimate(flops=work, bytes_accessed=2**20, transcendentals=0),
+        name="join",
+    )(a, b)
 
 
 def layouts():
@@ -196,7 +214,8 @@
     )(fac)
 
 
-def whiten_kernel(inverses, near, far, out, held):
+def finish_kernel(layout, inverses, near, far, *refs):
+    queries, (out, held, train, scores) = refs[:4], refs[4:]
     rank = inverses.shape[0]
     mat = inverses[...]
     inv_in = mat[:, :rank]
@@ -232,59 +251,49 @@
             a, b = even[:, cut], odd[:, cut]
             pieces.append(jnp.where(low, a, pltpu.roll(b, rank, 1)))
             pieces.append(jnp.where(low, pltpu.roll(a, rank, 1), b))
-        out[:, o * rank : (o + 2) * rank] = jnp.concatenate(pieces, axis=0).astype(BF16)
-
-
-def whiten(inverses, near, far):
-    rank = inverses.shape[0]
-    places = 2 * near.shape[0] // rank
-    examples = near.shape[1] // rank
-    return pl.pallas_call(
-        whiten_kernel,
-        out_shape=jax.ShapeDtypeStruct((places * examples, rank * rank), BF16),
-        scratch_shapes=[pltpu.VMEM((places, rank, near.shape[1]), F32)],
-        compiler_params=pltpu.CompilerParams(vmem_limit_bytes=16 * 2**20),
-        cost_estimate=pl.CostEstimate(
-            flops=60 * 10**8, bytes_accessed=2**20, transcendentals=0
-        ),
-        name="whiten",
-    )(inverses, near, far)
-
-
-def score_kernel(layout, train, near, far, out, held, *, places):
+        train[:, o * rank : (o + 2) * rank] = jnp.concatenate(pieces, axis=0).astype(BF16)
     nt = (((1,), (1,)), ((), ()))
-    for i, queries in enumerate((near, far)):
-        held[i] = lax.dot_general(train[...], queries[...], nt, preferred_element_type=F32)
-    examples = held.shape[1] // places
-    half = examples // 2
-    run = held.shape[2] // 4
+    for i in range(2):
+        parts = [
+            lax.dot_general(train[...], block[...], nt, preferred_element_type=F32)
+            for block in queries[2 * i : 2 * i + 2]
+        ]
+        scores[i] = jnp.concatenate(parts, axis=1)
+    examples = wide // rank
+    rows_out = examples // 2
+    run = scores.shape[2] // 4
     for p in range(places):
         for i in range(2):
-            rows = held[i, pl.ds(p, examples, places), :]
+            rows = scores[i, pl.ds(p, examples, places), :]
             for j in range(2):
                 pair = rows[:, 2 * j * run : 2 * (j + 1) * run]
                 turned = jnp.concatenate([pair[:, run:], pair[:, :run]], axis=1)
                 cut = jnp.where(layout[places + 4 + j] == 1, turned, pair)
                 target = layout[p] * 4 + layout[places + 2 * i + j]
-                out[target] = jnp.concatenate([cut[:half], cut[half:]], axis=1)
-
-
-def score(layout, train, near, far, places):
-    examples = train.shape[0] // places
-    return pl.pallas_call(
-        functools.partial(score_kernel, places=places),
-        out_shape=jax.ShapeDtypeStruct((places * 4, examples // 2, near.shape[0]), F32),
+                out[target] = jnp.concatenate([cut[:rows_out], cut[rows_out:]], axis=1)
+
+
+def finish(layout, inverses, near, far, queries):
+    rank = inverses.shape[0]
+    places = 2 * near.shape[0] // rank
+    examples = near.shape[1] // rank
+    count = queries[0].shape[0]
+    return pl.pallas_call(
+        finish_kernel,
+        out_shape=jax.ShapeDtypeStruct((places * 4, examples // 2, 2 * count), F32),
         in_specs=[pl.BlockSpec(memory_space=pltpu.SMEM)]
-        + [pl.BlockSpec(memory_space=pltpu.VMEM)] * 3,
-        scratch_shapes=[pltpu.VMEM((2, train.shape[0], near.shape[0]), F32)],
+        + [pl.BlockSpec(memory_space=pltpu.VMEM)] * 7,
+        scratch_shapes=[
+            pltpu.VMEM((places, rank, near.shape[1]), F32),
+            pltpu.VMEM((places * examples, rank * rank), BF16),
+            pltpu.VMEM((2, places * examples, 2 * count), F32),
+        ],
         compiler_params=pltpu.CompilerParams(vmem_limit_bytes=16 * 2**20),
         cost_estimate=pl.CostEstimate(
-            flops=4 * train.shape[0] * train.shape[1] * near.shape[0],
-            bytes_accessed=3 * 2**20,
-            transcendentals=0,
-        ),
-        name="score",
-    )(layout, train, near, far)
+            flops=40 * 10**8, bytes_accessed=2**20, transcendentals=0
+        ),
+        name="finish",
+    )(layout, inverses, near, far, *queries)
 
 
 def collect_kernel(parts, out, *, groups):
@@ -316,7 +325,7 @@
 
 
 def per_device(acts, out_grads, proj_in, proj_out, query_grads):
-    places, groups = lax.axis_size("z"), lax.axis_size(("yh", "core"))
+    groups = lax.axis_size(("yh", "core"))
     tie = lax.optimization_barrier
     own = query_grads[0]
     got = swap(own, "x", RING4[0])
@@ -324,30 +333,28 @@
         lax.axis_index("yl"), lax.axis_index("x"), lax.axis_index("z")
     ]
     fac, outer = project(acts[0], out_grads[0], proj_in[0], proj_out[0])
-    fac, outer, own, got = tie((fac, outer, own, got))
     seen = swap(outer, "z", RING8[0])
     fac = fac + swap(fac, "yl", PAIR)
-    own = jnp.concatenate([own, got], axis=0)
-    got = swap(own, "x", RING4[1])
-    fac = fac + swap(fac, "z", RING8[0])
-    fac, outer, seen = tie((fac, outer, seen))
-    outer = jnp.concatenate([outer, seen], axis=0)
+    fac, own, got = tie((fac, own, got))
+    first = join(own, got, 20 * 10**8)
+    second = swap(first, "x", RING4[1])
+    fac = fac + swap(fac, "z", RING8_LAST[0])
+    fac, first, outer, seen = tie((fac, first, outer, seen))
+    third = swap(first, "yl", PAIR)
+    outer = join(outer, seen, 60 * 10**8)
     seen = swap(outer, "z", RING8[1])
-    fac = fac + swap(fac, "z", RING8[1])
-    fac, own, got = tie((fac, own, got))
-    near = jnp.concatenate([own, got], axis=0)
-    far = swap(near, "yl", PAIR)
-    fac = fac + swap(fac, "z", RING8[2])
-    fac, outer, seen = tie((fac, outer, seen))
-    outer = jnp.concatenate([outer, seen], axis=0)
+    fac = fac + swap(fac, "z", RING8_LAST[1])
+    fac = fac + swap(fac, "z", RING8_LAST[2])
+    fac, outer, seen, second, third = tie((fac, outer, seen, second, third))
+    outer = join(outer, seen, 60 * 10**8)
     seen = swap(outer, "z", RING8[2])
+    fourth = swap(second, "yl", PAIR)
     fac = fac + swap(fac, "x", RING4[0])
     fac = fac + swap(fac, "x", RING4[1])
     tokens = acts.shape[1] * lax.axis_size(("yl", "x", "z"))
     inverses = invert(fac, tokens)
     inverses, outer, seen = tie((inverses, outer, seen))
-    train = whiten(inverses, outer, seen)
-    parts = score(layout, train, near, far, places)
+    parts = finish(layout, inverses, outer, seen, (first, second, third, fourth))
     parts = lax.all_to_all(parts, ("z", "yh", "core"), 0, 0, tiled=True)
     return collect(parts, groups).T
 

time: 72.1 us -> 67.8 us (0.940)
  waiting for transfers between devices: 11.3 us -> 9.13 us
  starting transfers between devices: 22.5 us -> 21.3 us
    ppermute x12 -> x13, waiting for transfers between devices: 11.3 us -> 9.13 us  [swap(): return lax.ppermute(value, axis, pairs + [(b, a) for a, b in pairs])]
    ppermute x12 -> x13, starting transfers between devices: 22.5 us -> 21.3 us  [swap(): return lax.ppermute(value, axis, pairs + [(b, a) for a, b in pairs])]
    pallas_call x2 -> x4, Pallas kernels: 4.11 us -> 3.97 us  [the longest x1 3.91 us: finish(): pl.pallas_call(finish_kernel, out_shape=jax.ShapeDtypeStruct((places * 4,...]
  transfers between devices with their start and end apart: 12 -> 13, of which waited for: 6 -> 7; matrix products, arithmetic and copies ran while one was open for 1% -> 1% of each run, Pallas kernels for 15% -> 13%
where the time goes in v4:
time: 67.8 us; the launch traced here: 67.7 us
  blocking collectives  23.2 us (34%)
  starting transfers between devices  21.3 us (31%)
  Pallas kernels  13.3 us (20%)
  waiting for transfers between devices  9.13 us (13%)
  local copies, waits for them, and re-layouts  0.69 us (1%)
    all_to_all x1, blocking collectives, per_device(): parts = lax.all_to_all(parts, ('z', 'yh', 'core'), 0, 0, tiled=True)  23.2 us
    ppermute x13, starting transfers between devices, swap(): return lax.ppermute(value, axis, pairs + [(b, a) for a, b in pairs])  21.3 us
    ppermute x13, waiting for transfers between devices, swap(): return lax.ppermute(value, axis, pairs + [(b, a) for a, b in pairs])  9.13 us
    pallas_call x1, Pallas kernels, project(): pl.pallas_call(functools.partial(project_kernel, scale=1.0 / math.sqrt(wi...  5.73 us
    pallas_call x1, Pallas kernels, finish(): pl.pallas_call(finish_kernel, out_shape=jax.ShapeDtypeStruct((places * 4,...  3.91 us
    pallas_call x1, Pallas kernels, invert(): pl.pallas_call(functools.partial(invert_kernel, tokens=tokens), out_shape...  2.88 us
  transfers between devices with their start and end apart: 13, of which 7 were waited for; matrix products, arithmetic and copies ran while one was open for 1% of the time, Pallas kernels for 13%

profile of v4, /device:TPU:1, one launch (start us, length us, event | category | flops | bytes accessed | tf_op | source)
XLA Modules:
  0.0 67.7 jit_solution(3538865336434369508)
XLA Ops:
  0.0 2.0 %collective-permute-start.1 = (bf16[32,4096]{1,0:T(8,128)(2,1)}, bf16[32,4096]{1,0:T(8,128)(2,1)S(1)}, u32[]{:S(2)}, u32[]{:S(2)}) collective-permute-start(bf16[32,4096]{1,0:T(8,128)(2,1)} %bitcast.8), channel_id=1, source_target_pairs={{0,32},{64,96},{32,0},{96,64},{1,33},{65,97},{33,1},{97,65},{2,34}... | collective-permute-start | bytes 786440 | tf_op jit(solution)/shard_map/ppermute | solution.py:30
  2.0 5.7 %project.1 = (f32[64,128]{1,0:T(8,128)S(1)}, bf16[64,512]{1,0:T(8,128)(2,1)S(1)}) custom-call(bf16[512,4096]{1,0:T(8,128)(2,1)} %bitcast.10, bf16[512,4096]{1,0:T(8,128)(2,1)} %bitcast.11, s32[64,4096]{1,0:T(8,128)} %bitcast.12, s32[64,4096]{1,0:T(8,128)} %bitcast.13), custom_call_target="tpu_custom_call" | custom-call | flops 536870912 | bytes 10485760 | tf_op jit(solution)/shard_map/project/pallas_call | solution.py:118
  7.8 1.4 %collective-permute-start = (f32[64,128]{1,0:T(8,128)S(1)}, f32[64,128]{1,0:T(8,128)S(1)}, u32[]{:S(2)}, u32[]{:S(2)}) collective-permute-start(f32[64,128]{1,0:T(8,128)S(1)} %get-tuple-element.22), channel_id=1, source_target_pairs={{0,128},{128,0},{1,129},{129,1},{2,130},{130,2},{3,131},{131,3},{4... | collective-permute-start | bytes 98312 | tf_op jit(solution)/shard_map/ppermute | solution.py:30
  9.2 6.5 %collective-permute-start.3 = (bf16[64,512]{1,0:T(8,128)(2,1)S(1)}, bf16[64,512]{1,0:T(8,128)(2,1)S(1)}, u32[]{:S(2)}, u32[]{:S(2)}) collective-permute-start(bf16[64,512]{1,0:T(8,128)(2,1)S(1)} %get-tuple-element.28.a), channel_id=1, source_target_pairs={{0,20},{4,16},{8,28},{12,24},{20,0},{16,4},{28,8},{24,12},{1,21},{... | collective-permute-start | bytes 196616 | tf_op jit(solution)/shard_map/ppermute | solution.py:30
  15.7 0.8 %collective-permute-start.2 = (f32[64,128]{1,0:T(8,128)S(1)}, f32[64,128]{1,0:T(8,128)S(1)}, u32[]{:S(2)}, u32[]{:S(2)}) collective-permute-start(f32[64,128]{1,0:T(8,128)S(1)} %add.30), channel_id=1, source_target_pairs={{0,4},{8,12},{16,20},{24,28},{4,0},{12,8},{20,16},{28,24},{1,5},{9... | collective-permute-start | bytes 98312 | tf_op jit(solution)/shard_map/ppermute | solution.py:30
  16.5 1.9 %collective-permute-start.7 = (bf16[64,4096]{1,0:T(8,128)(2,1)S(1)}, bf16[64,4096]{1,0:T(8,128)(2,1)S(1)}, u32[]{:S(2)}, u32[]{:S(2)}) collective-permute-start(bf16[64,4096]{1,0:T(8,128)(2,1)S(1)} %join.3.refs_0_), channel_id=1, source_target_pairs={{32,64},{96,0},{64,32},{0,96},{33,65},{97,1},{65,33},{1,97},{34,66... | collective-permute-start | bytes 1572872 | tf_op jit(solution)/shard_map/ppermute | solution.py:30
  18.4 0.6 collective-permute-done.2
  19.3 0.9 %collective-permute-start.6 = (bf16[128,512]{1,0:T(8,128)(2,1)S(1)}, bf16[128,512]{1,0:T(8,128)(2,1)S(1)}, u32[]{:S(2)}, u32[]{:S(2)}) collective-permute-start(bf16[128,512]{1,0:T(8,128)(2,1)S(1)} %join.4.a), channel_id=1, source_target_pairs={{0,4},{8,12},{16,20},{24,28},{4,0},{12,8},{20,16},{28,24},{1,5},{9... | collective-permute-start | bytes 393224 | tf_op jit(solution)/shard_map/ppermute | solution.py:30
  20.2 1.7 %collective-permute-start.4 = (f32[64,128]{1,0:T(8,128)S(1)}, f32[64,128]{1,0:T(8,128)S(1)}, u32[]{:S(2)}, u32[]{:S(2)}) collective-permute-start(f32[64,128]{1,0:T(8,128)S(1)} %add.31), channel_id=1, source_target_pairs={{4,8},{12,16},{20,24},{28,0},{8,4},{16,12},{24,20},{0,28},{5,9},{1... | collective-permute-start | bytes 98312 | tf_op jit(solution)/shard_map/ppermute | solution.py:30
  21.9 2.5 %collective-permute-done.4 = f32[64,128]{1,0:T(8,128)S(1)} collective-permute-done((f32[64,128]{1,0:T(8,128)S(1)}, f32[64,128]{1,0:T(8,128)S(1)}, u32[]{:S(2)}, u32[]{:S(2)}) %collective-permute-start.4) | collective-permute-done | bytes 32800 | tf_op jit(solution)/shard_map/ppermute | solution.py:30
  24.5 1.4 %collective-permute-start.5 = (f32[64,128]{1,0:T(8,128)S(1)}, f32[64,128]{1,0:T(8,128)S(1)}, u32[]{:S(2)}, u32[]{:S(2)}) collective-permute-start(f32[64,128]{1,0:T(8,128)S(1)} %add.32), channel_id=1, source_target_pairs={{4,24},{8,20},{0,12},{28,16},{24,4},{20,8},{12,0},{16,28},{5,25},{... | collective-permute-start | bytes 98312 | tf_op jit(solution)/shard_map/ppermute | solution.py:30
  25.8 3.2 %collective-permute-done.5 = f32[64,128]{1,0:T(8,128)S(1)} collective-permute-done((f32[64,128]{1,0:T(8,128)S(1)}, f32[64,128]{1,0:T(8,128)S(1)}, u32[]{:S(2)}, u32[]{:S(2)}) %collective-permute-start.5) | collective-permute-done | bytes 32800 | tf_op jit(solution)/shard_map/ppermute | solution.py:30
  29.0 0.4 collective-permute-done.7.refs_1_
  29.4 0.5 collective-permute-done.8.refs_2_
  30.2 0.4 collective-permute-start.12
  30.6 1.8 %collective-permute-start.11 = (bf16[256,512]{1,0:T(8,128)(2,1)S(1)}, bf16[256,512]{1,0:T(8,128)(2,1)S(1)}, u32[]{:S(2)}, u32[]{:S(2)}) collective-permute-start(bf16[256,512]{1,0:T(8,128)(2,1)S(1)} %join.5.near), channel_id=1, source_target_pairs={{4,8},{12,16},{20,24},{28,0},{8,4},{16,12},{24,20},{0,28},{5,9},{1... | collective-permute-start | bytes 786440 | tf_op jit(solution)/shard_map/ppermute | solution.py:30
  32.3 0.6 collective-permute-done.9
  33.0 2.0 %collective-permute-start.10 = (f32[64,128]{1,0:T(8,128)S(1)}, f32[64,128]{1,0:T(8,128)S(1)}, u32[]{:S(2)}, u32[]{:S(2)}) collective-permute-start(f32[64,128]{1,0:T(8,128)S(1)} %add.34), channel_id=1, source_target_pairs={{32,64},{96,0},{64,32},{0,96},{33,65},{97,1},{65,33},{1,97},{34,66... | collective-permute-start | bytes 98312 | tf_op jit(solution)/shard_map/ppermute | solution.py:30
  35.0 0.7 %dynamic-slice_bitcast_fusion.layout = s32[16]{0:T(128)S(1)} fusion(s32[2,4,8,16]{3,2,1,0:T(8,128)} %constant.26.clone, s32[]{:T(128)S(6)} %select_n.9, s32[]{:T(128)S(6)} %select_n.10, s32[]{:T(128)S(6)} %select_n.11), kind=kLoop, calls=%fused_computation | loop fusion | bytes 140 | tf_op jit(solution)/shard_map/squeeze | solution.py:332
  35.7 1.3 %collective-permute-done.10 = f32[64,128]{1,0:T(8,128)S(1)} collective-permute-done((f32[64,128]{1,0:T(8,128)S(1)}, f32[64,128]{1,0:T(8,128)S(1)}, u32[]{:S(2)}, u32[]{:S(2)}) %collective-permute-start.10) | collective-permute-done | bytes 32800 | tf_op jit(solution)/shard_map/ppermute | solution.py:30
  37.0 2.9 %invert.1.inverses = f32[64,128]{1,0:T(8,128)S(1)} custom-call(f32[64,128]{1,0:T(8,128)S(1)} %add.35.fac), custom_call_target="tpu_custom_call" | custom-call | flops 2500000000 | bytes 65536 | tf_op jit(solution)/shard_map/invert/pallas_call | solution.py:206
  39.9 3.9 %finish.1 = f32[32,4,128]{2,1,0:T(4,128)S(1)} custom-call(s32[16]{0:T(128)S(1)} %dynamic-slice_bitcast_fusion.layout, f32[64,128]{1,0:T(8,128)S(1)} %invert.1.inverses, bf16[256,512]{1,0:T(8,128)(2,1)S(1)} %join.5.near, bf16[256,512]{1,0:T(8,128)(2,1)S(1)} %collective-permute-done.11.far, bf16[64,4096]{1,0:T(8,128)(2,1)S(1)} %join.3.refs_0_, ...), custom_call_target="tpu_custom_call" | custom-call | flops 4000000000 | bytes 1048576 | tf_op jit(solution)/shard_map/finish/pallas_call | solution.py:281
  43.8 23.2 %all_to_all.5.parts = f32[32,4,128]{2,1,0:T(4,128)S(1)} all-to-all(f32[32,4,128]{2,1,0:T(4,128)S(1)} %finish.1), channel_id=1, replica_groups=mesh['yl'=2,'x'=4,'z'=8,'yh'=2,'core'=2] {'z','yh','core'}, dimensions={0} | all-to-all | bytes 131072 | tf_op jit(solution)/shard_map/all_to_all | solution.py:358
  67.0 0.7 %collect.1 = f32[8,512]{1,0:T(8,128)} custom-call(f32[32,4,128]{2,1,0:T(4,128)S(1)} %all_to_all.5.parts), custom_call_target="tpu_custom_call" | custom-call | tf_op jit(solution)/shard_map/collect/pallas_call | solution.py:317
  (19 shorter events, 0.6 us)
Async XLA Ops:
  0.0 15.6 %collective-permute-start.1 = (bf16[32,4096]{1,0:T(8,128)(2,1)}, bf16[32,4096]{1,0:T(8,128)(2,1)S(1)}, u32[]{:S(2)}, u32[]{:S(2)}) collective-permute-start(bf16[32,4096]{1,0:T(8,128)(2,1)} %bitcast.8), channel_id=1, source_target_pairs={{0,32},{64,96},{32,0},{96,64},{1,33},{65,97},{33,1},{97,65},{2,34}... | collective-permute-start | bytes 786440 | tf_op jit(solution)/shard_map/ppermute | solution.py:30
  2.0 14.4 %copy-start = (bf16[1,32,4096]{2,1,0:T(8,128)(2,1)S(1)}, bf16[1,32,4096]{2,1,0:T(8,128)(2,1)}, u32[]{:S(2)}) copy-start(bf16[1,32,4096]{2,1,0:T(8,128)(2,1)} %param.10) | copy-start | bytes 786436
  7.8 7.9 %collective-permute-start = (f32[64,128]{1,0:T(8,128)S(1)}, f32[64,128]{1,0:T(8,128)S(1)}, u32[]{:S(2)}, u32[]{:S(2)}) collective-permute-start(f32[64,128]{1,0:T(8,128)S(1)} %get-tuple-element.22), channel_id=1, source_target_pairs={{0,128},{128,0},{1,129},{129,1},{2,130},{130,2},{3,131},{131,3},{4... | collective-permute-start | bytes 98312 | tf_op jit(solution)/shard_map/ppermute | solution.py:30
  9.2 9.8 %collective-permute-start.3 = (bf16[64,512]{1,0:T(8,128)(2,1)S(1)}, bf16[64,512]{1,0:T(8,128)(2,1)S(1)}, u32[]{:S(2)}, u32[]{:S(2)}) collective-permute-start(bf16[64,512]{1,0:T(8,128)(2,1)S(1)} %get-tuple-element.28.a), channel_id=1, source_target_pairs={{0,20},{4,16},{8,28},{12,24},{20,0},{16,4},{28,8},{24,12},{1,21},{... | collective-permute-start | bytes 196616 | tf_op jit(solution)/shard_map/ppermute | solution.py:30
  15.7 3.3 %collective-permute-start.2 = (f32[64,128]{1,0:T(8,128)S(1)}, f32[64,128]{1,0:T(8,128)S(1)}, u32[]{:S(2)}, u32[]{:S(2)}) collective-permute-start(f32[64,128]{1,0:T(8,128)S(1)} %add.30), channel_id=1, source_target_pairs={{0,4},{8,12},{16,20},{24,28},{4,0},{12,8},{20,16},{28,24},{1,5},{9... | collective-permute-start | bytes 98312 | tf_op jit(solution)/shard_map/ppermute | solution.py:30
  16.5 12.9 %collective-permute-start.7 = (bf16[64,4096]{1,0:T(8,128)(2,1)S(1)}, bf16[64,4096]{1,0:T(8,128)(2,1)S(1)}, u32[]{:S(2)}, u32[]{:S(2)}) collective-permute-start(bf16[64,4096]{1,0:T(8,128)(2,1)S(1)} %join.3.refs_0_), channel_id=1, source_target_pairs={{32,64},{96,0},{64,32},{0,96},{33,65},{97,1},{65,33},{1,97},{34,66... | collective-permute-start | bytes 1572872 | tf_op jit(solution)/shard_map/ppermute | solution.py:30
  19.0 10.9 %collective-permute-start.8 = (bf16[64,4096]{1,0:T(8,128)(2,1)S(1)}, bf16[64,4096]{1,0:T(8,128)(2,1)S(1)}, u32[]{:S(2)}, u32[]{:S(2)}) collective-permute-start(bf16[64,4096]{1,0:T(8,128)(2,1)S(1)} %join.3.refs_0_), channel_id=1, source_target_pairs={{0,128},{128,0},{1,129},{129,1},{2,130},{130,2},{3,131},{131,3},{4... | collective-permute-start | bytes 1572872 | tf_op jit(solution)/shard_map/ppermute | solution.py:30
  19.3 9.8 %collective-permute-start.6 = (bf16[128,512]{1,0:T(8,128)(2,1)S(1)}, bf16[128,512]{1,0:T(8,128)(2,1)S(1)}, u32[]{:S(2)}, u32[]{:S(2)}) collective-permute-start(bf16[128,512]{1,0:T(8,128)(2,1)S(1)} %join.4.a), channel_id=1, source_target_pairs={{0,4},{8,12},{16,20},{24,28},{4,0},{12,8},{20,16},{28,24},{1,5},{9... | collective-permute-start | bytes 393224 | tf_op jit(solution)/shard_map/ppermute | solution.py:30
  20.2 4.3 %collective-permute-start.4 = (f32[64,128]{1,0:T(8,128)S(1)}, f32[64,128]{1,0:T(8,128)S(1)}, u32[]{:S(2)}, u32[]{:S(2)}) collective-permute-start(f32[64,128]{1,0:T(8,128)S(1)} %add.31), channel_id=1, source_target_pairs={{4,8},{12,16},{20,24},{28,0},{8,4},{16,12},{24,20},{0,28},{5,9},{1... | collective-permute-start | bytes 98312 | tf_op jit(solution)/shard_map/ppermute | solution.py:30
  24.5 4.6 %collective-permute-start.5 = (f32[64,128]{1,0:T(8,128)S(1)}, f32[64,128]{1,0:T(8,128)S(1)}, u32[]{:S(2)}, u32[]{:S(2)}) collective-permute-start(f32[64,128]{1,0:T(8,128)S(1)} %add.32), channel_id=1, source_target_pairs={{4,24},{8,20},{0,12},{28,16},{24,4},{20,8},{12,0},{16,28},{5,25},{... | collective-permute-start | bytes 98312 | tf_op jit(solution)/shard_map/ppermute | solution.py:30
  29.9 3.1 %collective-permute-start.9 = (f32[64,128]{1,0:T(8,128)S(1)}, f32[64,128]{1,0:T(8,128)S(1)}, u32[]{:S(2)}, u32[]{:S(2)}) collective-permute-start(f32[64,128]{1,0:T(8,128)S(1)} %add.33), channel_id=1, source_target_pairs={{0,32},{64,96},{32,0},{96,64},{1,33},{65,97},{33,1},{97,65},{2,34}... | collective-permute-start | bytes 98312 | tf_op jit(solution)/shard_map/ppermute | solution.py:30
  30.2 9.7 %collective-permute-start.12 = (bf16[64,4096]{1,0:T(8,128)(2,1)S(1)}, bf16[64,4096]{1,0:T(8,128)(2,1)S(1)}, u32[]{:S(2)}, u32[]{:S(2)}) collective-permute-start(bf16[64,4096]{1,0:T(8,128)(2,1)S(1)} %collective-permute-done.7.refs_1_), channel_id=1, source_target_pairs={{0,128},{128,0},{1,129},{129,1},{2,130},{130,2},{3,131},{131,3},{4... | collective-permute-start | bytes 1572872 | tf_op jit(solution)/shard_map/ppermute | solution.py:30
  30.6 9.3 %collective-permute-start.11 = (bf16[256,512]{1,0:T(8,128)(2,1)S(1)}, bf16[256,512]{1,0:T(8,128)(2,1)S(1)}, u32[]{:S(2)}, u32[]{:S(2)}) collective-permute-start(bf16[256,512]{1,0:T(8,128)(2,1)S(1)} %join.5.near), channel_id=1, source_target_pairs={{4,8},{12,16},{20,24},{28,0},{8,4},{16,12},{24,20},{0,28},{5,9},{1... | collective-permute-start | bytes 786440 | tf_op jit(solution)/shard_map/ppermute | solution.py:30
  33.0 4.0 %collective-permute-start.10 = (f32[64,128]{1,0:T(8,128)S(1)}, f32[64,128]{1,0:T(8,128)S(1)}, u32[]{:S(2)}, u32[]{:S(2)}) collective-permute-start(f32[64,128]{1,0:T(8,128)S(1)} %add.34), channel_id=1, source_target_pairs={{32,64},{96,0},{64,32},{0,96},{33,65},{97,1},{65,33},{1,97},{34,66... | collective-permute-start | bytes 98312 | tf_op jit(solution)/shard_map/ppermute | solution.py:30

commit v5 on v4

--- a/solution.py
+++ b/solution.py
@@ -215,7 +215,7 @@
 
 
 def finish_kernel(layout, inverses, near, far, *refs):
-    queries, (out, held, train, scores) = refs[:4], refs[4:]
+    queries, (out, held, train, scores, his, los) = refs[:4], refs[4:]
     rank = inverses.shape[0]
     mat = inverses[...]
     inv_in = mat[:, :rank]
@@ -231,16 +231,17 @@
     half = near.shape[0] // rank
     places = 2 * half
     wide = near.shape[1]
+    out_both = jnp.concatenate([out_hi, out_lo], axis=0)
     for p in range(places):
         at = p % half * rank
-        part = (near if p < half else far)[at : at + rank, :]
-        first = dot(out_hi, part) + dot(out_lo, part)
-        hi, lo = halves(first)
-        for c in range(wide // four):
-            cut = slice(c * four, (c + 1) * four)
-            held[p, :, cut] = dot(hi[:, cut], in_hi) + (
-                dot(hi[:, cut], in_lo) + dot(lo[:, cut], in_hi)
-            )
+        both = dot(out_both, (near if p < half else far)[at : at + rank, :])
+        hi, lo = halves(both[:rank] + both[rank:])
+        his[p * rank : (p + 1) * rank, :] = hi
+        los[p * rank : (p + 1) * rank, :] = lo
+    for c in range(wide // four):
+        cut = slice(c * four, (c + 1) * four)
+        second = dot(his[:, cut], in_hi) + (dot(his[:, cut], in_lo) + dot(los[:, cut], in_hi))
+        held[:, :, cut] = second.reshape(places, rank, four)
     low = lax.broadcasted_iota(jnp.int32, (places, 2 * rank), 1) < rank
     for o in range(0, rank, 2):
         even = held[:, o, :]
@@ -287,6 +288,8 @@
             pltpu.VMEM((places, rank, near.shape[1]), F32),
             pltpu.VMEM((places * examples, rank * rank), BF16),
             pltpu.VMEM((2, places * examples, 2 * count), F32),
+            pltpu.VMEM((places * rank, near.shape[1]), BF16),
+            pltpu.VMEM((places * rank, near.shape[1]), BF16),
         ],
         compiler_params=pltpu.CompilerParams(vmem_limit_bytes=16 * 2**20),
         cost_estimate=pl.CostEstimate(

time: 67.8 us -> 66.5 us (0.981)
  Pallas kernels: 13.3 us -> 11.9 us
    pallas_call x1, Pallas kernels: 3.91 us -> 2.54 us  [finish(): pl.pallas_call(finish_kernel, out_shape=jax.ShapeDtypeStruct((places * 4,...]
where the time goes in v5:
time: 66.5 us; the launch traced here: 66.3 us
  blocking collectives  23.2 us (35%)
  starting transfers between devices  21.3 us (32%)
  Pallas kernels  11.9 us (18%)
  waiting for transfers between devices  9.13 us (14%)
  local copies, waits for them, and re-layouts  0.69 us (1%)
    all_to_all x1, blocking collectives, per_device(): parts = lax.all_to_all(parts, ('z', 'yh', 'core'), 0, 0, tiled=True)  23.2 us
    ppermute x13, starting transfers between devices, swap(): return lax.ppermute(value, axis, pairs + [(b, a) for a, b in pairs])  21.3 us
    ppermute x13, waiting for transfers between devices, swap(): return lax.ppermute(value, axis, pairs + [(b, a) for a, b in pairs])  9.13 us
    pallas_call x1, Pallas kernels, project(): pl.pallas_call(functools.partial(project_kernel, scale=1.0 / math.sqrt(wi...  5.73 us
    pallas_call x1, Pallas kernels, invert(): pl.pallas_call(functools.partial(invert_kernel, tokens=tokens), out_shape...  2.88 us
    pallas_call x1, Pallas kernels, finish(): pl.pallas_call(finish_kernel, out_shape=jax.ShapeDtypeStruct((places * 4,...  2.54 us
  transfers between devices with their start and end apart: 13, of which 7 were waited for; matrix products, arithmetic and copies ran while one was open for 1% of the time, Pallas kernels for 13%

profile of v5, /device:TPU:1, one launch (start us, length us, event | category | flops | bytes accessed | tf_op | source)
XLA Modules:
  0.0 66.3 jit_solution(471792957660678263)
XLA Ops:
  0.0 2.0 %collective-permute-start.1 = (bf16[32,4096]{1,0:T(8,128)(2,1)}, bf16[32,4096]{1,0:T(8,128)(2,1)S(1)}, u32[]{:S(2)}, u32[]{:S(2)}) collective-permute-start(bf16[32,4096]{1,0:T(8,128)(2,1)} %bitcast.8), channel_id=1, source_target_pairs={{0,32},{64,96},{32,0},{96,64},{1,33},{65,97},{33,1},{97,65},{2,34}... | collective-permute-start | bytes 786440 | tf_op jit(solution)/shard_map/ppermute | solution.py:30
  2.0 5.7 %project.1 = (f32[64,128]{1,0:T(8,128)S(1)}, bf16[64,512]{1,0:T(8,128)(2,1)S(1)}) custom-call(bf16[512,4096]{1,0:T(8,128)(2,1)} %bitcast.10, bf16[512,4096]{1,0:T(8,128)(2,1)} %bitcast.11, s32[64,4096]{1,0:T(8,128)} %bitcast.12, s32[64,4096]{1,0:T(8,128)} %bitcast.13), custom_call_target="tpu_custom_call" | custom-call | flops 536870912 | bytes 10485760 | tf_op jit(solution)/shard_map/project/pallas_call | solution.py:118
  7.8 1.4 %collective-permute-start = (f32[64,128]{1,0:T(8,128)S(1)}, f32[64,128]{1,0:T(8,128)S(1)}, u32[]{:S(2)}, u32[]{:S(2)}) collective-permute-start(f32[64,128]{1,0:T(8,128)S(1)} %get-tuple-element.22), channel_id=1, source_target_pairs={{0,128},{128,0},{1,129},{129,1},{2,130},{130,2},{3,131},{131,3},{4... | collective-permute-start | bytes 98312 | tf_op jit(solution)/shard_map/ppermute | solution.py:30
  9.2 6.5 %collective-permute-start.3 = (bf16[64,512]{1,0:T(8,128)(2,1)S(1)}, bf16[64,512]{1,0:T(8,128)(2,1)S(1)}, u32[]{:S(2)}, u32[]{:S(2)}) collective-permute-start(bf16[64,512]{1,0:T(8,128)(2,1)S(1)} %get-tuple-element.28.a), channel_id=1, source_target_pairs={{0,20},{4,16},{8,28},{12,24},{20,0},{16,4},{28,8},{24,12},{1,21},{... | collective-permute-start | bytes 196616 | tf_op jit(solution)/shard_map/ppermute | solution.py:30
  15.7 0.8 %collective-permute-start.2 = (f32[64,128]{1,0:T(8,128)S(1)}, f32[64,128]{1,0:T(8,128)S(1)}, u32[]{:S(2)}, u32[]{:S(2)}) collective-permute-start(f32[64,128]{1,0:T(8,128)S(1)} %add.30), channel_id=1, source_target_pairs={{0,4},{8,12},{16,20},{24,28},{4,0},{12,8},{20,16},{28,24},{1,5},{9... | collective-permute-start | bytes 98312 | tf_op jit(solution)/shard_map/ppermute | solution.py:30
  16.5 1.9 %collective-permute-start.7 = (bf16[64,4096]{1,0:T(8,128)(2,1)S(1)}, bf16[64,4096]{1,0:T(8,128)(2,1)S(1)}, u32[]{:S(2)}, u32[]{:S(2)}) collective-permute-start(bf16[64,4096]{1,0:T(8,128)(2,1)S(1)} %join.3.refs_0_), channel_id=1, source_target_pairs={{32,64},{96,0},{64,32},{0,96},{33,65},{97,1},{65,33},{1,97},{34,66... | collective-permute-start | bytes 1572872 | tf_op jit(solution)/shard_map/ppermute | solution.py:30
  18.4 0.6 collective-permute-done.2
  19.3 0.9 %collective-permute-start.6 = (bf16[128,512]{1,0:T(8,128)(2,1)S(1)}, bf16[128,512]{1,0:T(8,128)(2,1)S(1)}, u32[]{:S(2)}, u32[]{:S(2)}) collective-permute-start(bf16[128,512]{1,0:T(8,128)(2,1)S(1)} %join.4.a), channel_id=1, source_target_pairs={{0,4},{8,12},{16,20},{24,28},{4,0},{12,8},{20,16},{28,24},{1,5},{9... | collective-permute-start | bytes 393224 | tf_op jit(solution)/shard_map/ppermute | solution.py:30
  20.2 1.7 %collective-permute-start.4 = (f32[64,128]{1,0:T(8,128)S(1)}, f32[64,128]{1,0:T(8,128)S(1)}, u32[]{:S(2)}, u32[]{:S(2)}) collective-permute-start(f32[64,128]{1,0:T(8,128)S(1)} %add.31), channel_id=1, source_target_pairs={{4,8},{12,16},{20,24},{28,0},{8,4},{16,12},{24,20},{0,28},{5,9},{1... | collective-permute-start | bytes 98312 | tf_op jit(solution)/shard_map/ppermute | solution.py:30
  21.9 2.5 %collective-permute-done.4 = f32[64,128]{1,0:T(8,128)S(1)} collective-permute-done((f32[64,128]{1,0:T(8,128)S(1)}, f32[64,128]{1,0:T(8,128)S(1)}, u32[]{:S(2)}, u32[]{:S(2)}) %collective-permute-start.4) | collective-permute-done | bytes 32800 | tf_op jit(solution)/shard_map/ppermute | solution.py:30
  24.5 1.4 %collective-permute-start.5 = (f32[64,128]{1,0:T(8,128)S(1)}, f32[64,128]{1,0:T(8,128)S(1)}, u32[]{:S(2)}, u32[]{:S(2)}) collective-permute-start(f32[64,128]{1,0:T(8,128)S(1)} %add.32), channel_id=1, source_target_pairs={{4,24},{8,20},{0,12},{28,16},{24,4},{20,8},{12,0},{16,28},{5,25},{... | collective-permute-start | bytes 98312 | tf_op jit(solution)/shard_map/ppermute | solution.py:30
  25.8 3.2 %collective-permute-done.5 = f32[64,128]{1,0:T(8,128)S(1)} collective-permute-done((f32[64,128]{1,0:T(8,128)S(1)}, f32[64,128]{1,0:T(8,128)S(1)}, u32[]{:S(2)}, u32[]{:S(2)}) %collective-permute-start.5) | collective-permute-done | bytes 32800 | tf_op jit(solution)/shard_map/ppermute | solution.py:30
  29.0 0.4 collective-permute-done.7.refs_1_
  29.4 0.5 collective-permute-done.8.refs_2_
  30.2 0.4 collective-permute-start.12
  30.6 1.8 %collective-permute-start.11 = (bf16[256,512]{1,0:T(8,128)(2,1)S(1)}, bf16[256,512]{1,0:T(8,128)(2,1)S(1)}, u32[]{:S(2)}, u32[]{:S(2)}) collective-permute-start(bf16[256,512]{1,0:T(8,128)(2,1)S(1)} %join.5.near), channel_id=1, source_target_pairs={{4,8},{12,16},{20,24},{28,0},{8,4},{16,12},{24,20},{0,28},{5,9},{1... | collective-permute-start | bytes 786440 | tf_op jit(solution)/shard_map/ppermute | solution.py:30
  32.3 0.6 collective-permute-done.9
  33.0 2.0 %collective-permute-start.10 = (f32[64,128]{1,0:T(8,128)S(1)}, f32[64,128]{1,0:T(8,128)S(1)}, u32[]{:S(2)}, u32[]{:S(2)}) collective-permute-start(f32[64,128]{1,0:T(8,128)S(1)} %add.34), channel_id=1, source_target_pairs={{32,64},{96,0},{64,32},{0,96},{33,65},{97,1},{65,33},{1,97},{34,66... | collective-permute-start | bytes 98312 | tf_op jit(solution)/shard_map/ppermute | solution.py:30
  35.0 0.7 %dynamic-slice_bitcast_fusion.layout = s32[16]{0:T(128)S(1)} fusion(s32[2,4,8,16]{3,2,1,0:T(8,128)} %constant.26.clone, s32[]{:T(128)S(6)} %select_n.9, s32[]{:T(128)S(6)} %select_n.10, s32[]{:T(128)S(6)} %select_n.11), kind=kLoop, calls=%fused_computation | loop fusion | bytes 140 | tf_op jit(solution)/shard_map/squeeze | solution.py:335
  35.7 1.3 %collective-permute-done.10 = f32[64,128]{1,0:T(8,128)S(1)} collective-permute-done((f32[64,128]{1,0:T(8,128)S(1)}, f32[64,128]{1,0:T(8,128)S(1)}, u32[]{:S(2)}, u32[]{:S(2)}) %collective-permute-start.10) | collective-permute-done | bytes 32800 | tf_op jit(solution)/shard_map/ppermute | solution.py:30
  37.0 2.9 %invert.1.inverses = f32[64,128]{1,0:T(8,128)S(1)} custom-call(f32[64,128]{1,0:T(8,128)S(1)} %add.35.fac), custom_call_target="tpu_custom_call" | custom-call | flops 2500000000 | bytes 65536 | tf_op jit(solution)/shard_map/invert/pallas_call | solution.py:206
  39.9 2.5 %finish.1 = f32[32,4,128]{2,1,0:T(4,128)S(1)} custom-call(s32[16]{0:T(128)S(1)} %dynamic-slice_bitcast_fusion.layout, f32[64,128]{1,0:T(8,128)S(1)} %invert.1.inverses, bf16[256,512]{1,0:T(8,128)(2,1)S(1)} %join.5.near, bf16[256,512]{1,0:T(8,128)(2,1)S(1)} %collective-permute-done.11.far, bf16[64,4096]{1,0:T(8,128)(2,1)S(1)} %join.3.refs_0_, ...), custom_call_target="tpu_custom_call" | custom-call | flops 4000000000 | bytes 1048576 | tf_op jit(solution)/shard_map/finish/pallas_call | solution.py:282
  42.4 23.2 %all_to_all.5.parts = f32[32,4,128]{2,1,0:T(4,128)S(1)} all-to-all(f32[32,4,128]{2,1,0:T(4,128)S(1)} %finish.1), channel_id=1, replica_groups=mesh['yl'=2,'x'=4,'z'=8,'yh'=2,'core'=2] {'z','yh','core'}, dimensions={0} | all-to-all | bytes 131072 | tf_op jit(solution)/shard_map/all_to_all | solution.py:361
  65.6 0.7 %collect.1 = f32[8,512]{1,0:T(8,128)} custom-call(f32[32,4,128]{2,1,0:T(4,128)S(1)} %all_to_all.5.parts), custom_call_target="tpu_custom_call" | custom-call | tf_op jit(solution)/shard_map/collect/pallas_call | solution.py:320
  (19 shorter events, 0.6 us)
Async XLA Ops:
  0.0 15.6 %collective-permute-start.1 = (bf16[32,4096]{1,0:T(8,128)(2,1)}, bf16[32,4096]{1,0:T(8,128)(2,1)S(1)}, u32[]{:S(2)}, u32[]{:S(2)}) collective-permute-start(bf16[32,4096]{1,0:T(8,128)(2,1)} %bitcast.8), channel_id=1, source_target_pairs={{0,32},{64,96},{32,0},{96,64},{1,33},{65,97},{33,1},{97,65},{2,34}... | collective-permute-start | bytes 786440 | tf_op jit(solution)/shard_map/ppermute | solution.py:30
  2.0 14.4 %copy-start = (bf16[1,32,4096]{2,1,0:T(8,128)(2,1)S(1)}, bf16[1,32,4096]{2,1,0:T(8,128)(2,1)}, u32[]{:S(2)}) copy-start(bf16[1,32,4096]{2,1,0:T(8,128)(2,1)} %param.10) | copy-start | bytes 786436
  7.8 7.9 %collective-permute-start = (f32[64,128]{1,0:T(8,128)S(1)}, f32[64,128]{1,0:T(8,128)S(1)}, u32[]{:S(2)}, u32[]{:S(2)}) collective-permute-start(f32[64,128]{1,0:T(8,128)S(1)} %get-tuple-element.22), channel_id=1, source_target_pairs={{0,128},{128,0},{1,129},{129,1},{2,130},{130,2},{3,131},{131,3},{4... | collective-permute-start | bytes 98312 | tf_op jit(solution)/shard_map/ppermute | solution.py:30
  9.2 9.8 %collective-permute-start.3 = (bf16[64,512]{1,0:T(8,128)(2,1)S(1)}, bf16[64,512]{1,0:T(8,128)(2,1)S(1)}, u32[]{:S(2)}, u32[]{:S(2)}) collective-permute-start(bf16[64,512]{1,0:T(8,128)(2,1)S(1)} %get-tuple-element.28.a), channel_id=1, source_target_pairs={{0,20},{4,16},{8,28},{12,24},{20,0},{16,4},{28,8},{24,12},{1,21},{... | collective-permute-start | bytes 196616 | tf_op jit(solution)/shard_map/ppermute | solution.py:30
  15.7 3.3 %collective-permute-start.2 = (f32[64,128]{1,0:T(8,128)S(1)}, f32[64,128]{1,0:T(8,128)S(1)}, u32[]{:S(2)}, u32[]{:S(2)}) collective-permute-start(f32[64,128]{1,0:T(8,128)S(1)} %add.30), channel_id=1, source_target_pairs={{0,4},{8,12},{16,20},{24,28},{4,0},{12,8},{20,16},{28,24},{1,5},{9... | collective-permute-start | bytes 98312 | tf_op jit(solution)/shard_map/ppermute | solution.py:30
  16.5 12.9 %collective-permute-start.7 = (bf16[64,4096]{1,0:T(8,128)(2,1)S(1)}, bf16[64,4096]{1,0:T(8,128)(2,1)S(1)}, u32[]{:S(2)}, u32[]{:S(2)}) collective-permute-start(bf16[64,4096]{1,0:T(8,128)(2,1)S(1)} %join.3.refs_0_), channel_id=1, source_target_pairs={{32,64},{96,0},{64,32},{0,96},{33,65},{97,1},{65,33},{1,97},{34,66... | collective-permute-start | bytes 1572872 | tf_op jit(solution)/shard_map/ppermute | solution.py:30
  19.0 10.9 %collective-permute-start.8 = (bf16[64,4096]{1,0:T(8,128)(2,1)S(1)}, bf16[64,4096]{1,0:T(8,128)(2,1)S(1)}, u32[]{:S(2)}, u32[]{:S(2)}) collective-permute-start(bf16[64,4096]{1,0:T(8,128)(2,1)S(1)} %join.3.refs_0_), channel_id=1, source_target_pairs={{0,128},{128,0},{1,129},{129,1},{2,130},{130,2},{3,131},{131,3},{4... | collective-permute-start | bytes 1572872 | tf_op jit(solution)/shard_map/ppermute | solution.py:30
  19.3 9.8 %collective-permute-start.6 = (bf16[128,512]{1,0:T(8,128)(2,1)S(1)}, bf16[128,512]{1,0:T(8,128)(2,1)S(1)}, u32[]{:S(2)}, u32[]{:S(2)}) collective-permute-start(bf16[128,512]{1,0:T(8,128)(2,1)S(1)} %join.4.a), channel_id=1, source_target_pairs={{0,4},{8,12},{16,20},{24,28},{4,0},{12,8},{20,16},{28,24},{1,5},{9... | collective-permute-start | bytes 393224 | tf_op jit(solution)/shard_map/ppermute | solution.py:30
  20.2 4.3 %collective-permute-start.4 = (f32[64,128]{1,0:T(8,128)S(1)}, f32[64,128]{1,0:T(8,128)S(1)}, u32[]{:S(2)}, u32[]{:S(2)}) collective-permute-start(f32[64,128]{1,0:T(8,128)S(1)} %add.31), channel_id=1, source_target_pairs={{4,8},{12,16},{20,24},{28,0},{8,4},{16,12},{24,20},{0,28},{5,9},{1... | collective-permute-start | bytes 98312 | tf_op jit(solution)/shard_map/ppermute | solution.py:30
  24.5 4.6 %collective-permute-start.5 = (f32[64,128]{1,0:T(8,128)S(1)}, f32[64,128]{1,0:T(8,128)S(1)}, u32[]{:S(2)}, u32[]{:S(2)}) collective-permute-start(f32[64,128]{1,0:T(8,128)S(1)} %add.32), channel_id=1, source_target_pairs={{4,24},{8,20},{0,12},{28,16},{24,4},{20,8},{12,0},{16,28},{5,25},{... | collective-permute-start | bytes 98312 | tf_op jit(solution)/shard_map/ppermute | solution.py:30
  29.9 3.1 %collective-permute-start.9 = (f32[64,128]{1,0:T(8,128)S(1)}, f32[64,128]{1,0:T(8,128)S(1)}, u32[]{:S(2)}, u32[]{:S(2)}) collective-permute-start(f32[64,128]{1,0:T(8,128)S(1)} %add.33), channel_id=1, source_target_pairs={{0,32},{64,96},{32,0},{96,64},{1,33},{65,97},{33,1},{97,65},{2,34}... | collective-permute-start | bytes 98312 | tf_op jit(solution)/shard_map/ppermute | solution.py:30
  30.2 9.7 %collective-permute-start.12 = (bf16[64,4096]{1,0:T(8,128)(2,1)S(1)}, bf16[64,4096]{1,0:T(8,128)(2,1)S(1)}, u32[]{:S(2)}, u32[]{:S(2)}) collective-permute-start(bf16[64,4096]{1,0:T(8,128)(2,1)S(1)} %collective-permute-done.7.refs_1_), channel_id=1, source_target_pairs={{0,128},{128,0},{1,129},{129,1},{2,130},{130,2},{3,131},{131,3},{4... | collective-permute-start | bytes 1572872 | tf_op jit(solution)/shard_map/ppermute | solution.py:30
  30.6 9.3 %collective-permute-start.11 = (bf16[256,512]{1,0:T(8,128)(2,1)S(1)}, bf16[256,512]{1,0:T(8,128)(2,1)S(1)}, u32[]{:S(2)}, u32[]{:S(2)}) collective-permute-start(bf16[256,512]{1,0:T(8,128)(2,1)S(1)} %join.5.near), channel_id=1, source_target_pairs={{4,8},{12,16},{20,24},{28,0},{8,4},{16,12},{24,20},{0,28},{5,9},{1... | collective-permute-start | bytes 786440 | tf_op jit(solution)/shard_map/ppermute | solution.py:30
  33.0 4.0 %collective-permute-start.10 = (f32[64,128]{1,0:T(8,128)S(1)}, f32[64,128]{1,0:T(8,128)S(1)}, u32[]{:S(2)}, u32[]{:S(2)}) collective-permute-start(f32[64,128]{1,0:T(8,128)S(1)} %add.34), channel_id=1, source_target_pairs={{32,64},{96,0},{64,32},{0,96},{33,65},{97,1},{65,33},{1,97},{34,66... | collective-permute-start | bytes 98312 | tf_op jit(solution)/shard_map/ppermute | solution.py:30

commit v6 on v5

--- a/solution.py
+++ b/solution.py
@@ -339,17 +339,17 @@
     seen = swap(outer, "z", RING8[0])
     fac = fac + swap(fac, "yl", PAIR)
     fac, own, got = tie((fac, own, got))
-    first = join(own, got, 20 * 10**8)
+    first = join(own, got, 1 * 10**8)
     second = swap(first, "x", RING4[1])
+    third = swap(first, "yl", PAIR)
     fac = fac + swap(fac, "z", RING8_LAST[0])
-    fac, first, outer, seen = tie((fac, first, outer, seen))
-    third = swap(first, "yl", PAIR)
-    outer = join(outer, seen, 60 * 10**8)
+    fac, outer, seen = tie((fac, outer, seen))
+    outer = join(outer, seen, 100 * 10**8)
     seen = swap(outer, "z", RING8[1])
     fac = fac + swap(fac, "z", RING8_LAST[1])
     fac = fac + swap(fac, "z", RING8_LAST[2])
     fac, outer, seen, second, third = tie((fac, outer, seen, second, third))
-    outer = join(outer, seen, 60 * 10**8)
+    outer = join(outer, seen, 100 * 10**8)
     seen = swap(outer, "z", RING8[2])
     fourth = swap(second, "yl", PAIR)
     fac = fac + swap(fac, "x", RING4[0])

time: 66.5 us -> 65.8 us (0.989)
  starting transfers between devices: 21.3 us -> 20.4 us
    ppermute x13, starting transfers between devices: 21.3 us -> 20.4 us  [swap(): return lax.ppermute(value, axis, pairs + [(b, a) for a, b in pairs])]
  transfers between devices with their start and end apart: 13 -> 13, of which waited for: 7 -> 6; matrix products, arithmetic and copies ran while one was open for 1% -> 1% of each run, Pallas kernels for 13% -> 13%
where the time goes in v6:
time: 65.8 us; the launch traced here: 65.6 us
  blocking collectives  23.1 us (35%)
  starting transfers between devices  20.4 us (31%)
  Pallas kernels  11.9 us (18%)
  waiting for transfers between devices  9.4 us (14%)
  local copies, waits for them, and re-layouts  0.69 us (1%)
    all_to_all x1, blocking collectives, per_device(): parts = lax.all_to_all(parts, ('z', 'yh', 'core'), 0, 0, tiled=True)  23.1 us
    ppermute x13, starting transfers between devices, swap(): return lax.ppermute(value, axis, pairs + [(b, a) for a, b in pairs])  20.4 us
    ppermute x13, waiting for transfers between devices, swap(): return lax.ppermute(value, axis, pairs + [(b, a) for a, b in pairs])  9.4 us
    pallas_call x1, Pallas kernels, project(): pl.pallas_call(functools.partial(project_kernel, scale=1.0 / math.sqrt(wi...  5.73 us
    pallas_call x1, Pallas kernels, invert(): pl.pallas_call(functools.partial(invert_kernel, tokens=tokens), out_shape...  2.88 us
    pallas_call x1, Pallas kernels, finish(): pl.pallas_call(finish_kernel, out_shape=jax.ShapeDtypeStruct((places * 4,...  2.55 us
  transfers between devices with their start and end apart: 13, of which 6 were waited for; matrix products, arithmetic and copies ran while one was open for 1% of the time, Pallas kernels for 13%

profile of v6, /device:TPU:1, one launch (start us, length us, event | category | flops | bytes accessed | tf_op | source)
XLA Modules:
  0.0 65.6 jit_solution(14321828342272603503)
XLA Ops:
  0.0 2.0 %collective-permute-start.1 = (bf16[32,4096]{1,0:T(8,128)(2,1)}, bf16[32,4096]{1,0:T(8,128)(2,1)S(1)}, u32[]{:S(2)}, u32[]{:S(2)}) collective-permute-start(bf16[32,4096]{1,0:T(8,128)(2,1)} %bitcast.8), channel_id=1, source_target_pairs={{0,32},{64,96},{32,0},{96,64},{1,33},{65,97},{33,1},{97,65},{2,34}... | collective-permute-start | bytes 786440 | tf_op jit(solution)/shard_map/ppermute | solution.py:30
  2.0 5.7 %project.1 = (f32[64,128]{1,0:T(8,128)S(1)}, bf16[64,512]{1,0:T(8,128)(2,1)S(1)}) custom-call(bf16[512,4096]{1,0:T(8,128)(2,1)} %bitcast.10, bf16[512,4096]{1,0:T(8,128)(2,1)} %bitcast.11, s32[64,4096]{1,0:T(8,128)} %bitcast.12, s32[64,4096]{1,0:T(8,128)} %bitcast.13), custom_call_target="tpu_custom_call" | custom-call | flops 536870912 | bytes 10485760 | tf_op jit(solution)/shard_map/project/pallas_call | solution.py:118
  7.8 1.4 %collective-permute-start = (f32[64,128]{1,0:T(8,128)S(1)}, f32[64,128]{1,0:T(8,128)S(1)}, u32[]{:S(2)}, u32[]{:S(2)}) collective-permute-start(f32[64,128]{1,0:T(8,128)S(1)} %get-tuple-element.21), channel_id=1, source_target_pairs={{0,128},{128,0},{1,129},{129,1},{2,130},{130,2},{3,131},{131,3},{4... | collective-permute-start | bytes 98312 | tf_op jit(solution)/shard_map/ppermute | solution.py:30
  9.2 6.5 %collective-permute-start.3 = (bf16[64,512]{1,0:T(8,128)(2,1)S(1)}, bf16[64,512]{1,0:T(8,128)(2,1)S(1)}, u32[]{:S(2)}, u32[]{:S(2)}) collective-permute-start(bf16[64,512]{1,0:T(8,128)(2,1)S(1)} %get-tuple-element.25.a), channel_id=1, source_target_pairs={{0,20},{4,16},{8,28},{12,24},{20,0},{16,4},{28,8},{24,12},{1,21},{... | collective-permute-start | bytes 196616 | tf_op jit(solution)/shard_map/ppermute | solution.py:30
  15.7 0.8 %collective-permute-start.2 = (f32[64,128]{1,0:T(8,128)S(1)}, f32[64,128]{1,0:T(8,128)S(1)}, u32[]{:S(2)}, u32[]{:S(2)}) collective-permute-start(f32[64,128]{1,0:T(8,128)S(1)} %add.30), channel_id=1, source_target_pairs={{0,4},{8,12},{16,20},{24,28},{4,0},{12,8},{20,16},{28,24},{1,5},{9... | collective-permute-start | bytes 98312 | tf_op jit(solution)/shard_map/ppermute | solution.py:30
  16.5 0.3 collective-permute-start.8
  16.8 1.8 %collective-permute-start.7 = (bf16[64,4096]{1,0:T(8,128)(2,1)S(1)}, bf16[64,4096]{1,0:T(8,128)(2,1)S(1)}, u32[]{:S(2)}, u32[]{:S(2)}) collective-permute-start(bf16[64,4096]{1,0:T(8,128)(2,1)S(1)} %join.4.refs_0_), channel_id=1, source_target_pairs={{32,64},{96,0},{64,32},{0,96},{33,65},{97,1},{65,33},{1,97},{34,66... | collective-permute-start | bytes 1572872 | tf_op jit(solution)/shard_map/ppermute | solution.py:30
  18.6 0.4 collective-permute-done.2
  19.0 0.9 %collective-permute-start.6 = (bf16[128,512]{1,0:T(8,128)(2,1)S(1)}, bf16[128,512]{1,0:T(8,128)(2,1)S(1)}, u32[]{:S(2)}, u32[]{:S(2)}) collective-permute-start(bf16[128,512]{1,0:T(8,128)(2,1)S(1)} %join.3.a), channel_id=1, source_target_pairs={{0,4},{8,12},{16,20},{24,28},{4,0},{12,8},{20,16},{28,24},{1,5},{9... | collective-permute-start | bytes 393224 | tf_op jit(solution)/shard_map/ppermute | solution.py:30
  19.9 1.8 %collective-permute-start.4 = (f32[64,128]{1,0:T(8,128)S(1)}, f32[64,128]{1,0:T(8,128)S(1)}, u32[]{:S(2)}, u32[]{:S(2)}) collective-permute-start(f32[64,128]{1,0:T(8,128)S(1)} %add.31), channel_id=1, source_target_pairs={{4,8},{12,16},{20,24},{28,0},{8,4},{16,12},{24,20},{0,28},{5,9},{1... | collective-permute-start | bytes 98312 | tf_op jit(solution)/shard_map/ppermute | solution.py:30
  21.7 2.5 %collective-permute-done.4 = f32[64,128]{1,0:T(8,128)S(1)} collective-permute-done((f32[64,128]{1,0:T(8,128)S(1)}, f32[64,128]{1,0:T(8,128)S(1)}, u32[]{:S(2)}, u32[]{:S(2)}) %collective-permute-start.4) | collective-permute-done | bytes 32800 | tf_op jit(solution)/shard_map/ppermute | solution.py:30
  24.2 1.4 %collective-permute-start.5 = (f32[64,128]{1,0:T(8,128)S(1)}, f32[64,128]{1,0:T(8,128)S(1)}, u32[]{:S(2)}, u32[]{:S(2)}) collective-permute-start(f32[64,128]{1,0:T(8,128)S(1)} %add.32), channel_id=1, source_target_pairs={{4,24},{8,20},{0,12},{28,16},{24,4},{20,8},{12,0},{16,28},{5,25},{... | collective-permute-start | bytes 98312 | tf_op jit(solution)/shard_map/ppermute | solution.py:30
  25.6 3.2 %collective-permute-done.5 = f32[64,128]{1,0:T(8,128)S(1)} collective-permute-done((f32[64,128]{1,0:T(8,128)S(1)}, f32[64,128]{1,0:T(8,128)S(1)}, u32[]{:S(2)}, u32[]{:S(2)}) %collective-permute-start.5) | collective-permute-done | bytes 32800 | tf_op jit(solution)/shard_map/ppermute | solution.py:30
  28.8 0.5 collective-permute-done.7.refs_1_
  29.3 1.3 %collective-permute-start.12 = (bf16[64,4096]{1,0:T(8,128)(2,1)S(1)}, bf16[64,4096]{1,0:T(8,128)(2,1)S(1)}, u32[]{:S(2)}, u32[]{:S(2)}) collective-permute-start(bf16[64,4096]{1,0:T(8,128)(2,1)S(1)} %collective-permute-done.7.refs_1_), channel_id=1, source_target_pairs={{0,128},{128,0},{1,129},{129,1},{2,130},{130,2},{3,131},{131,3},{4... | collective-permute-start | bytes 1572872 | tf_op jit(solution)/shard_map/ppermute | solution.py:30
  30.6 0.5 collective-permute-start.11
  31.1 1.3 %collective-permute-done.9 = f32[64,128]{1,0:T(8,128)S(1)} collective-permute-done((f32[64,128]{1,0:T(8,128)S(1)}, f32[64,128]{1,0:T(8,128)S(1)}, u32[]{:S(2)}, u32[]{:S(2)}) %collective-permute-start.9) | collective-permute-done | bytes 32800 | tf_op jit(solution)/shard_map/ppermute | solution.py:30
  32.4 1.8 %collective-permute-start.10 = (f32[64,128]{1,0:T(8,128)S(1)}, f32[64,128]{1,0:T(8,128)S(1)}, u32[]{:S(2)}, u32[]{:S(2)}) collective-permute-start(f32[64,128]{1,0:T(8,128)S(1)} %add.34), channel_id=1, source_target_pairs={{32,64},{96,0},{64,32},{0,96},{33,65},{97,1},{65,33},{1,97},{34,66... | collective-permute-start | bytes 98312 | tf_op jit(solution)/shard_map/ppermute | solution.py:30
  34.2 0.7 %dynamic-slice_bitcast_fusion.layout = s32[16]{0:T(128)S(1)} fusion(s32[2,4,8,16]{3,2,1,0:T(8,128)} %constant.26.clone, s32[]{:T(128)S(6)} %select_n.9, s32[]{:T(128)S(6)} %select_n.10, s32[]{:T(128)S(6)} %select_n.11), kind=kLoop, calls=%fused_computation | loop fusion | bytes 140 | tf_op jit(solution)/shard_map/squeeze | solution.py:335
  34.9 1.5 %collective-permute-done.10 = f32[64,128]{1,0:T(8,128)S(1)} collective-permute-done((f32[64,128]{1,0:T(8,128)S(1)}, f32[64,128]{1,0:T(8,128)S(1)}, u32[]{:S(2)}, u32[]{:S(2)}) %collective-permute-start.10) | collective-permute-done | bytes 32800 | tf_op jit(solution)/shard_map/ppermute | solution.py:30
  36.4 2.9 %invert.1.inverses = f32[64,128]{1,0:T(8,128)S(1)} custom-call(f32[64,128]{1,0:T(8,128)S(1)} %add.35.fac), custom_call_target="tpu_custom_call" | custom-call | flops 2500000000 | bytes 65536 | tf_op jit(solution)/shard_map/invert/pallas_call | solution.py:206
  39.3 2.5 %finish.1 = f32[32,4,128]{2,1,0:T(4,128)S(1)} custom-call(s32[16]{0:T(128)S(1)} %dynamic-slice_bitcast_fusion.layout, f32[64,128]{1,0:T(8,128)S(1)} %invert.1.inverses, bf16[256,512]{1,0:T(8,128)(2,1)S(1)} %join.5.near, bf16[256,512]{1,0:T(8,128)(2,1)S(1)} %collective-permute-done.11.far, bf16[64,4096]{1,0:T(8,128)(2,1)S(1)} %join.4.refs_0_, ...), custom_call_target="tpu_custom_call" | custom-call | flops 4000000000 | bytes 1048576 | tf_op jit(solution)/shard_map/finish/pallas_call | solution.py:282
  41.8 23.1 %all_to_all.5.parts = f32[32,4,128]{2,1,0:T(4,128)S(1)} all-to-all(f32[32,4,128]{2,1,0:T(4,128)S(1)} %finish.1), channel_id=1, replica_groups=mesh['yl'=2,'x'=4,'z'=8,'yh'=2,'core'=2] {'z','yh','core'}, dimensions={0} | all-to-all | bytes 131072 | tf_op jit(solution)/shard_map/all_to_all | solution.py:361
  64.9 0.7 %collect.1 = f32[8,512]{1,0:T(8,128)} custom-call(f32[32,4,128]{2,1,0:T(4,128)S(1)} %all_to_all.5.parts), custom_call_target="tpu_custom_call" | custom-call | tf_op jit(solution)/shard_map/collect/pallas_call | solution.py:320
  (19 shorter events, 0.1 us)
Async XLA Ops:
  0.0 15.6 %collective-permute-start.1 = (bf16[32,4096]{1,0:T(8,128)(2,1)}, bf16[32,4096]{1,0:T(8,128)(2,1)S(1)}, u32[]{:S(2)}, u32[]{:S(2)}) collective-permute-start(bf16[32,4096]{1,0:T(8,128)(2,1)} %bitcast.8), channel_id=1, source_target_pairs={{0,32},{64,96},{32,0},{96,64},{1,33},{65,97},{33,1},{97,65},{2,34}... | collective-permute-start | bytes 786440 | tf_op jit(solution)/shard_map/ppermute | solution.py:30
  2.0 14.4 %copy-start = (bf16[1,32,4096]{2,1,0:T(8,128)(2,1)S(1)}, bf16[1,32,4096]{2,1,0:T(8,128)(2,1)}, u32[]{:S(2)}) copy-start(bf16[1,32,4096]{2,1,0:T(8,128)(2,1)} %param.10) | copy-start | bytes 786436
  7.8 7.9 %collective-permute-start = (f32[64,128]{1,0:T(8,128)S(1)}, f32[64,128]{1,0:T(8,128)S(1)}, u32[]{:S(2)}, u32[]{:S(2)}) collective-permute-start(f32[64,128]{1,0:T(8,128)S(1)} %get-tuple-element.21), channel_id=1, source_target_pairs={{0,128},{128,0},{1,129},{129,1},{2,130},{130,2},{3,131},{131,3},{4... | collective-permute-start | bytes 98312 | tf_op jit(solution)/shard_map/ppermute | solution.py:30
  9.2 9.8 %collective-permute-start.3 = (bf16[64,512]{1,0:T(8,128)(2,1)S(1)}, bf16[64,512]{1,0:T(8,128)(2,1)S(1)}, u32[]{:S(2)}, u32[]{:S(2)}) collective-permute-start(bf16[64,512]{1,0:T(8,128)(2,1)S(1)} %get-tuple-element.25.a), channel_id=1, source_target_pairs={{0,20},{4,16},{8,28},{12,24},{20,0},{16,4},{28,8},{24,12},{1,21},{... | collective-permute-start | bytes 196616 | tf_op jit(solution)/shard_map/ppermute | solution.py:30
  15.7 3.3 %collective-permute-start.2 = (f32[64,128]{1,0:T(8,128)S(1)}, f32[64,128]{1,0:T(8,128)S(1)}, u32[]{:S(2)}, u32[]{:S(2)}) collective-permute-start(f32[64,128]{1,0:T(8,128)S(1)} %add.30), channel_id=1, source_target_pairs={{0,4},{8,12},{16,20},{24,28},{4,0},{12,8},{20,16},{28,24},{1,5},{9... | collective-permute-start | bytes 98312 | tf_op jit(solution)/shard_map/ppermute | solution.py:30
  16.5 12.3 %collective-permute-start.8 = (bf16[64,4096]{1,0:T(8,128)(2,1)S(1)}, bf16[64,4096]{1,0:T(8,128)(2,1)S(1)}, u32[]{:S(2)}, u32[]{:S(2)}) collective-permute-start(bf16[64,4096]{1,0:T(8,128)(2,1)S(1)} %join.4.refs_0_), channel_id=1, source_target_pairs={{0,128},{128,0},{1,129},{129,1},{2,130},{130,2},{3,131},{131,3},{4... | collective-permute-start | bytes 1572872 | tf_op jit(solution)/shard_map/ppermute | solution.py:30
  16.8 12.5 %collective-permute-start.7 = (bf16[64,4096]{1,0:T(8,128)(2,1)S(1)}, bf16[64,4096]{1,0:T(8,128)(2,1)S(1)}, u32[]{:S(2)}, u32[]{:S(2)}) collective-permute-start(bf16[64,4096]{1,0:T(8,128)(2,1)S(1)} %join.4.refs_0_), channel_id=1, source_target_pairs={{32,64},{96,0},{64,32},{0,96},{33,65},{97,1},{65,33},{1,97},{34,66... | collective-permute-start | bytes 1572872 | tf_op jit(solution)/shard_map/ppermute | solution.py:30
  19.0 9.8 %collective-permute-start.6 = (bf16[128,512]{1,0:T(8,128)(2,1)S(1)}, bf16[128,512]{1,0:T(8,128)(2,1)S(1)}, u32[]{:S(2)}, u32[]{:S(2)}) collective-permute-start(bf16[128,512]{1,0:T(8,128)(2,1)S(1)} %join.3.a), channel_id=1, source_target_pairs={{0,4},{8,12},{16,20},{24,28},{4,0},{12,8},{20,16},{28,24},{1,5},{9... | collective-permute-start | bytes 393224 | tf_op jit(solution)/shard_map/ppermute | solution.py:30
  19.9 4.3 %collective-permute-start.4 = (f32[64,128]{1,0:T(8,128)S(1)}, f32[64,128]{1,0:T(8,128)S(1)}, u32[]{:S(2)}, u32[]{:S(2)}) collective-permute-start(f32[64,128]{1,0:T(8,128)S(1)} %add.31), channel_id=1, source_target_pairs={{4,8},{12,16},{20,24},{28,0},{8,4},{16,12},{24,20},{0,28},{5,9},{1... | collective-permute-start | bytes 98312 | tf_op jit(solution)/shard_map/ppermute | solution.py:30
  24.2 4.6 %collective-permute-start.5 = (f32[64,128]{1,0:T(8,128)S(1)}, f32[64,128]{1,0:T(8,128)S(1)}, u32[]{:S(2)}, u32[]{:S(2)}) collective-permute-start(f32[64,128]{1,0:T(8,128)S(1)} %add.32), channel_id=1, source_target_pairs={{4,24},{8,20},{0,12},{28,16},{24,4},{20,8},{12,0},{16,28},{5,25},{... | collective-permute-start | bytes 98312 | tf_op jit(solution)/shard_map/ppermute | solution.py:30
  29.3 3.1 %collective-permute-start.9 = (f32[64,128]{1,0:T(8,128)S(1)}, f32[64,128]{1,0:T(8,128)S(1)}, u32[]{:S(2)}, u32[]{:S(2)}) collective-permute-start(f32[64,128]{1,0:T(8,128)S(1)} %add.33), channel_id=1, source_target_pairs={{0,32},{64,96},{32,0},{96,64},{1,33},{65,97},{33,1},{97,65},{2,34}... | collective-permute-start | bytes 98312 | tf_op jit(solution)/shard_map/ppermute | solution.py:30
  29.3 9.9 %collective-permute-start.12 = (bf16[64,4096]{1,0:T(8,128)(2,1)S(1)}, bf16[64,4096]{1,0:T(8,128)(2,1)S(1)}, u32[]{:S(2)}, u32[]{:S(2)}) collective-permute-start(bf16[64,4096]{1,0:T(8,128)(2,1)S(1)} %collective-permute-done.7.refs_1_), channel_id=1, source_target_pairs={{0,128},{128,0},{1,129},{129,1},{2,130},{130,2},{3,131},{131,3},{4... | collective-permute-start | bytes 1572872 | tf_op jit(solution)/shard_map/ppermute | solution.py:30
  30.6 8.6 %collective-permute-start.11 = (bf16[256,512]{1,0:T(8,128)(2,1)S(1)}, bf16[256,512]{1,0:T(8,128)(2,1)S(1)}, u32[]{:S(2)}, u32[]{:S(2)}) collective-permute-start(bf16[256,512]{1,0:T(8,128)(2,1)S(1)} %join.5.near), channel_id=1, source_target_pairs={{4,8},{12,16},{20,24},{28,0},{8,4},{16,12},{24,20},{0,28},{5,9},{1... | collective-permute-start | bytes 786440 | tf_op jit(solution)/shard_map/ppermute | solution.py:30
  32.4 4.0 %collective-permute-start.10 = (f32[64,128]{1,0:T(8,128)S(1)}, f32[64,128]{1,0:T(8,128)S(1)}, u32[]{:S(2)}, u32[]{:S(2)}) collective-permute-start(f32[64,128]{1,0:T(8,128)S(1)} %add.34), channel_id=1, source_target_pairs={{32,64},{96,0},{64,32},{0,96},{33,65},{97,1},{65,33},{1,97},{34,66... | collective-permute-start | bytes 98312 | tf_op jit(solution)/shard_map/ppermute | solution.py:30

commit v7 on v6

--- a/solution.py
+++ b/solution.py
@@ -215,7 +215,7 @@
 
 
 def finish_kernel(layout, inverses, near, far, *refs):
-    queries, (out, held, train, scores, his, los) = refs[:4], refs[4:]
+    queries, (out, held, train, scores, parts_v) = refs[:4], refs[4:]
     rank = inverses.shape[0]
     mat = inverses[...]
     inv_in = mat[:, :rank]
@@ -236,11 +236,13 @@
         at = p % half * rank
         both = dot(out_both, (near if p < half else far)[at : at + rank, :])
         hi, lo = halves(both[:rank] + both[rank:])
-        his[p * rank : (p + 1) * rank, :] = hi
-        los[p * rank : (p + 1) * rank, :] = lo
+        parts_v[p * rank : (p + 1) * rank, :] = hi
+        parts_v[(places + p) * rank : (places + p + 1) * rank, :] = lo
     for c in range(wide // four):
         cut = slice(c * four, (c + 1) * four)
-        second = dot(his[:, cut], in_hi) + (dot(his[:, cut], in_lo) + dot(los[:, cut], in_hi))
+        main = dot(parts_v[:, cut], in_hi)
+        rest = dot(parts_v[: places * rank, cut], in_lo)
+        second = main[: places * rank] + (rest + main[places * rank :])
         held[:, :, cut] = second.reshape(places, rank, four)
     low = lax.broadcasted_iota(jnp.int32, (places, 2 * rank), 1) < rank
     for o in range(0, rank, 2):
@@ -288,8 +290,7 @@
             pltpu.VMEM((places, rank, near.shape[1]), F32),
             pltpu.VMEM((places * examples, rank * rank), BF16),
             pltpu.VMEM((2, places * examples, 2 * count), F32),
-            pltpu.VMEM((places * rank, near.shape[1]), BF16),
-            pltpu.VMEM((places * rank, near.shape[1]), BF16),
+            pltpu.VMEM((2 * places * rank, near.shape[1]), BF16),
         ],
         compiler_params=pltpu.CompilerParams(vmem_limit_bytes=16 * 2**20),
         cost_estimate=pl.CostEstimate(

time: 65.8 us -> 65.8 us (level)
  no operation moved by 1% of the time
where the time goes in v7:
time: 65.8 us; the launch traced here: 65.6 us
  blocking collectives  23.1 us (35%)
  starting transfers between devices  20.4 us (31%)
  Pallas kernels  11.9 us (18%)
  waiting for transfers between devices  9.4 us (14%)
  local copies, waits for them, and re-layouts  0.69 us (1%)
    all_to_all x1, blocking collectives, per_device(): parts = lax.all_to_all(parts, ('z', 'yh', 'core'), 0, 0, tiled=True)  23.1 us
    ppermute x13, starting transfers between devices, swap(): return lax.ppermute(value, axis, pairs + [(b, a) for a, b in pairs])  20.4 us
    ppermute x13, waiting for transfers between devices, swap(): return lax.ppermute(value, axis, pairs + [(b, a) for a, b in pairs])  9.4 us
    pallas_call x1, Pallas kernels, project(): pl.pallas_call(functools.partial(project_kernel, scale=1.0 / math.sqrt(wi...  5.73 us
    pallas_call x1, Pallas kernels, invert(): pl.pallas_call(functools.partial(invert_kernel, tokens=tokens), out_shape...  2.88 us
    pallas_call x1, Pallas kernels, finish(): pl.pallas_call(finish_kernel, out_shape=jax.ShapeDtypeStruct((places * 4,...  2.54 us
  transfers between devices with their start and end apart: 13, of which 6 were waited for; matrix products, arithmetic and copies ran while one was open for 1% of the time, Pallas kernels for 13%

profile of v7, /device:TPU:1, one launch (start us, length us, event | category | flops | bytes accessed | tf_op | source)
XLA Modules:
  0.0 65.6 jit_solution(12454379735812365808)
XLA Ops:
  0.0 2.0 %collective-permute-start.1 = (bf16[32,4096]{1,0:T(8,128)(2,1)}, bf16[32,4096]{1,0:T(8,128)(2,1)S(1)}, u32[]{:S(2)}, u32[]{:S(2)}) collective-permute-start(bf16[32,4096]{1,0:T(8,128)(2,1)} %bitcast.8), channel_id=1, source_target_pairs={{0,32},{64,96},{32,0},{96,64},{1,33},{65,97},{33,1},{97,65},{2,34}... | collective-permute-start | bytes 786440 | tf_op jit(solution)/shard_map/ppermute | solution.py:30
  2.0 5.7 %project.1 = (f32[64,128]{1,0:T(8,128)S(1)}, bf16[64,512]{1,0:T(8,128)(2,1)S(1)}) custom-call(bf16[512,4096]{1,0:T(8,128)(2,1)} %bitcast.10, bf16[512,4096]{1,0:T(8,128)(2,1)} %bitcast.11, s32[64,4096]{1,0:T(8,128)} %bitcast.12, s32[64,4096]{1,0:T(8,128)} %bitcast.13), custom_call_target="tpu_custom_call" | custom-call | flops 536870912 | bytes 10485760 | tf_op jit(solution)/shard_map/project/pallas_call | solution.py:118
  7.8 1.4 %collective-permute-start = (f32[64,128]{1,0:T(8,128)S(1)}, f32[64,128]{1,0:T(8,128)S(1)}, u32[]{:S(2)}, u32[]{:S(2)}) collective-permute-start(f32[64,128]{1,0:T(8,128)S(1)} %get-tuple-element.21), channel_id=1, source_target_pairs={{0,128},{128,0},{1,129},{129,1},{2,130},{130,2},{3,131},{131,3},{4... | collective-permute-start | bytes 98312 | tf_op jit(solution)/shard_map/ppermute | solution.py:30
  9.2 6.5 %collective-permute-start.3 = (bf16[64,512]{1,0:T(8,128)(2,1)S(1)}, bf16[64,512]{1,0:T(8,128)(2,1)S(1)}, u32[]{:S(2)}, u32[]{:S(2)}) collective-permute-start(bf16[64,512]{1,0:T(8,128)(2,1)S(1)} %get-tuple-element.25.a), channel_id=1, source_target_pairs={{0,20},{4,16},{8,28},{12,24},{20,0},{16,4},{28,8},{24,12},{1,21},{... | collective-permute-start | bytes 196616 | tf_op jit(solution)/shard_map/ppermute | solution.py:30
  15.7 0.8 %collective-permute-start.2 = (f32[64,128]{1,0:T(8,128)S(1)}, f32[64,128]{1,0:T(8,128)S(1)}, u32[]{:S(2)}, u32[]{:S(2)}) collective-permute-start(f32[64,128]{1,0:T(8,128)S(1)} %add.30), channel_id=1, source_target_pairs={{0,4},{8,12},{16,20},{24,28},{4,0},{12,8},{20,16},{28,24},{1,5},{9... | collective-permute-start | bytes 98312 | tf_op jit(solution)/shard_map/ppermute | solution.py:30
  16.5 0.3 collective-permute-start.8
  16.8 1.8 %collective-permute-start.7 = (bf16[64,4096]{1,0:T(8,128)(2,1)S(1)}, bf16[64,4096]{1,0:T(8,128)(2,1)S(1)}, u32[]{:S(2)}, u32[]{:S(2)}) collective-permute-start(bf16[64,4096]{1,0:T(8,128)(2,1)S(1)} %join.4.refs_0_), channel_id=1, source_target_pairs={{32,64},{96,0},{64,32},{0,96},{33,65},{97,1},{65,33},{1,97},{34,66... | collective-permute-start | bytes 1572872 | tf_op jit(solution)/shard_map/ppermute | solution.py:30
  18.6 0.4 collective-permute-done.2
  19.0 0.9 %collective-permute-start.6 = (bf16[128,512]{1,0:T(8,128)(2,1)S(1)}, bf16[128,512]{1,0:T(8,128)(2,1)S(1)}, u32[]{:S(2)}, u32[]{:S(2)}) collective-permute-start(bf16[128,512]{1,0:T(8,128)(2,1)S(1)} %join.3.a), channel_id=1, source_target_pairs={{0,4},{8,12},{16,20},{24,28},{4,0},{12,8},{20,16},{28,24},{1,5},{9... | collective-permute-start | bytes 393224 | tf_op jit(solution)/shard_map/ppermute | solution.py:30
  19.9 1.8 %collective-permute-start.4 = (f32[64,128]{1,0:T(8,128)S(1)}, f32[64,128]{1,0:T(8,128)S(1)}, u32[]{:S(2)}, u32[]{:S(2)}) collective-permute-start(f32[64,128]{1,0:T(8,128)S(1)} %add.31), channel_id=1, source_target_pairs={{4,8},{12,16},{20,24},{28,0},{8,4},{16,12},{24,20},{0,28},{5,9},{1... | collective-permute-start | bytes 98312 | tf_op jit(solution)/shard_map/ppermute | solution.py:30
  21.7 2.5 %collective-permute-done.4 = f32[64,128]{1,0:T(8,128)S(1)} collective-permute-done((f32[64,128]{1,0:T(8,128)S(1)}, f32[64,128]{1,0:T(8,128)S(1)}, u32[]{:S(2)}, u32[]{:S(2)}) %collective-permute-start.4) | collective-permute-done | bytes 32800 | tf_op jit(solution)/shard_map/ppermute | solution.py:30
  24.2 1.4 %collective-permute-start.5 = (f32[64,128]{1,0:T(8,128)S(1)}, f32[64,128]{1,0:T(8,128)S(1)}, u32[]{:S(2)}, u32[]{:S(2)}) collective-permute-start(f32[64,128]{1,0:T(8,128)S(1)} %add.32), channel_id=1, source_target_pairs={{4,24},{8,20},{0,12},{28,16},{24,4},{20,8},{12,0},{16,28},{5,25},{... | collective-permute-start | bytes 98312 | tf_op jit(solution)/shard_map/ppermute | solution.py:30
  25.6 3.2 %collective-permute-done.5 = f32[64,128]{1,0:T(8,128)S(1)} collective-permute-done((f32[64,128]{1,0:T(8,128)S(1)}, f32[64,128]{1,0:T(8,128)S(1)}, u32[]{:S(2)}, u32[]{:S(2)}) %collective-permute-start.5) | collective-permute-done | bytes 32800 | tf_op jit(solution)/shard_map/ppermute | solution.py:30
  28.8 0.5 collective-permute-done.7.refs_1_
  29.3 1.3 %collective-permute-start.12 = (bf16[64,4096]{1,0:T(8,128)(2,1)S(1)}, bf16[64,4096]{1,0:T(8,128)(2,1)S(1)}, u32[]{:S(2)}, u32[]{:S(2)}) collective-permute-start(bf16[64,4096]{1,0:T(8,128)(2,1)S(1)} %collective-permute-done.7.refs_1_), channel_id=1, source_target_pairs={{0,128},{128,0},{1,129},{129,1},{2,130},{130,2},{3,131},{131,3},{4... | collective-permute-start | bytes 1572872 | tf_op jit(solution)/shard_map/ppermute | solution.py:30
  30.6 0.5 collective-permute-start.11
  31.1 1.3 %collective-permute-done.9 = f32[64,128]{1,0:T(8,128)S(1)} collective-permute-done((f32[64,128]{1,0:T(8,128)S(1)}, f32[64,128]{1,0:T(8,128)S(1)}, u32[]{:S(2)}, u32[]{:S(2)}) %collective-permute-start.9) | collective-permute-done | bytes 32800 | tf_op jit(solution)/shard_map/ppermute | solution.py:30
  32.4 1.8 %collective-permute-start.10 = (f32[64,128]{1,0:T(8,128)S(1)}, f32[64,128]{1,0:T(8,128)S(1)}, u32[]{:S(2)}, u32[]{:S(2)}) collective-permute-start(f32[64,128]{1,0:T(8,128)S(1)} %add.34), channel_id=1, source_target_pairs={{32,64},{96,0},{64,32},{0,96},{33,65},{97,1},{65,33},{1,97},{34,66... | collective-permute-start | bytes 98312 | tf_op jit(solution)/shard_map/ppermute | solution.py:30
  34.2 0.7 %dynamic-slice_bitcast_fusion.layout = s32[16]{0:T(128)S(1)} fusion(s32[2,4,8,16]{3,2,1,0:T(8,128)} %constant.26.clone, s32[]{:T(128)S(6)} %select_n.9, s32[]{:T(128)S(6)} %select_n.10, s32[]{:T(128)S(6)} %select_n.11), kind=kLoop, calls=%fused_computation | loop fusion | bytes 140 | tf_op jit(solution)/shard_map/squeeze | solution.py:336
  34.9 1.5 %collective-permute-done.10 = f32[64,128]{1,0:T(8,128)S(1)} collective-permute-done((f32[64,128]{1,0:T(8,128)S(1)}, f32[64,128]{1,0:T(8,128)S(1)}, u32[]{:S(2)}, u32[]{:S(2)}) %collective-permute-start.10) | collective-permute-done | bytes 32800 | tf_op jit(solution)/shard_map/ppermute | solution.py:30
  36.4 2.9 %invert.1.inverses = f32[64,128]{1,0:T(8,128)S(1)} custom-call(f32[64,128]{1,0:T(8,128)S(1)} %add.35.fac), custom_call_target="tpu_custom_call" | custom-call | flops 2500000000 | bytes 65536 | tf_op jit(solution)/shard_map/invert/pallas_call | solution.py:206
  39.3 2.5 %finish.1 = f32[32,4,128]{2,1,0:T(4,128)S(1)} custom-call(s32[16]{0:T(128)S(1)} %dynamic-slice_bitcast_fusion.layout, f32[64,128]{1,0:T(8,128)S(1)} %invert.1.inverses, bf16[256,512]{1,0:T(8,128)(2,1)S(1)} %join.5.near, bf16[256,512]{1,0:T(8,128)(2,1)S(1)} %collective-permute-done.11.far, bf16[64,4096]{1,0:T(8,128)(2,1)S(1)} %join.4.refs_0_, ...), custom_call_target="tpu_custom_call" | custom-call | flops 4000000000 | bytes 1048576 | tf_op jit(solution)/shard_map/finish/pallas_call | solution.py:284
  41.8 23.1 %all_to_all.5.parts = f32[32,4,128]{2,1,0:T(4,128)S(1)} all-to-all(f32[32,4,128]{2,1,0:T(4,128)S(1)} %finish.1), channel_id=1, replica_groups=mesh['yl'=2,'x'=4,'z'=8,'yh'=2,'core'=2] {'z','yh','core'}, dimensions={0} | all-to-all | bytes 131072 | tf_op jit(solution)/shard_map/all_to_all | solution.py:362
  64.9 0.7 %collect.1 = f32[8,512]{1,0:T(8,128)} custom-call(f32[32,4,128]{2,1,0:T(4,128)S(1)} %all_to_all.5.parts), custom_call_target="tpu_custom_call" | custom-call | tf_op jit(solution)/shard_map/collect/pallas_call | solution.py:321
  (19 shorter events, 0.1 us)
Async XLA Ops:
  0.0 15.6 %collective-permute-start.1 = (bf16[32,4096]{1,0:T(8,128)(2,1)}, bf16[32,4096]{1,0:T(8,128)(2,1)S(1)}, u32[]{:S(2)}, u32[]{:S(2)}) collective-permute-start(bf16[32,4096]{1,0:T(8,128)(2,1)} %bitcast.8), channel_id=1, source_target_pairs={{0,32},{64,96},{32,0},{96,64},{1,33},{65,97},{33,1},{97,65},{2,34}... | collective-permute-start | bytes 786440 | tf_op jit(solution)/shard_map/ppermute | solution.py:30
  2.0 14.4 %copy-start = (bf16[1,32,4096]{2,1,0:T(8,128)(2,1)S(1)}, bf16[1,32,4096]{2,1,0:T(8,128)(2,1)}, u32[]{:S(2)}) copy-start(bf16[1,32,4096]{2,1,0:T(8,128)(2,1)} %param.10) | copy-start | bytes 786436
  7.8 7.9 %collective-permute-start = (f32[64,128]{1,0:T(8,128)S(1)}, f32[64,128]{1,0:T(8,128)S(1)}, u32[]{:S(2)}, u32[]{:S(2)}) collective-permute-start(f32[64,128]{1,0:T(8,128)S(1)} %get-tuple-element.21), channel_id=1, source_target_pairs={{0,128},{128,0},{1,129},{129,1},{2,130},{130,2},{3,131},{131,3},{4... | collective-permute-start | bytes 98312 | tf_op jit(solution)/shard_map/ppermute | solution.py:30
  9.2 9.8 %collective-permute-start.3 = (bf16[64,512]{1,0:T(8,128)(2,1)S(1)}, bf16[64,512]{1,0:T(8,128)(2,1)S(1)}, u32[]{:S(2)}, u32[]{:S(2)}) collective-permute-start(bf16[64,512]{1,0:T(8,128)(2,1)S(1)} %get-tuple-element.25.a), channel_id=1, source_target_pairs={{0,20},{4,16},{8,28},{12,24},{20,0},{16,4},{28,8},{24,12},{1,21},{... | collective-permute-start | bytes 196616 | tf_op jit(solution)/shard_map/ppermute | solution.py:30
  15.7 3.3 %collective-permute-start.2 = (f32[64,128]{1,0:T(8,128)S(1)}, f32[64,128]{1,0:T(8,128)S(1)}, u32[]{:S(2)}, u32[]{:S(2)}) collective-permute-start(f32[64,128]{1,0:T(8,128)S(1)} %add.30), channel_id=1, source_target_pairs={{0,4},{8,12},{16,20},{24,28},{4,0},{12,8},{20,16},{28,24},{1,5},{9... | collective-permute-start | bytes 98312 | tf_op jit(solution)/shard_map/ppermute | solution.py:30
  16.5 12.3 %collective-permute-start.8 = (bf16[64,4096]{1,0:T(8,128)(2,1)S(1)}, bf16[64,4096]{1,0:T(8,128)(2,1)S(1)}, u32[]{:S(2)}, u32[]{:S(2)}) collective-permute-start(bf16[64,4096]{1,0:T(8,128)(2,1)S(1)} %join.4.refs_0_), channel_id=1, source_target_pairs={{0,128},{128,0},{1,129},{129,1},{2,130},{130,2},{3,131},{131,3},{4... | collective-permute-start | bytes 1572872 | tf_op jit(solution)/shard_map/ppermute | solution.py:30
  16.8 12.5 %collective-permute-start.7 = (bf16[64,4096]{1,0:T(8,128)(2,1)S(1)}, bf16[64,4096]{1,0:T(8,128)(2,1)S(1)}, u32[]{:S(2)}, u32[]{:S(2)}) collective-permute-start(bf16[64,4096]{1,0:T(8,128)(2,1)S(1)} %join.4.refs_0_), channel_id=1, source_target_pairs={{32,64},{96,0},{64,32},{0,96},{33,65},{97,1},{65,33},{1,97},{34,66... | collective-permute-start | bytes 1572872 | tf_op jit(solution)/shard_map/ppermute | solution.py:30
  19.0 9.8 %collective-permute-start.6 = (bf16[128,512]{1,0:T(8,128)(2,1)S(1)}, bf16[128,512]{1,0:T(8,128)(2,1)S(1)}, u32[]{:S(2)}, u32[]{:S(2)}) collective-permute-start(bf16[128,512]{1,0:T(8,128)(2,1)S(1)} %join.3.a), channel_id=1, source_target_pairs={{0,4},{8,12},{16,20},{24,28},{4,0},{12,8},{20,16},{28,24},{1,5},{9... | collective-permute-start | bytes 393224 | tf_op jit(solution)/shard_map/ppermute | solution.py:30
  19.9 4.3 %collective-permute-start.4 = (f32[64,128]{1,0:T(8,128)S(1)}, f32[64,128]{1,0:T(8,128)S(1)}, u32[]{:S(2)}, u32[]{:S(2)}) collective-permute-start(f32[64,128]{1,0:T(8,128)S(1)} %add.31), channel_id=1, source_target_pairs={{4,8},{12,16},{20,24},{28,0},{8,4},{16,12},{24,20},{0,28},{5,9},{1... | collective-permute-start | bytes 98312 | tf_op jit(solution)/shard_map/ppermute | solution.py:30
  24.2 4.6 %collective-permute-start.5 = (f32[64,128]{1,0:T(8,128)S(1)}, f32[64,128]{1,0:T(8,128)S(1)}, u32[]{:S(2)}, u32[]{:S(2)}) collective-permute-start(f32[64,128]{1,0:T(8,128)S(1)} %add.32), channel_id=1, source_target_pairs={{4,24},{8,20},{0,12},{28,16},{24,4},{20,8},{12,0},{16,28},{5,25},{... | collective-permute-start | bytes 98312 | tf_op jit(solution)/shard_map/ppermute | solution.py:30
  29.3 3.1 %collective-permute-start.9 = (f32[64,128]{1,0:T(8,128)S(1)}, f32[64,128]{1,0:T(8,128)S(1)}, u32[]{:S(2)}, u32[]{:S(2)}) collective-permute-start(f32[64,128]{1,0:T(8,128)S(1)} %add.33), channel_id=1, source_target_pairs={{0,32},{64,96},{32,0},{96,64},{1,33},{65,97},{33,1},{97,65},{2,34}... | collective-permute-start | bytes 98312 | tf_op jit(solution)/shard_map/ppermute | solution.py:30
  29.3 9.9 %collective-permute-start.12 = (bf16[64,4096]{1,0:T(8,128)(2,1)S(1)}, bf16[64,4096]{1,0:T(8,128)(2,1)S(1)}, u32[]{:S(2)}, u32[]{:S(2)}) collective-permute-start(bf16[64,4096]{1,0:T(8,128)(2,1)S(1)} %collective-permute-done.7.refs_1_), channel_id=1, source_target_pairs={{0,128},{128,0},{1,129},{129,1},{2,130},{130,2},{3,131},{131,3},{4... | collective-permute-start | bytes 1572872 | tf_op jit(solution)/shard_map/ppermute | solution.py:30
  30.6 8.6 %collective-permute-start.11 = (bf16[256,512]{1,0:T(8,128)(2,1)S(1)}, bf16[256,512]{1,0:T(8,128)(2,1)S(1)}, u32[]{:S(2)}, u32[]{:S(2)}) collective-permute-start(bf16[256,512]{1,0:T(8,128)(2,1)S(1)} %join.5.near), channel_id=1, source_target_pairs={{4,8},{12,16},{20,24},{28,0},{8,4},{16,12},{24,20},{0,28},{5,9},{1... | collective-permute-start | bytes 786440 | tf_op jit(solution)/shard_map/ppermute | solution.py:30
  32.4 4.0 %collective-permute-start.10 = (f32[64,128]{1,0:T(8,128)S(1)}, f32[64,128]{1,0:T(8,128)S(1)}, u32[]{:S(2)}, u32[]{:S(2)}) collective-permute-start(f32[64,128]{1,0:T(8,128)S(1)} %add.34), channel_id=1, source_target_pairs={{32,64},{96,0},{64,32},{0,96},{33,65},{97,1},{65,33},{1,97},{34,66... | collective-permute-start | bytes 98312 | tf_op jit(solution)/shard_map/ppermute | solution.py:30
